TPU v7x, 32 devices: a whole 2x2x4 slice. The times are simulated.
32 devices in a mesh: leaf: 16 (over z, y, core), grp: 2 (over x).
Axes of the slice: x: 2, y: 2, z: 4, core: 2. Of those that a mesh axis runs over, the one named last changes fastest.
Arguments:
- slot_parent: int32 [32], P(('leaf', 'grp')), may hold values from -1 to 7, as said below
- leaf_matrix: float32 [32, 384, 384], P(('leaf', 'grp')), as said below
- coupling: float32 [32, 384, 128], P(('leaf', 'grp')), may hold values from -0.3125 to 0.3125
- leaf_residual_rows: float32 [32, 384], P(('leaf', 'grp')), may hold values from -6 to 6
- node_matrix: float32 [16, 128, 128], P('grp', 'leaf'), as said below
- node_link: float32 [16, 128, 128], P('grp', 'leaf'), may hold values from -0.5 to 0.5
- node_rhs: float32 [16, 128], P('grp', 'leaf'), may hold values from -6 to 6
- root_matrix: float32 [128, 128], replicated, as said below
- root_rhs: float32 [128], replicated, may hold values from -6 to 6
Outputs:
- leaf_dir: float32 [32, 384], P(('leaf', 'grp'))
- node_dir: float32 [16, 128], P('grp', 'leaf')
- root_dir: float32 [128], replicated
Inputs may be any that keep to these rules, and one draw needn't show every extreme that they name: `slot_parent`: -1 marks an empty slot; otherwise the value is the section-2 node, among the 8 nodes of the slot's grp index, to which the leaf belongs. On every device the live slots come first; a device may hold no live slot or only live slots. `leaf_matrix`: each block is symmetric positive definite with smallest eigenvalue at least 0.1. `node_matrix`: each block is symmetric positive definite with smallest eigenvalue at least 0.1. `root_matrix`: symmetric positive definite with smallest eigenvalue at least 0.1.
All inputs are finite; a program needn't handle non-finite values.
Results may differ from a plain program's by a relative error of at most 0.00018.
Values sent between devices are 32-bit elements; how exact they have to be, the bound alone decides.
No kernel may reach another device: no remote copies, remote signals or barrier semaphores. Data moves between devices by JAX's collectives and lax.ppermute only.
A program may use at most 64 MiB of HBM per device.

v0:
```python
import functools

import jax
import jax.numpy as jnp
from jax import lax
from jax.experimental import pallas as pl
from jax.experimental.pallas import tpu as pltpu
from jax.sharding import PartitionSpec as P

f32 = jnp.float32
bf16 = jnp.bfloat16
FLOOR = 0.1
COARSE = 0.15
MOST_STEPS = 24
ACCEPT = 4e-8


def mul(a, b):
    return jnp.dot(a, b, preferred_element_type=f32)


def nt(a, b):
    return lax.dot_general(a, b, (((1,), (1,)), ((), ())), preferred_element_type=f32)


def split(a):
    high = a.astype(bf16)
    return high, (a - high.astype(f32)).astype(bf16)


def split3(a):
    high = a.astype(bf16)
    rest = a - high.astype(f32)
    mid = rest.astype(bf16)
    return high, mid, (rest - mid.astype(f32)).astype(bf16)


def mul3(a, b):
    ah, al = split(a)
    bh, bl = split(b)
    return mul(ah, bh) + (mul(ah, bl) + mul(al, bh))


def nt3(a, b):
    ah, al = split(a)
    bh, bl = split(b)
    return nt(ah, bh) + (nt(ah, bl) + nt(al, bh))


def grid_of(rows, cols):
    return (
        lax.broadcasted_iota(jnp.int32, (rows, cols), 0),
        lax.broadcasted_iota(jnp.int32, (rows, cols), 1),
    )


def identity(n):
    row, col = grid_of(n, n)
    return (row == col).astype(f32)


def column_of(row_vector, n):
    return jnp.broadcast_to(row_vector, (128, n)).T


def pack_symmetric(full, extra):
    n = full.shape[0]
    half = n // 2
    row, col = grid_of(half, n)
    lower = full[half:]
    moved = pltpu.roll(lower, half, 1)
    top = jnp.where(col < row, moved, full[:half])
    diagonal = jnp.sum(jnp.where(col == row + half, lower, 0.0), axis=0, keepdims=True)
    row8, _ = grid_of(8, n)
    tail = jnp.where(row8 == 0, jnp.broadcast_to(extra, (8, n)), 0.0)
    tail = jnp.where(row8 == 1, jnp.broadcast_to(diagonal, (8, n)), tail)
    return top, tail


def unpack_symmetric(top, diagonal):
    half, n = top.shape
    row, col = grid_of(half, n)
    flipped = jnp.concatenate([top, jnp.zeros_like(top)], axis=0).T
    upper = jnp.where((col < half) & (col < row), flipped[:half], top)
    inner = pltpu.roll(jnp.where(col < row, top, flipped[:half]), half, 1)
    inner = jnp.where(col == row + half, jnp.broadcast_to(diagonal, (half, n)), inner)
    lower = jnp.where(col < half, flipped[half:], inner)
    return jnp.concatenate([upper, lower], axis=0)


def coarse_inverse(count, bound, matrix_of, high, inv):
    n = high.shape[1]
    delta = (bound - FLOOR) / (bound + FLOOR)
    alpha = 2.0 / (bound + FLOOR)
    scale = alpha * 2.0 / (2.0 - delta * delta)
    for i in range(count):
        inv[i] = (scale * (2.0 * identity(n) - alpha * matrix_of(i))).astype(bf16)

    def step(carry):
        delta, count_left = carry
        scale = 2.0 / (2.0 - delta * delta)
        for i in range(count):
            now = inv[i]
            error = (identity(n) - mul(high[i], now)).astype(bf16)
            inv[i] = (scale * (now.astype(f32) + mul(now, error))).astype(bf16)
        return delta * delta / (2.0 - delta * delta), count_left - 1

    start = (delta * delta / (2.0 - delta * delta), jnp.int32(MOST_STEPS))
    lax.while_loop(lambda c: (c[0] > COARSE) & (c[1] > 0), step, start)


def refine(matrix, inverse, right):
    high, mid, low = split3(matrix)
    step0 = mul(inverse, right.astype(bf16)).astype(bf16)
    rest = right - (mul(high, step0) + (mul(mid, step0) + mul(low, step0)))
    step1 = mul(inverse, rest.astype(bf16)).astype(bf16)
    rest = rest - (mul(high, step1) + mul(mid, step1))
    step2 = mul(inverse, rest.astype(bf16)).astype(bf16)
    rest = rest - (mul(high, step2) + mul(mid, step2))
    step3 = mul(inverse, rest.astype(bf16))
    return step0.astype(f32) + (step1.astype(f32) + (step2.astype(f32) + step3)), rest


def misfits(rest, right):
    got = jnp.sum(rest * rest, axis=0, keepdims=True)
    allowed = ACCEPT * jnp.sum(right * right, axis=0, keepdims=True)
    return jnp.where(got <= allowed, 0.0, 1.0)


def eliminate(work):
    n, width = work.shape

    def step(k, carry):
        row, col = grid_of(8, width)
        base = pl.multiple_of((k // 8) * 8, 8)
        block = work[pl.ds(base, 8), :]
        pivot_row = jnp.sum(jnp.where(row == k - base, block, 0.0), axis=0, keepdims=True)
        pivot = jnp.sum(jnp.where(col[:1] == k, pivot_row, 0.0), axis=1, keepdims=True)
        scaled = pivot_row / pivot
        full = work[...]
        row, col = grid_of(n, width)
        column = jnp.sum(jnp.where(col == k, full, 0.0), axis=1, keepdims=True)
        work[...] = jnp.where(row == k, scaled, full - column * scaled)
        return carry

    lax.fori_loop(0, n, step, 0)


def leaf_kernel(parent, matrix, coupling, residual, solved, message, high, inv, work):
    n = matrix.shape[1]
    width = coupling.shape[2]
    for s in range(matrix.shape[0]):
        block = matrix[s]
        high[0] = block.astype(bf16)
        bound = jnp.max(jnp.sum(jnp.abs(block), axis=0, keepdims=True))
        coarse_inverse(1, bound, lambda i: matrix[s], high, inv)
        residual_row = residual[s : s + 1, :]
        right = jnp.concatenate([coupling[s], column_of(residual_row, n)], axis=1)
        found, rest = refine(matrix[s], inv[0], right)
        solved[s] = found

        @pl.when(jnp.sum(misfits(rest, right)) > 0.0)
        def _():
            work[:, :n] = matrix[s]
            work[:, n:] = jnp.concatenate([coupling[s], column_of(residual_row, n)], axis=1)
            eliminate(work)
            solved[s] = work[:, n:]

        left = jnp.concatenate(
            [coupling[s].T, jnp.broadcast_to(residual_row, (16, n))], axis=0
        )
        product = mul3(left, solved[s][:, :width])
        top, tail = pack_symmetric(product[:width], product[width : width + 1])
        row8, _ = grid_of(8, width)
        tail = jnp.where(row8 == 2, parent[s].astype(f32), tail)
        message[s, : width // 2, :] = top
        message[s, width // 2 :, :] = tail


def node_kernel(
    sources, groups, band, slots, messages, data, answers, message, links, rights, full, high, inv, work
):
    positions = data.shape[0]
    n = data.shape[2]
    half = n // 2
    here = lax.axis_index("leaf") if positions > 1 else 0
    rows = groups * band
    for j in range(positions):
        place = pl.multiple_of((here ^ sources[j]) * band, band) if positions > 1 else 0
        for q in range(groups):
            full[q, pl.ds(place, band), :] = data[j, q * band : (q + 1) * band, :]
            links[q, pl.ds(place, band), :] = data[j, rows + q * band : rows + (q + 1) * band, :]
    shift = data[0, 2 * rows :, :]
    for j in range(1, positions):
        shift = shift + data[j, 2 * rows :, :]
    tops = [None] * groups
    tails = [None] * groups
    for j in range(messages.shape[0]):
        owner = messages[j, half + 2 : half + 3, :]
        for q in range(groups):
            hit = owner == q
            top = jnp.where(hit, messages[j, :half, :], 0.0)
            tail = jnp.where(hit, messages[j, half:, :], 0.0)
            tops[q] = top if j == 0 else tops[q] + top
            tails[q] = tail if j == 0 else tails[q] + tail
    bound = None
    vectors = []
    for q in range(groups):
        schur = full[q] + unpack_symmetric(tops[q], tails[q][1:2])
        full[q] = schur
        high[q] = schur.astype(bf16)
        size = jnp.sum(jnp.abs(schur), axis=0, keepdims=True)
        bound = size if q == 0 else jnp.maximum(bound, size)
        vector = tails[q][:1] - shift[q : q + 1]
        vectors.append(vector)
        rights[q] = jnp.concatenate([links[q], column_of(vector, n)], axis=1)
    coarse_inverse(groups, jnp.max(bound), lambda i: full[i], high, inv)
    bad = None
    for q in range(groups):
        found, rest = refine(full[q], inv[q], rights[q])
        answers[q] = found
        wrong = misfits(rest, rights[q])
        bad = wrong if q == 0 else bad + wrong

    @pl.when(jnp.sum(bad) > 0.0)
    def _():
        def one(q, carry):
            work[:, :n] = full[q]
            work[:, n:] = rights[q]
            eliminate(work)
            answers[q] = work[:, n:]
            return carry

        lax.fori_loop(0, groups, one, 0)

    width = links.shape[2]
    total = None
    for q in range(groups):
        left = jnp.concatenate([links[q].T, jnp.broadcast_to(vectors[q], (16, n))], axis=0)
        part = mul3(left, answers[q][:, :width])
        total = part if q == 0 else total + part
    top, tail = pack_symmetric(total[:width], total[width : width + 1])
    message[: width // 2, :] = top
    message[width // 2 :, :] = tail


def root_kernel(
    groups, band, parent, part, matrix, rhs, answers, solved, leaf_dir, node_dir, root_dir, full, high, inv, work
):
    size = matrix.shape[0]
    half = size // 2
    system = matrix[...] + unpack_symmetric(part[:half, :], part[half + 1 : half + 2, :])
    full[...] = system
    high[0] = system.astype(bf16)
    bound = jnp.max(jnp.sum(jnp.abs(system), axis=0, keepdims=True))
    coarse_inverse(1, bound, lambda i: full[...], high, inv)
    right = column_of(rhs[...] - part[half : half + 1, :], size)
    found, rest = refine(full[...], inv[0], right)
    work[:, size:] = found

    @pl.when(jnp.sum(misfits(rest, right)) > 0.0)
    def _():
        work[:, :size] = full[...]
        work[:, size:] = column_of(rhs[...] - part[half : half + 1, :], size)
        eliminate(work)

    answer = work[:, size:].T[:8]
    root_dir[...] = answer[:1]
    n = answers.shape[1]
    _, col = grid_of(8, 128)
    pick = (col == 0).astype(f32)
    left = jnp.concatenate([answer, pick], axis=1)
    flat = nt3(left, answers[...].reshape(groups * n, size + 128))
    every = jnp.concatenate([flat[:1, q * n : (q + 1) * n] for q in range(groups)], axis=0)
    if band == n:
        node_dir[...] = every
    else:
        me = lax.axis_index("leaf")
        moved = pltpu.roll(every, lax.rem(n - me * band, n), 1)
        node_dir[...] = moved[:, :band]
    row, _ = grid_of(groups, n)
    for s in range(solved.shape[0]):
        q = parent[s]
        own = jnp.sum(jnp.where(row == q, every, 0.0), axis=0, keepdims=True)
        left = jnp.concatenate([-jnp.broadcast_to(own, (8, n)), pick], axis=1)
        moved = nt3(left, solved[s])[:1]
        leaf_dir[s : s + 1, :] = jnp.where(q >= 0, moved, 0.0)


def gather_steps(extent):
    steps = []
    while extent > 1:
        extent //= 2
        steps.append(extent)
    return steps


def doubled(values, axis, extent):
    for distance in gather_steps(extent):
        moved = lax.ppermute(values, axis, [(i, i ^ distance) for i in range(extent)])
        values = jnp.concatenate([values, moved], axis=0)
    return values


def source_offsets(extent):
    offsets = [0]
    for distance in gather_steps(extent):
        offsets = offsets + [o ^ distance for o in offsets]
    return tuple(offsets)


def sum_over(values, axis, extent):
    if extent & (extent - 1):
        return lax.psum(values, axis)
    for distance in reversed(gather_steps(extent)):
        values = values + lax.ppermute(values, axis, [(i, i ^ distance) for i in range(extent)])
    return values


def body(
    leaves,
    sets,
    slot_parent,
    leaf_matrix,
    coupling,
    leaf_residual_rows,
    node_matrix,
    node_link,
    node_rhs,
    root_matrix,
    root_rhs,
):
    slots, n = leaf_residual_rows.shape
    groups, band, width = node_matrix.shape
    size = node_link.shape[2]
    doubling = leaves & (leaves - 1) == 0
    shape = jax.ShapeDtypeStruct
    vmem = pl.BlockSpec(memory_space=pltpu.VMEM)
    smem = pl.BlockSpec(memory_space=pltpu.SMEM)

    rank = lax.axis_index("leaf")
    placed = lax.dynamic_update_slice(
        jnp.zeros((groups, width), f32), node_rhs, (jnp.zeros((), jnp.int32), rank * band)
    )
    if doubling and band % 8 == 0:
        own = jnp.concatenate(
            [node_matrix.reshape(-1, width), node_link.reshape(-1, width), placed], axis=0
        )
        data = doubled(own[None], "leaf", leaves)
        held = band
        sources = source_offsets(leaves)
    else:
        every = lax.all_gather(
            jnp.concatenate([node_matrix, node_link], axis=0), "leaf", axis=1, tiled=True
        )
        data = jnp.concatenate(
            [every.reshape(-1, width), lax.psum(placed, "leaf")], axis=0
        )[None]
        held = width
        sources = (0,)

    solved, message = pl.pallas_call(
        leaf_kernel,
        out_shape=(
            shape((slots, n, width + 128), f32),
            shape((slots, width // 2 + 8, width), f32),
        ),
        in_specs=[smem, vmem, vmem, vmem],
        out_specs=(vmem, vmem),
        scratch_shapes=[
            pltpu.VMEM((1, n, n), bf16),
            pltpu.VMEM((1, n, n), bf16),
            pltpu.VMEM((n, n + width + 128), f32),
        ],
        name="leaf_solve",
    )(slot_parent, leaf_matrix, coupling, leaf_residual_rows)

    if doubling:
        messages = doubled(message, "leaf", leaves)
    else:
        messages = lax.all_gather(message, "leaf", axis=0, tiled=True)

    answers, part = pl.pallas_call(
        functools.partial(node_kernel, sources, groups, held, slots),
        out_shape=(
            shape((groups, width, size + 128), f32),
            shape((size // 2 + 8, size), f32),
        ),
        in_specs=[vmem, vmem],
        out_specs=(vmem, vmem),
        scratch_shapes=[
            pltpu.VMEM((groups, width, size), f32),
            pltpu.VMEM((groups, width, size + 128), f32),
            pltpu.VMEM((groups, width, width), f32),
            pltpu.VMEM((groups, width, width), bf16),
            pltpu.VMEM((groups, width, width), bf16),
            pltpu.VMEM((width, width + size + 128), f32),
        ],
        name="node_solve",
    )(messages, data)

    part = sum_over(part, "grp", sets)

    leaf_dir, node_dir, root_dir = pl.pallas_call(
        functools.partial(root_kernel, groups, band),
        out_shape=(
            shape((slots, n), f32),
            shape((groups, band), f32),
            shape((1, size), f32),
        ),
        in_specs=[smem, vmem, vmem, vmem, vmem, vmem],
        out_specs=(vmem, vmem, vmem),
        scratch_shapes=[
            pltpu.VMEM((size, size), f32),
            pltpu.VMEM((1, size, size), bf16),
            pltpu.VMEM((1, size, size), bf16),
            pltpu.VMEM((size, size + 128), f32),
        ],
        name="root_solve",
    )(slot_parent, part, root_matrix, root_rhs[None, :], answers, solved)
    return leaf_dir, node_dir, root_dir[0]


def solution(mesh):
    return jax.shard_map(
        functools.partial(body, mesh.shape["leaf"], mesh.shape["grp"]),
        mesh=mesh,
        in_specs=(
            P(("leaf", "grp")),
            P(("leaf", "grp"), None, None),
            P(("leaf", "grp"), None, None),
            P(("leaf", "grp"), None),
            P("grp", "leaf", None),
            P("grp", "leaf", None),
            P("grp", "leaf"),
            P(),
            P(),
        ),
        out_specs=(P(("leaf", "grp"), None), P("grp", "leaf"), P()),
        check_vma=False,
    )
```

profile of v0, /device:TPU:0, one launch (start us, length us, event | category | flops | bytes accessed | tf_op | source)
XLA Modules:
  0.0 76.9 jit_solution(17339824190635781348)
XLA Ops:
  0.6 0.8 %dynamic_update_slice.3 = f32[8,128]{1,0:T(8,128)S(1)} dynamic-update-slice(f32[8,128]{1,0:T(8,128)S(1)} %broadcast_in_dim.9, f32[8,8]{1,0:T(8,128)} %param.15, s32[]{:T(128)} %constant.3.clone.1, s32[]{:T(128)S(6)} %select_n.3) | dynamic-update-slice | bytes 516 | tf_op jit(solution)/shard_map/dynamic_update_slice | solution.py:342
  1.5 0.8 %maximum_bitcast_fusion = f32[1,136,128]{2,1,0:T(8,128)S(1)} fusion(f32[8,128]{1,0:T(8,128)S(1)} %dynamic_update_slice.3, f32[64,128]{1,0:T(8,128)} %bitcast.8, f32[64,128]{1,0:T(8,128)} %bitcast.10), kind=kLoop, calls=%fused_computation.6 | loop fusion | flops 34816 | bytes 139264 | tf_op jit(solution)/shard_map/broadcast_in_dim | solution.py:349
  2.2 4.1 %collective-permute-start.4 = (f32[1,136,128]{2,1,0:T(8,128)S(1)}, f32[1,136,128]{2,1,0:T(8,128)S(1)}, u32[]{:S(2)}, u32[]{:S(2)}) collective-permute-start(f32[1,136,128]{2,1,0:T(8,128)S(1)} %maximum_bitcast_fusion), channel_id=1, source_target_pairs={{0,16},{2,18},{4,20},{6,22},{8,24},{10,26},{12,28},{14,30},{16,0},... | collective-permute-start | bytes 208904 | tf_op jit(solution)/shard_map/ppermute | solution.py:300
  7.0 8.3 %leaf_solve.1 = (f32[1,384,256]{2,1,0:T(8,128)}, f32[1,72,128]{2,1,0:T(8,128)}) custom-call(s32[1]{0:T(128)S(6)} %copy.21.parent, f32[1,384,384]{2,1,0:T(8,128)} %matrix.2, f32[1,384,128]{2,1,0:T(8,128)} %coupling.1, f32[1,384]{1,0:T(1,128)} %residual.1), custom_call_target="tpu_custom_call" | custom-call | tf_op jit(solution)/shard_map/leaf_solve/pallas_call | solution.py:362
  15.3 0.0 copy-start.2
  15.3 0.0 collective-permute-start
  15.3 0.8 %constant_dynamic-update-slice_fusion.9 = f32[16,136,128]{2,1,0:T(8,128)S(1)} fusion(f32[8,128]{1,0:T(8,128)S(1)} %dynamic_update_slice.3, f32[64,128]{1,0:T(8,128)} %bitcast.9, f32[64,128]{1,0:T(8,128)} %bitcast.11), kind=kLoop, calls=%fused_computation.16 | loop fusion | flops 34815 | bytes 139264
  16.1 0.8 %constant_dynamic-update-slice_fusion.4 = f32[16,72,128]{2,1,0:T(8,128)S(1)} fusion(f32[1,72,128]{2,1,0:T(8,128)} %get-tuple-element.10), kind=kLoop, calls=%fused_computation.11 | loop fusion | bytes 73728
  16.9 0.0 collective-permute-done.4
  16.9 2.0 %collective-permute-start.5 = (f32[2,136,128]{2,1,0:T(8,128)S(1)}, f32[2,136,128]{2,1,0:T(8,128)S(1)}, u32[]{:S(2)}, u32[]{:S(2)}) collective-permute-start(f32[2,136,128]{2,1,0:T(8,128)S(1)} %pad_maximum_fusion.4), channel_id=1, source_target_pairs={{0,8},{2,10},{4,12},{6,14},{8,0},{10,2},{12,4},{14,6},{16,24},{18,... | collective-permute-start | bytes 417800 | tf_op jit(solution)/shard_map/ppermute | solution.py:300
  18.9 1.6 %collective-permute-done = f32[1,72,128]{2,1,0:T(8,128)S(1)} collective-permute-done((f32[1,72,128]{2,1,0:T(8,128)}, f32[1,72,128]{2,1,0:T(8,128)S(1)}, u32[]{:S(2)}, u32[]{:S(2)}) %collective-permute-start) | collective-permute-done | bytes 36896 | tf_op jit(solution)/shard_map/ppermute | solution.py:300
  20.5 0.8 %pad_maximum_fusion.5 = f32[2,72,128]{2,1,0:T(8,128)S(1)} fusion(f32[1,72,128]{2,1,0:T(8,128)S(1)} %collective-permute-done, f32[1,72,128]{2,1,0:T(8,128)} %get-tuple-element.10), kind=kLoop, calls=%fused_computation.5 | loop fusion | flops 18432 | bytes 147456 | tf_op jit(solution)/shard_map/concatenate | solution.py:301
  21.3 1.7 %collective-permute-start.1 = (f32[2,72,128]{2,1,0:T(8,128)S(1)}, f32[2,72,128]{2,1,0:T(8,128)S(1)}, u32[]{:S(2)}, u32[]{:S(2)}) collective-permute-start(f32[2,72,128]{2,1,0:T(8,128)S(1)} %pad_maximum_fusion.5), channel_id=1, source_target_pairs={{0,8},{2,10},{4,12},{6,14},{8,0},{10,2},{12,4},{14,6},{16,24},{18,... | collective-permute-start | bytes 221192 | tf_op jit(solution)/shard_map/ppermute | solution.py:300
  23.0 0.0 collective-permute-done.5
  23.0 1.6 %collective-permute-start.6 = (f32[4,136,128]{2,1,0:T(8,128)S(1)}, f32[4,136,128]{2,1,0:T(8,128)S(1)}, u32[]{:S(2)}, u32[]{:S(2)}) collective-permute-start(f32[4,136,128]{2,1,0:T(8,128)S(1)} %pad_maximum_fusion.2), channel_id=1, source_target_pairs={{0,4},{2,6},{4,0},{6,2},{8,12},{10,14},{12,8},{14,10},{16,20},{18,... | collective-permute-start | bytes 835592 | tf_op jit(solution)/shard_map/ppermute | solution.py:300
  24.6 1.0 %collective-permute-done.1 = f32[2,72,128]{2,1,0:T(8,128)S(1)} collective-permute-done((f32[2,72,128]{2,1,0:T(8,128)S(1)}, f32[2,72,128]{2,1,0:T(8,128)S(1)}, u32[]{:S(2)}, u32[]{:S(2)}) %collective-permute-start.1) | collective-permute-done | bytes 73760 | tf_op jit(solution)/shard_map/ppermute | solution.py:300
  25.6 0.0 copy-done.2
  25.6 1.6 %collective-permute-start.2 = (f32[4,72,128]{2,1,0:T(8,128)S(1)}, f32[4,72,128]{2,1,0:T(8,128)S(1)}, u32[]{:S(2)}, u32[]{:S(2)}) collective-permute-start(f32[4,72,128]{2,1,0:T(8,128)S(1)} %pad_maximum_fusion.3), channel_id=1, source_target_pairs={{0,4},{2,6},{4,0},{6,2},{8,12},{10,14},{12,8},{14,10},{16,20},{18,... | collective-permute-start | bytes 442376 | tf_op jit(solution)/shard_map/ppermute | solution.py:300
  27.2 4.5 %collective-permute-done.6 = f32[4,136,128]{2,1,0:T(8,128)S(1)} collective-permute-done((f32[4,136,128]{2,1,0:T(8,128)S(1)}, f32[4,136,128]{2,1,0:T(8,128)S(1)}, u32[]{:S(2)}, u32[]{:S(2)}) %collective-permute-start.6) | collective-permute-done | bytes 278560 | tf_op jit(solution)/shard_map/ppermute | solution.py:300
  31.8 0.1 collective-permute-start.7
  31.9 1.5 %collective-permute-done.2 = f32[4,72,128]{2,1,0:T(8,128)S(1)} collective-permute-done((f32[4,72,128]{2,1,0:T(8,128)S(1)}, f32[4,72,128]{2,1,0:T(8,128)S(1)}, u32[]{:S(2)}, u32[]{:S(2)}) %collective-permute-start.2) | collective-permute-done | bytes 147488 | tf_op jit(solution)/shard_map/ppermute | solution.py:300
  33.4 0.1 collective-permute-start.3
  33.5 1.5 %collective-permute-done.3 = f32[8,72,128]{2,1,0:T(8,128)S(1)} collective-permute-done((f32[8,72,128]{2,1,0:T(8,128)S(1)}, f32[8,72,128]{2,1,0:T(8,128)S(1)}, u32[]{:S(2)}, u32[]{:S(2)}) %collective-permute-start.3) | collective-permute-done | bytes 294944 | tf_op jit(solution)/shard_map/ppermute | solution.py:300
  35.0 0.0 copy-start.1
  35.1 0.0 collective-permute-done.7
  35.1 0.7 copy-done.1
  35.9 0.0 copy-start
  35.9 1.0 %copy-done = f32[16,136,128]{2,1,0:T(8,128)} copy-done((f32[16,136,128]{2,1,0:T(8,128)}, f32[16,136,128]{2,1,0:T(8,128)S(1)}, u32[]{:S(2)}) %copy-start) | copy-done | bytes 1114136
  36.9 14.2 %node_solve.1 = (f32[8,128,256]{2,1,0:T(8,128)}, f32[72,128]{1,0:T(8,128)}) custom-call(f32[16,72,128]{2,1,0:T(8,128)} %copy-done.1, f32[16,136,128]{2,1,0:T(8,128)} %copy-done), custom_call_target="tpu_custom_call" | custom-call | tf_op jit(solution)/shard_map/node_solve/pallas_call | solution.py:383
  51.0 1.3 %collective-permute-start.8 = (f32[72,128]{1,0:T(8,128)}, f32[72,128]{1,0:T(8,128)S(1)}, u32[]{:S(2)}, u32[]{:S(2)}) collective-permute-start(f32[72,128]{1,0:T(8,128)} %get-tuple-element.11), channel_id=1, source_target_pairs={{0,1},{1,0},{2,3},{3,2},{4,5},{5,4},{6,7},{7,6},{8,9},{9,8},{10,11... | collective-permute-start | bytes 110600 | tf_op jit(solution)/shard_map/ppermute | solution.py:316
  52.4 2.8 %collective-permute-done.8 = f32[72,128]{1,0:T(8,128)S(1)} collective-permute-done((f32[72,128]{1,0:T(8,128)}, f32[72,128]{1,0:T(8,128)S(1)}, u32[]{:S(2)}, u32[]{:S(2)}) %collective-permute-start.8) | collective-permute-done | bytes 36896 | tf_op jit(solution)/shard_map/ppermute | solution.py:316
  55.2 1.4 %add.7.part = f32[72,128]{1,0:T(8,128)} add(f32[72,128]{1,0:T(8,128)} %get-tuple-element.11, f32[72,128]{1,0:T(8,128)S(1)} %collective-permute-done.8) | non-fusion elementwise | flops 9216 | bytes 110592 | tf_op jit(solution)/shard_map/add | solution.py:316
  56.6 20.3 %root_solve.1 = (f32[1,384]{1,0:T(1,128)}, f32[8,8]{1,0:T(8,128)}, f32[1,128]{1,0:T(1,128)}) custom-call(s32[1]{0:T(128)S(6)} %copy.21.parent, f32[72,128]{1,0:T(8,128)} %add.7.part, f32[128,128]{1,0:T(8,128)} %matrix.3, f32[1,128]{1,0:T(1,128)} %bitcast.12, f32[8,128,256]{2,1,0:T(8,128)} %get-tuple-element.12.answers, f32[1,384,256]{2,1,0:T(8,128)} %get-tuple-element.13.solved), custom_call_target="tpu_custom_call" | custom-call | tf_op jit(solution)/shard_map/root_solve/pallas_call | solution.py:404
  (14 shorter events, 0.2 us)
Async XLA Ops:
  2.2 14.7 %collective-permute-start.4 = (f32[1,136,128]{2,1,0:T(8,128)S(1)}, f32[1,136,128]{2,1,0:T(8,128)S(1)}, u32[]{:S(2)}, u32[]{:S(2)}) collective-permute-start(f32[1,136,128]{2,1,0:T(8,128)S(1)} %maximum_bitcast_fusion), channel_id=1, source_target_pairs={{0,16},{2,18},{4,20},{6,22},{8,24},{10,26},{12,28},{14,30},{16,0},... | collective-permute-start | bytes 208904 | tf_op jit(solution)/shard_map/ppermute | solution.py:300
  15.3 10.3 %copy-start.2 = (f32[1,72,128]{2,1,0:T(8,128)S(1)}, f32[1,72,128]{2,1,0:T(8,128)}, u32[]{:S(2)}) copy-start(f32[1,72,128]{2,1,0:T(8,128)} %get-tuple-element.10) | copy-start | bytes 110596
  15.3 5.2 %collective-permute-start = (f32[1,72,128]{2,1,0:T(8,128)}, f32[1,72,128]{2,1,0:T(8,128)S(1)}, u32[]{:S(2)}, u32[]{:S(2)}) collective-permute-start(f32[1,72,128]{2,1,0:T(8,128)} %get-tuple-element.10), channel_id=1, source_target_pairs={{0,16},{2,18},{4,20},{6,22},{8,24},{10,26},{12,28},{14,30},{16,0},... | collective-permute-start | bytes 110600 | tf_op jit(solution)/shard_map/ppermute | solution.py:300
  16.9 6.0 %collective-permute-start.5 = (f32[2,136,128]{2,1,0:T(8,128)S(1)}, f32[2,136,128]{2,1,0:T(8,128)S(1)}, u32[]{:S(2)}, u32[]{:S(2)}) collective-permute-start(f32[2,136,128]{2,1,0:T(8,128)S(1)} %pad_maximum_fusion.4), channel_id=1, source_target_pairs={{0,8},{2,10},{4,12},{6,14},{8,0},{10,2},{12,4},{14,6},{16,24},{18,... | collective-permute-start | bytes 417800 | tf_op jit(solution)/shard_map/ppermute | solution.py:300
  21.3 4.4 %collective-permute-start.1 = (f32[2,72,128]{2,1,0:T(8,128)S(1)}, f32[2,72,128]{2,1,0:T(8,128)S(1)}, u32[]{:S(2)}, u32[]{:S(2)}) collective-permute-start(f32[2,72,128]{2,1,0:T(8,128)S(1)} %pad_maximum_fusion.5), channel_id=1, source_target_pairs={{0,8},{2,10},{4,12},{6,14},{8,0},{10,2},{12,4},{14,6},{16,24},{18,... | collective-permute-start | bytes 221192 | tf_op jit(solution)/shard_map/ppermute | solution.py:300
  23.0 8.8 %collective-permute-start.6 = (f32[4,136,128]{2,1,0:T(8,128)S(1)}, f32[4,136,128]{2,1,0:T(8,128)S(1)}, u32[]{:S(2)}, u32[]{:S(2)}) collective-permute-start(f32[4,136,128]{2,1,0:T(8,128)S(1)} %pad_maximum_fusion.2), channel_id=1, source_target_pairs={{0,4},{2,6},{4,0},{6,2},{8,12},{10,14},{12,8},{14,10},{16,20},{18,... | collective-permute-start | bytes 835592 | tf_op jit(solution)/shard_map/ppermute | solution.py:300
  25.6 7.7 %collective-permute-start.2 = (f32[4,72,128]{2,1,0:T(8,128)S(1)}, f32[4,72,128]{2,1,0:T(8,128)S(1)}, u32[]{:S(2)}, u32[]{:S(2)}) collective-permute-start(f32[4,72,128]{2,1,0:T(8,128)S(1)} %pad_maximum_fusion.3), channel_id=1, source_target_pairs={{0,4},{2,6},{4,0},{6,2},{8,12},{10,14},{12,8},{14,10},{16,20},{18,... | collective-permute-start | bytes 442376 | tf_op jit(solution)/shard_map/ppermute | solution.py:300
  31.8 3.3 %collective-permute-start.7 = (f32[8,136,128]{2,1,0:T(8,128)S(1)}, f32[8,136,128]{2,1,0:T(8,128)S(1)}, u32[]{:S(2)}, u32[]{:S(2)}) collective-permute-start(f32[8,136,128]{2,1,0:T(8,128)S(1)} %pad_maximum_fusion), channel_id=1, source_target_pairs={{0,2},{2,0},{4,6},{6,4},{8,10},{10,8},{12,14},{14,12},{16,18},{18,... | collective-permute-start | bytes 1671176 | tf_op jit(solution)/shard_map/ppermute | solution.py:300
  33.4 1.6 %collective-permute-start.3 = (f32[8,72,128]{2,1,0:T(8,128)S(1)}, f32[8,72,128]{2,1,0:T(8,128)S(1)}, u32[]{:S(2)}, u32[]{:S(2)}) collective-permute-start(f32[8,72,128]{2,1,0:T(8,128)S(1)} %pad_maximum_fusion.1), channel_id=1, source_target_pairs={{0,2},{2,0},{4,6},{6,4},{8,10},{10,8},{12,14},{14,12},{16,18},{18,... | collective-permute-start | bytes 884744 | tf_op jit(solution)/shard_map/ppermute | solution.py:300
  35.0 0.8 %copy-start.1 = (f32[16,72,128]{2,1,0:T(8,128)}, f32[16,72,128]{2,1,0:T(8,128)S(1)}, u32[]{:S(2)}) copy-start(f32[16,72,128]{2,1,0:T(8,128)S(1)} %constant_dynamic-update-slice_fusion.messages) | copy-start | bytes 1769476
  35.9 1.0 %copy-start = (f32[16,136,128]{2,1,0:T(8,128)}, f32[16,136,128]{2,1,0:T(8,128)S(1)}, u32[]{:S(2)}) copy-start(f32[16,136,128]{2,1,0:T(8,128)S(1)} %constant_dynamic-update-slice_fusion.5.data) | copy-start | bytes 3342340
  51.0 4.2 %collective-permute-start.8 = (f32[72,128]{1,0:T(8,128)}, f32[72,128]{1,0:T(8,128)S(1)}, u32[]{:S(2)}, u32[]{:S(2)}) collective-permute-start(f32[72,128]{1,0:T(8,128)} %get-tuple-element.11), channel_id=1, source_target_pairs={{0,1},{1,0},{2,3},{3,2},{4,5},{5,4},{6,7},{7,6},{8,9},{9,8},{10,11... | collective-permute-start | bytes 110600 | tf_op jit(solution)/shard_map/ppermute | solution.py:316
where the time goes:
time: 77.5 us; the launch traced here: 76.9 us
  Pallas kernels  42.8 us (55%)
  waiting for transfers between devices  13 us (17%)
  starting transfers between devices  12.4 us (16%)
  other arithmetic  3.85 us (5%)
  local copies, waits for them, and re-layouts  3.45 us (4%)
  between operations  1.39 us (2%)
    pallas_call x1, Pallas kernels, body(): pl.pallas_call(functools.partial(root_kernel, groups, band), out_shape=(s...  20.3 us
    pallas_call x1, Pallas kernels, body(): pl.pallas_call(functools.partial(node_kernel, sources, groups, held, slot...  14.2 us
    ppermute x8, starting transfers between devices, doubled(): lax.ppermute(values, axis, [(i, i ^ distance) for i in range(extent)])  11.1 us
    ppermute x8, waiting for transfers between devices, doubled(): lax.ppermute(values, axis, [(i, i ^ distance) for i in range(extent)])  10.1 us
    pallas_call x1, Pallas kernels, body(): pl.pallas_call(leaf_kernel, out_shape=(shape((slots, n, width + 128), f32...  8.32 us
    ppermute x1, waiting for transfers between devices, sum_over(): lax.ppermute(values, axis, [(i, i ^ distance) for i in range(extent)])  2.84 us
    unnamed x13, local copies, waits for them, and re-layouts  2.58 us
  transfers between devices with their start and end apart: 9, of which 6 were waited for; matrix products, arithmetic and copies ran while one was open for 3% of the time, Pallas kernels for 11%

commit v1 on v0

v1 whole, which is shorter than its diff:
```python
import functools

import jax
import jax.numpy as jnp
from jax import lax
from jax.experimental import pallas as pl
from jax.experimental.pallas import tpu as pltpu
from jax.sharding import PartitionSpec as P

f32 = jnp.float32
bf16 = jnp.bfloat16
FLOOR = 0.1
COARSE = 0.04
MOST_STEPS = 24
KERNEL_VMEM = 24 << 20
ACCEPT = 4e-8


def mul(a, b):
    return jnp.dot(a, b, preferred_element_type=f32)


def split(a):
    high = a.astype(bf16)
    return high, (a - high.astype(f32)).astype(bf16)


def split3(a):
    high = a.astype(bf16)
    rest = a - high.astype(f32)
    mid = rest.astype(bf16)
    return high, mid, (rest - mid.astype(f32)).astype(bf16)


def beside(*parts):
    return jnp.concatenate(parts, axis=1)


def above(*parts):
    return jnp.concatenate(parts, axis=0)


def mul3(a, b):
    ah, al = split(a)
    bh, bl = split(b)
    return mul(beside(ah, ah, al), above(bh, bl, bh))


def grid_of(rows, cols):
    return (
        lax.broadcasted_iota(jnp.int32, (rows, cols), 0),
        lax.broadcasted_iota(jnp.int32, (rows, cols), 1),
    )


def identity(n):
    row, col = grid_of(n, n)
    return (row == col).astype(f32)


def pack_symmetric(full, extra):
    n = full.shape[0]
    half = n // 2
    row, col = grid_of(half, n)
    lower = full[half:]
    moved = pltpu.roll(lower, half, 1)
    top = jnp.where(col < row, moved, full[:half])
    diagonal = jnp.sum(jnp.where(col == row + half, lower, 0.0), axis=0, keepdims=True)
    row8, _ = grid_of(8, n)
    tail = jnp.where(row8 == 0, jnp.broadcast_to(extra, (8, n)), 0.0)
    tail = jnp.where(row8 == 1, jnp.broadcast_to(diagonal, (8, n)), tail)
    return top, tail


def unpack_symmetric(top, diagonal):
    half, n = top.shape
    row, col = grid_of(half, n)
    flipped = jnp.concatenate([top, jnp.zeros_like(top)], axis=0).T
    upper = jnp.where((col < half) & (col < row), flipped[:half], top)
    inner = pltpu.roll(jnp.where(col < row, top, flipped[:half]), half, 1)
    inner = jnp.where(col == row + half, jnp.broadcast_to(diagonal, (half, n)), inner)
    lower = jnp.where(col < half, flipped[half:], inner)
    return jnp.concatenate([upper, lower], axis=0)


def coarse_inverse(count, bound, matrix_of, high, inv):
    n = high.shape[1]
    delta = (bound - FLOOR) / (bound + FLOOR)
    alpha = 2.0 / (bound + FLOOR)
    scale = alpha * 2.0 / (2.0 - delta * delta)
    for i in range(count):
        inv[i] = (scale * (2.0 * identity(n) - alpha * matrix_of(i))).astype(bf16)

    def step(carry):
        delta, count_left = carry
        scale = 2.0 / (2.0 - delta * delta)
        now = [inv[i] for i in range(count)]
        error = [(identity(n) - mul(now[i], high[i])).astype(bf16) for i in range(count)]
        for i in range(count):
            inv[i] = (scale * (now[i].astype(f32) + mul(error[i], now[i]))).astype(bf16)
        return delta * delta / (2.0 - delta * delta), count_left - 1

    start = (delta * delta / (2.0 - delta * delta), jnp.int32(MOST_STEPS))
    lax.while_loop(lambda c: (c[0] > COARSE) & (c[1] > 0), step, start)


def refine(matrices, inverses, rights):
    pieces = [split3(m) for m in matrices]
    step0 = [mul(r.astype(bf16), v).astype(bf16) for r, v in zip(rights, inverses)]
    rest = [
        r - mul(beside(s, s, s), above(*p)) for r, s, p in zip(rights, step0, pieces)
    ]
    step1 = [mul(r.astype(bf16), v).astype(bf16) for r, v in zip(rest, inverses)]
    rest = [r - mul(beside(s, s), above(*p[:2])) for r, s, p in zip(rest, step1, pieces)]
    step2 = [mul(r.astype(bf16), v).astype(bf16) for r, v in zip(rest, inverses)]
    rest = [r - mul(beside(s, s), above(*p[:2])) for r, s, p in zip(rest, step2, pieces)]
    step3 = [mul(r.astype(bf16), v) for r, v in zip(rest, inverses)]
    found = [
        a.astype(f32) + (b.astype(f32) + (c.astype(f32) + d))
        for a, b, c, d in zip(step0, step1, step2, step3)
    ]
    return found, rest


def misfits(rest, right):
    got = jnp.sum(rest * rest, axis=1, keepdims=True)
    allowed = ACCEPT * jnp.sum(right * right, axis=1, keepdims=True)
    return jnp.where(got <= allowed, 0.0, 1.0)


def eliminate(work):
    n, width = work.shape

    def step(k, carry):
        row, col = grid_of(8, width)
        base = pl.multiple_of((k // 8) * 8, 8)
        block = work[pl.ds(base, 8), :]
        pivot_row = jnp.sum(jnp.where(row == k - base, block, 0.0), axis=0, keepdims=True)
        pivot = jnp.sum(jnp.where(col[:1] == k, pivot_row, 0.0), axis=1, keepdims=True)
        scaled = pivot_row / pivot
        full = work[...]
        row, col = grid_of(n, width)
        column = jnp.sum(jnp.where(col == k, full, 0.0), axis=1, keepdims=True)
        work[...] = jnp.where(row == k, scaled, full - column * scaled)
        return carry

    lax.fori_loop(0, n, step, 0)


def solve_again(work, matrix, right):
    n, rows = matrix.shape[0], right.shape[0]
    work[:, :n] = matrix
    padded = above(right, jnp.zeros((work.shape[1] - n - rows, n), f32))
    work[:, n:] = padded.T
    eliminate(work)
    return work[:, n:].T[:rows]


def norm_bound(matrix):
    return jnp.sum(jnp.abs(matrix), axis=0, keepdims=True)


def leaf_kernel(parent, matrix, coupling, residual, solved, message, high, inv, work):
    n = matrix.shape[1]
    width = coupling.shape[2]
    for s in range(matrix.shape[0]):
        block = matrix[s]
        high[0] = block.astype(bf16)
        coarse_inverse(1, jnp.max(norm_bound(block)), lambda i: matrix[s], high, inv)
        right = above(coupling[s].T, jnp.broadcast_to(residual[s : s + 1, :], (16, n)))
        found, rest = refine([matrix[s]], [inv[0]], [right])
        solved[s] = found[0]

        @pl.when(jnp.sum(misfits(rest[0], right)) > 0.0)
        def _():
            right = above(coupling[s].T, jnp.broadcast_to(residual[s : s + 1, :], (16, n)))
            solved[s] = solve_again(work, matrix[s], right)

        product = mul3(solved[s], coupling[s])
        top, tail = pack_symmetric(product[:width], product[width : width + 1])
        row8, _ = grid_of(8, width)
        tail = jnp.where(row8 == 2, parent[s].astype(f32), tail)
        message[s, : width // 2, :] = top
        message[s, width // 2 :, :] = tail


def node_kernel(sources, groups, band, counts, *refs):
    messages, data = refs[: counts[0]], refs[counts[0] : sum(counts)]
    answers, message, links, full, high, inv, work = refs[sum(counts) :]
    n = full.shape[1]
    width = links.shape[2]
    half = n // 2
    rows = groups * band
    here = lax.axis_index("leaf") if len(sources) > 1 else 0
    at = 0
    shift = None
    for piece in data:
        for j in range(piece.shape[0]):
            place = pl.multiple_of((here ^ sources[at]) * band, band) if len(sources) > 1 else 0
            at += 1
            for q in range(groups):
                full[q, pl.ds(place, band), :] = piece[j, q * band : (q + 1) * band, :]
                links[q, pl.ds(place, band), :] = piece[j, rows + q * band : rows + (q + 1) * band, :]
            last = piece[j, 2 * rows :, :]
            shift = last if shift is None else shift + last
    tops = [jnp.zeros((half, n), f32)] * groups
    tails = [jnp.zeros((8, n), f32)] * groups
    for piece in messages:
        for j in range(piece.shape[0]):
            owner = piece[j, half + 2 : half + 3, :]
            for q in range(groups):
                hit = owner == q
                tops[q] = tops[q] + jnp.where(hit, piece[j, :half, :], 0.0)
                tails[q] = tails[q] + jnp.where(hit, piece[j, half:, :], 0.0)
    bound = None
    vectors = []
    for q in range(groups):
        schur = full[q] + unpack_symmetric(tops[q], tails[q][1:2])
        full[q] = schur
        high[q] = schur.astype(bf16)
        size = norm_bound(schur)
        bound = size if q == 0 else jnp.maximum(bound, size)
        vectors.append(jnp.broadcast_to(tails[q][:1] - shift[q : q + 1], (16, n)))
    coarse_inverse(groups, jnp.max(bound), lambda i: full[i], high, inv)
    rights = [above(links[q].T, vectors[q]) for q in range(groups)]
    found, rest = refine(
        [full[q] for q in range(groups)], [inv[q] for q in range(groups)], rights
    )
    bad = None
    for q in range(groups):
        answers[q] = found[q]
        wrong = misfits(rest[q], rights[q])
        bad = wrong if q == 0 else bad + wrong

    @pl.when(jnp.sum(bad) > 0.0)
    def _():
        for q in range(groups):
            answers[q] = solve_again(work, full[q], above(links[q].T, vectors[q]))

    total = None
    for q in range(groups):
        part = mul3(answers[q], links[q])
        total = part if q == 0 else total + part
    top, tail = pack_symmetric(total[:width], total[width : width + 1])
    message[: width // 2, :] = top
    message[width // 2 :, :] = tail


def root_kernel(
    groups, band, count, parent, matrix, rhs, answers, solved, *refs
):
    parts = refs[:count]
    leaf_dir, node_dir, root_dir, full, high, inv, work, found_root = refs[count:]
    size = matrix.shape[0]
    half = size // 2
    n = answers.shape[2]
    part = parts[0][...]
    for other in parts[1:]:
        part = part + other[...]
    system = matrix[...] + unpack_symmetric(part[:half, :], part[half + 1 : half + 2, :])
    full[...] = system
    high[0] = system.astype(bf16)
    coarse_inverse(1, jnp.max(norm_bound(system)), lambda i: full[...], high, inv)
    right = jnp.broadcast_to(rhs[...] - part[half : half + 1, :], (16, size))
    found, rest = refine([full[...]], [inv[0]], [right])
    found_root[...] = found[0]

    @pl.when(jnp.sum(misfits(rest[0], right)) > 0.0)
    def _():
        found_root[...] = solve_again(work, full[...], right)

    answer = found_root[...]
    root_dir[...] = answer[:1]
    moves = [mul3(answer, answers[q][:size])[:1] + answers[q][size : size + 1] for q in range(groups)]
    every = above(*moves)
    if band == n:
        node_dir[...] = every
    else:
        me = lax.axis_index("leaf")
        node_dir[...] = pltpu.roll(every, lax.rem(n - me * band, n), 1)[:, :band]
    row, _ = grid_of(groups, n)
    for s in range(solved.shape[0]):
        q = parent[s]
        own = jnp.sum(jnp.where(row == q, every, 0.0), axis=0, keepdims=True)
        moved = mul3(jnp.broadcast_to(own, (16, n)), solved[s][:n])
        moved = solved[s][n : n + 1] - moved[:1]
        leaf_dir[s : s + 1, :] = jnp.where(q >= 0, moved, 0.0)


def gather_steps(extent):
    steps = []
    while extent > 1:
        extent //= 2
        steps.append(extent)
    return steps


def doubled(values, axis, extent):
    pieces = [values]
    for distance in gather_steps(extent):
        sent = pieces[0] if len(pieces) == 1 else jnp.concatenate(pieces, axis=0)
        pieces.append(lax.ppermute(sent, axis, [(i, i ^ distance) for i in range(extent)]))
    return pieces


def source_offsets(extent):
    offsets = [0]
    for distance in gather_steps(extent):
        offsets = offsets + [o ^ distance for o in offsets]
    return tuple(offsets)


def sum_parts(values, axis, extent):
    if extent & (extent - 1):
        return [lax.psum(values, axis)]
    steps = gather_steps(extent)
    for i, distance in enumerate(reversed(steps)):
        moved = lax.ppermute(values, axis, [(i, i ^ distance) for i in range(extent)])
        if i + 1 == len(steps):
            return [values, moved]
        values = values + moved
    return [values]


def local(*values):
    return [pltpu.with_memory_space_constraint(v, pltpu.VMEM) for v in values]


def body(
    leaves,
    sets,
    slot_parent,
    leaf_matrix,
    coupling,
    leaf_residual_rows,
    node_matrix,
    node_link,
    node_rhs,
    root_matrix,
    root_rhs,
):
    slots, n = leaf_residual_rows.shape
    groups, band, width = node_matrix.shape
    size = node_link.shape[2]
    doubling = leaves & (leaves - 1) == 0
    vmem = pl.BlockSpec(memory_space=pltpu.VMEM)
    smem = pl.BlockSpec(memory_space=pltpu.SMEM)
    params = pltpu.CompilerParams(vmem_limit_bytes=KERNEL_VMEM)

    rank = lax.axis_index("leaf")
    placed = lax.dynamic_update_slice(
        jnp.zeros((groups, width), f32), node_rhs, (jnp.zeros((), jnp.int32), rank * band)
    )
    if doubling and band % 8 == 0:
        own = jnp.concatenate(
            [node_matrix.reshape(-1, width), node_link.reshape(-1, width), placed], axis=0
        )
        data = doubled(own[None], "leaf", leaves)
        held = band
        sources = source_offsets(leaves)
    else:
        every = lax.all_gather(
            jnp.concatenate([node_matrix, node_link], axis=0), "leaf", axis=1, tiled=True
        )
        data = [
            jnp.concatenate([every.reshape(-1, width), lax.psum(placed, "leaf")], axis=0)[None]
        ]
        held = width
        sources = (0,)

    solved, message = pl.pallas_call(
        leaf_kernel,
        out_shape=(
            pltpu.VMEM((slots, width + 16, n), f32),
            pltpu.VMEM((slots, width // 2 + 8, width), f32),
        ),
        in_specs=[smem, vmem, vmem, vmem],
        out_specs=(vmem, vmem),
        scratch_shapes=[
            pltpu.VMEM((1, n, n), bf16),
            pltpu.VMEM((1, n, n), bf16),
            pltpu.VMEM((n, n + 2 * width), f32),
        ],
        compiler_params=params,
        name="leaf_solve",
    )(slot_parent, leaf_matrix, coupling, leaf_residual_rows)

    if doubling:
        messages = doubled(message, "leaf", leaves)
    else:
        messages = [lax.all_gather(message, "leaf", axis=0, tiled=True)]

    answers, part = pl.pallas_call(
        functools.partial(node_kernel, sources, groups, held, (len(messages), len(data))),
        out_shape=(
            pltpu.VMEM((groups, size + 16, width), f32),
            pltpu.VMEM((size // 2 + 8, size), f32),
        ),
        in_specs=[vmem] * (len(messages) + len(data)),
        out_specs=(vmem, vmem),
        scratch_shapes=[
            pltpu.VMEM((groups, width, size), f32),
            pltpu.VMEM((groups, width, width), f32),
            pltpu.VMEM((groups, width, width), bf16),
            pltpu.VMEM((groups, width, width), bf16),
            pltpu.VMEM((width, width + 2 * size), f32),
        ],
        compiler_params=params,
        name="node_solve",
    )(*local(*messages, *data))

    parts = sum_parts(part, "grp", sets)

    leaf_dir, node_dir, root_dir = pl.pallas_call(
        functools.partial(root_kernel, groups, band, len(parts)),
        out_shape=(
            jax.ShapeDtypeStruct((slots, n), f32),
            jax.ShapeDtypeStruct((groups, band), f32),
            jax.ShapeDtypeStruct((1, size), f32),
        ),
        in_specs=[smem] + [vmem] * (4 + len(parts)),
        out_specs=(vmem, vmem, vmem),
        scratch_shapes=[
            pltpu.VMEM((size, size), f32),
            pltpu.VMEM((1, size, size), bf16),
            pltpu.VMEM((1, size, size), bf16),
            pltpu.VMEM((size, 2 * size), f32),
            pltpu.VMEM((16, size), f32),
        ],
        compiler_params=params,
        name="root_solve",
    )(slot_parent, root_matrix, root_rhs[None, :], *local(answers, solved, *parts))
    return leaf_dir, node_dir, root_dir[0]


def solution(mesh):
    return jax.shard_map(
        functools.partial(body, mesh.shape["leaf"], mesh.shape["grp"]),
        mesh=mesh,
        in_specs=(
            P(("leaf", "grp")),
            P(("leaf", "grp"), None, None),
            P(("leaf", "grp"), None, None),
            P(("leaf", "grp"), None),
            P("grp", "leaf", None),
            P("grp", "leaf", None),
            P("grp", "leaf"),
            P(),
            P(),
        ),
        out_specs=(P(("leaf", "grp"), None), P("grp", "leaf"), P()),
        check_vma=False,
    )
```

time: 77.5 us -> 47.2 us (0.61)
  Pallas kernels: 42.8 us -> 12.9 us
  other arithmetic: 3.85 us -> 0.92 us
  waiting for transfers between devices: 13 us -> 15.1 us
  starting transfers between devices: 12.4 us -> 14 us
  local copies, waits for them, and re-layouts: 3.45 us -> 2.54 us
    pallas_call x3, Pallas kernels: 42.8 us -> 12.9 us  [the longest x1 4.82 us: body(): pl.pallas_call(leaf_kernel, out_shape=(pltpu.VMEM((slots, width + 16, n),...]
    ppermute x9, waiting for transfers between devices: 13 us -> 15.1 us  [the longest x8 12.6 us: doubled(): lax.ppermute(sent, axis, [(i, i ^ distance) for i in range(extent)])]
    ppermute x9, starting transfers between devices: 12.4 us -> 14 us  [the longest x8 12.5 us: doubled(): lax.ppermute(sent, axis, [(i, i ^ distance) for i in range(extent)])]
    add x1 -> x0, other arithmetic: 1.38 us -> none  [sum_over(): values + lax.ppermute(values, axis, [(i, i ^ distance) for i in range(ext...]
    unnamed x13 -> x12, local copies, waits for them, and re-layouts: 2.58 us -> 1.73 us
    unnamed x1 -> x0, other arithmetic: 0.79 us -> none
  transfers between devices with their start and end apart: 9 -> 9, of which waited for: 6 -> 7; matrix products, arithmetic and copies ran while one was open for 3% -> 0% of each run, Pallas kernels for 11% -> 10%
where the time goes in v1:
time: 47.2 us; the launch traced here: 46.9 us
  waiting for transfers between devices  15.1 us (32%)
  starting transfers between devices  14 us (30%)
  Pallas kernels  12.9 us (27%)
  local copies, waits for them, and re-layouts  2.54 us (5%)
  between operations  1.4 us (3%)
  other arithmetic  0.92 us (2%)
    ppermute x8, waiting for transfers between devices, doubled(): lax.ppermute(sent, axis, [(i, i ^ distance) for i in range(extent)])  12.6 us
    ppermute x8, starting transfers between devices, doubled(): lax.ppermute(sent, axis, [(i, i ^ distance) for i in range(extent)])  12.5 us
    pallas_call x1, Pallas kernels, body(): pl.pallas_call(leaf_kernel, out_shape=(pltpu.VMEM((slots, width + 16, n),...  4.82 us
    pallas_call x1, Pallas kernels, body(): pl.pallas_call(functools.partial(node_kernel, sources, groups, held, (len...  4.5 us
    pallas_call x1, Pallas kernels, body(): pl.pallas_call(functools.partial(root_kernel, groups, band, len(parts)),...  3.58 us
    ppermute x1, waiting for transfers between devices, sum_parts(): lax.ppermute(values, axis, [(i, i ^ distance) for i in range(extent)])  2.48 us
    unnamed x12, local copies, waits for them, and re-layouts  1.73 us
    ppermute x1, starting transfers between devices, sum_parts(): lax.ppermute(values, axis, [(i, i ^ distance) for i in range(extent)])  1.54 us
  transfers between devices with their start and end apart: 9, of which 7 were waited for; matrix products, arithmetic and copies ran while one was open for 0% of the time, Pallas kernels for 10%

profile of v1, /device:TPU:0, one launch (start us, length us, event | category | flops | bytes accessed | tf_op | source)
XLA Modules:
  0.0 46.9 jit_solution(11569389728751530649)
XLA Ops:
  0.6 0.0 copy-start.5
  0.7 0.8 %dynamic_update_slice.3 = f32[8,128]{1,0:T(8,128)S(1)} dynamic-update-slice(f32[8,128]{1,0:T(8,128)S(1)} %broadcast_in_dim.10, f32[8,8]{1,0:T(8,128)} %param.15, s32[]{:T(128)} %constant.3.clone.1, s32[]{:T(128)S(6)} %select_n.3) | dynamic-update-slice | bytes 516 | tf_op jit(solution)/shard_map/dynamic_update_slice | solution.py:351
  1.5 0.0 copy-done.5
  1.5 0.0 copy-start.1
  1.5 0.8 %maximum_bitcast_fusion.refs_5_ = f32[1,136,128]{2,1,0:T(8,128)S(1)} fusion(f32[8,128]{1,0:T(8,128)S(1)} %dynamic_update_slice.3, f32[64,128]{1,0:T(8,128)S(1)} %bitcast.7, f32[64,128]{1,0:T(8,128)} %bitcast.8), kind=kLoop, calls=%fused_computation.6 | loop fusion | flops 34816 | bytes 139264 | tf_op jit(solution)/shard_map/broadcast_in_dim | solution.py:358
  2.3 4.1 %collective-permute-start.4 = (f32[1,136,128]{2,1,0:T(8,128)S(1)}, f32[1,136,128]{2,1,0:T(8,128)S(1)}, u32[]{:S(2)}, u32[]{:S(2)}) collective-permute-start(f32[1,136,128]{2,1,0:T(8,128)S(1)} %maximum_bitcast_fusion.refs_5_), channel_id=1, source_target_pairs={{0,16},{2,18},{4,20},{6,22},{8,24},{10,26},{12,28},{14,30},{16,0},... | collective-permute-start | bytes 208904 | tf_op jit(solution)/shard_map/ppermute | solution.py:302
  6.4 3.8 %collective-permute-done.4.refs_6_ = f32[1,136,128]{2,1,0:T(8,128)S(1)} collective-permute-done((f32[1,136,128]{2,1,0:T(8,128)S(1)}, f32[1,136,128]{2,1,0:T(8,128)S(1)}, u32[]{:S(2)}, u32[]{:S(2)}) %collective-permute-start.4) | collective-permute-done | bytes 69664 | tf_op jit(solution)/shard_map/ppermute | solution.py:302
  10.2 0.0 copy-start.3
  10.2 0.7 %collective-permute-start.5 = (f32[2,136,128]{2,1,0:T(8,128)S(1)}, f32[2,136,128]{2,1,0:T(8,128)S(1)}, u32[]{:S(2)}, u32[]{:S(2)}) collective-permute-start(f32[2,136,128]{2,1,0:T(8,128)S(1)} %pad_maximum_fusion.4), channel_id=1, source_target_pairs={{0,8},{2,10},{4,12},{6,14},{8,0},{10,2},{12,4},{14,6},{16,24},{18,... | collective-permute-start | bytes 417800 | tf_op jit(solution)/shard_map/ppermute | solution.py:302
  11.5 0.0 copy-done.1
  11.6 0.0 copy-done.3
  11.6 0.0 copy-start
  11.6 1.1 %copy-done = f32[1,384,384]{2,1,0:T(8,128)S(1)} copy-done((f32[1,384,384]{2,1,0:T(8,128)S(1)}, f32[1,384,384]{2,1,0:T(8,128)}, u32[]{:S(2)}) %copy-start) | copy-done | bytes 589848
  12.6 4.8 %leaf_solve.1 = (f32[1,144,384]{2,1,0:T(8,128)S(1)}, f32[1,72,128]{2,1,0:T(8,128)S(1)}) custom-call(s32[1]{0:T(128)S(6)} %copy.13.parent, f32[1,384,384]{2,1,0:T(8,128)S(1)} %copy-done, f32[1,384,128]{2,1,0:T(8,128)S(1)} %copy-done.1, f32[1,384]{1,0:T(1,128)S(1)} %copy-done.3), custom_call_target="tpu_custom_call" | custom-call | tf_op jit(solution)/shard_map/leaf_solve/pallas_call | solution.py:371
  17.5 3.4 %collective-permute-start = (f32[1,72,128]{2,1,0:T(8,128)S(1)}, f32[1,72,128]{2,1,0:T(8,128)S(1)}, u32[]{:S(2)}, u32[]{:S(2)}) collective-permute-start(f32[1,72,128]{2,1,0:T(8,128)S(1)} %get-tuple-element.10.refs_0_), channel_id=1, source_target_pairs={{0,16},{2,18},{4,20},{6,22},{8,24},{10,26},{12,28},{14,30},{16,0},... | collective-permute-start | bytes 110600 | tf_op jit(solution)/shard_map/ppermute | solution.py:302
  20.9 0.0 collective-permute-done.5.refs_7_
  20.9 1.6 %collective-permute-start.6 = (f32[4,136,128]{2,1,0:T(8,128)S(1)}, f32[4,136,128]{2,1,0:T(8,128)S(1)}, u32[]{:S(2)}, u32[]{:S(2)}) collective-permute-start(f32[4,136,128]{2,1,0:T(8,128)S(1)} %pad_maximum_fusion.2), channel_id=1, source_target_pairs={{0,4},{2,6},{4,0},{6,2},{8,12},{10,14},{12,8},{14,10},{16,20},{18,... | collective-permute-start | bytes 835592 | tf_op jit(solution)/shard_map/ppermute | solution.py:302
  22.5 0.3 collective-permute-done.refs_1_
  22.9 0.9 %collective-permute-start.1 = (f32[2,72,128]{2,1,0:T(8,128)S(1)}, f32[2,72,128]{2,1,0:T(8,128)S(1)}, u32[]{:S(2)}, u32[]{:S(2)}) collective-permute-start(f32[2,72,128]{2,1,0:T(8,128)S(1)} %pad_maximum_fusion.5), channel_id=1, source_target_pairs={{0,8},{2,10},{4,12},{6,14},{8,0},{10,2},{12,4},{14,6},{16,24},{18,... | collective-permute-start | bytes 221192 | tf_op jit(solution)/shard_map/ppermute | solution.py:302
  23.8 3.4 %collective-permute-done.1.refs_2_ = f32[2,72,128]{2,1,0:T(8,128)S(1)} collective-permute-done((f32[2,72,128]{2,1,0:T(8,128)S(1)}, f32[2,72,128]{2,1,0:T(8,128)S(1)}, u32[]{:S(2)}, u32[]{:S(2)}) %collective-permute-start.1) | collective-permute-done | bytes 73760 | tf_op jit(solution)/shard_map/ppermute | solution.py:302
  27.2 1.6 %collective-permute-start.2 = (f32[4,72,128]{2,1,0:T(8,128)S(1)}, f32[4,72,128]{2,1,0:T(8,128)S(1)}, u32[]{:S(2)}, u32[]{:S(2)}) collective-permute-start(f32[4,72,128]{2,1,0:T(8,128)S(1)} %pad_maximum_fusion.3), channel_id=1, source_target_pairs={{0,4},{2,6},{4,0},{6,2},{8,12},{10,14},{12,8},{14,10},{16,20},{18,... | collective-permute-start | bytes 442376 | tf_op jit(solution)/shard_map/ppermute | solution.py:302
  28.8 0.8 %collective-permute-done.6.refs_8_ = f32[4,136,128]{2,1,0:T(8,128)S(1)} collective-permute-done((f32[4,136,128]{2,1,0:T(8,128)S(1)}, f32[4,136,128]{2,1,0:T(8,128)S(1)}, u32[]{:S(2)}, u32[]{:S(2)}) %collective-permute-start.6) | collective-permute-done | bytes 278560 | tf_op jit(solution)/shard_map/ppermute | solution.py:302
  29.7 0.1 collective-permute-start.7
  29.8 2.7 %collective-permute-done.2.refs_3_ = f32[4,72,128]{2,1,0:T(8,128)S(1)} collective-permute-done((f32[4,72,128]{2,1,0:T(8,128)S(1)}, f32[4,72,128]{2,1,0:T(8,128)S(1)}, u32[]{:S(2)}, u32[]{:S(2)}) %collective-permute-start.2) | collective-permute-done | bytes 147488 | tf_op jit(solution)/shard_map/ppermute | solution.py:302
  32.5 0.0 copy-start.2
  32.5 0.1 collective-permute-start.3
  32.6 1.6 %collective-permute-done.3.refs_4_ = f32[8,72,128]{2,1,0:T(8,128)S(1)} collective-permute-done((f32[8,72,128]{2,1,0:T(8,128)S(1)}, f32[8,72,128]{2,1,0:T(8,128)S(1)}, u32[]{:S(2)}, u32[]{:S(2)}) %collective-permute-start.3) | collective-permute-done | bytes 294944 | tf_op jit(solution)/shard_map/ppermute | solution.py:302
  34.1 0.0 collective-permute-done.7.refs_9_
  34.1 4.5 %node_solve.1 = (f32[8,144,128]{2,1,0:T(8,128)S(1)}, f32[72,128]{1,0:T(8,128)S(1)}) custom-call(f32[1,72,128]{2,1,0:T(8,128)S(1)} %get-tuple-element.10.refs_0_, f32[1,72,128]{2,1,0:T(8,128)S(1)} %collective-permute-done.refs_1_, f32[2,72,128]{2,1,0:T(8,128)S(1)} %collective-permute-done.1.refs_2_, f32[4,72,128]{2,1,0:T(8,128)S(1)} %collective-permute-done.2.refs_3_, ...), custom_call_target="tpu_custom_call" | custom-call | tf_op jit(solution)/shard_map/node_solve/pallas_call | solution.py:393
  38.6 1.5 %collective-permute-start.8 = (f32[72,128]{1,0:T(8,128)S(1)}, f32[72,128]{1,0:T(8,128)S(1)}, u32[]{:S(2)}, u32[]{:S(2)}) collective-permute-start(f32[72,128]{1,0:T(8,128)S(1)} %get-tuple-element.13.refs_0_), channel_id=1, source_target_pairs={{0,1},{1,0},{2,3},{3,2},{4,5},{5,4},{6,7},{7,6},{8,9},{9,8},{10,11... | collective-permute-start | bytes 110600 | tf_op jit(solution)/shard_map/ppermute | solution.py:318
  40.2 2.5 %collective-permute-done.8.refs_1_ = f32[72,128]{1,0:T(8,128)S(1)} collective-permute-done((f32[72,128]{1,0:T(8,128)S(1)}, f32[72,128]{1,0:T(8,128)S(1)}, u32[]{:S(2)}, u32[]{:S(2)}) %collective-permute-start.8) | collective-permute-done | bytes 36896 | tf_op jit(solution)/shard_map/ppermute | solution.py:318
  42.7 0.0 copy-start.4
  42.7 0.0 copy-done.2
  42.7 0.7 %copy-done.4 = f32[128]{0:T(128)S(1)} copy-done((f32[128]{0:T(128)S(1)}, f32[128]{0:T(128)}, u32[]{:S(2)}) %copy-start.4) | copy-done | bytes 536
  43.3 3.6 %root_solve.1 = (f32[1,384]{1,0:T(1,128)}, f32[8,8]{1,0:T(8,128)}, f32[1,128]{1,0:T(1,128)}) custom-call(s32[1]{0:T(128)S(6)} %copy.13.parent, f32[128,128]{1,0:T(8,128)S(1)} %copy-done.2, f32[1,128]{1,0:T(1,128)S(1)} %bitcast.6, f32[8,144,128]{2,1,0:T(8,128)S(1)} %get-tuple-element.11.answers, f32[1,144,384]{2,1,0:T(8,128)S(1)} %get-tuple-element.12.solved, ...), custom_call_target="tpu_custom_call" | custom-call | tf_op jit(solution)/shard_map/root_solve/pallas_call | solution.py:414
  (7 shorter events, 0.1 us)
Async XLA Ops:
  0.6 0.8 %copy-start.5 = (f32[8,8,128]{2,1,0:T(8,128)S(1)}, f32[8,8,128]{2,1,0:T(8,128)}, u32[]{:S(2)}) copy-start(f32[8,8,128]{2,1,0:T(8,128)} %param.14) | copy-start | bytes 98308
  1.5 10.1 %copy-start.1 = (f32[1,384,128]{2,1,0:T(8,128)S(1)}, f32[1,384,128]{2,1,0:T(8,128)}, u32[]{:S(2)}) copy-start(f32[1,384,128]{2,1,0:T(8,128)} %coupling.1) | copy-start | bytes 589828
  2.3 7.9 %collective-permute-start.4 = (f32[1,136,128]{2,1,0:T(8,128)S(1)}, f32[1,136,128]{2,1,0:T(8,128)S(1)}, u32[]{:S(2)}, u32[]{:S(2)}) collective-permute-start(f32[1,136,128]{2,1,0:T(8,128)S(1)} %maximum_bitcast_fusion.refs_5_), channel_id=1, source_target_pairs={{0,16},{2,18},{4,20},{6,22},{8,24},{10,26},{12,28},{14,30},{16,0},... | collective-permute-start | bytes 208904 | tf_op jit(solution)/shard_map/ppermute | solution.py:302
  10.2 1.4 %copy-start.3 = (f32[1,384]{1,0:T(1,128)S(1)}, f32[1,384]{1,0:T(1,128)}, u32[]{:S(2)}) copy-start(f32[1,384]{1,0:T(1,128)} %residual.1) | copy-start | bytes 4612
  10.2 10.7 %collective-permute-start.5 = (f32[2,136,128]{2,1,0:T(8,128)S(1)}, f32[2,136,128]{2,1,0:T(8,128)S(1)}, u32[]{:S(2)}, u32[]{:S(2)}) collective-permute-start(f32[2,136,128]{2,1,0:T(8,128)S(1)} %pad_maximum_fusion.4), channel_id=1, source_target_pairs={{0,8},{2,10},{4,12},{6,14},{8,0},{10,2},{12,4},{14,6},{16,24},{18,... | collective-permute-start | bytes 417800 | tf_op jit(solution)/shard_map/ppermute | solution.py:302
  11.6 1.1 %copy-start = (f32[1,384,384]{2,1,0:T(8,128)S(1)}, f32[1,384,384]{2,1,0:T(8,128)}, u32[]{:S(2)}) copy-start(f32[1,384,384]{2,1,0:T(8,128)} %matrix.2) | copy-start | bytes 1769476
  17.5 5.4 %collective-permute-start = (f32[1,72,128]{2,1,0:T(8,128)S(1)}, f32[1,72,128]{2,1,0:T(8,128)S(1)}, u32[]{:S(2)}, u32[]{:S(2)}) collective-permute-start(f32[1,72,128]{2,1,0:T(8,128)S(1)} %get-tuple-element.10.refs_0_), channel_id=1, source_target_pairs={{0,16},{2,18},{4,20},{6,22},{8,24},{10,26},{12,28},{14,30},{16,0},... | collective-permute-start | bytes 110600 | tf_op jit(solution)/shard_map/ppermute | solution.py:302
  20.9 8.7 %collective-permute-start.6 = (f32[4,136,128]{2,1,0:T(8,128)S(1)}, f32[4,136,128]{2,1,0:T(8,128)S(1)}, u32[]{:S(2)}, u32[]{:S(2)}) collective-permute-start(f32[4,136,128]{2,1,0:T(8,128)S(1)} %pad_maximum_fusion.2), channel_id=1, source_target_pairs={{0,4},{2,6},{4,0},{6,2},{8,12},{10,14},{12,8},{14,10},{16,20},{18,... | collective-permute-start | bytes 835592 | tf_op jit(solution)/shard_map/ppermute | solution.py:302
  22.9 4.4 %collective-permute-start.1 = (f32[2,72,128]{2,1,0:T(8,128)S(1)}, f32[2,72,128]{2,1,0:T(8,128)S(1)}, u32[]{:S(2)}, u32[]{:S(2)}) collective-permute-start(f32[2,72,128]{2,1,0:T(8,128)S(1)} %pad_maximum_fusion.5), channel_id=1, source_target_pairs={{0,8},{2,10},{4,12},{6,14},{8,0},{10,2},{12,4},{14,6},{16,24},{18,... | collective-permute-start | bytes 221192 | tf_op jit(solution)/shard_map/ppermute | solution.py:302
  27.2 5.2 %collective-permute-start.2 = (f32[4,72,128]{2,1,0:T(8,128)S(1)}, f32[4,72,128]{2,1,0:T(8,128)S(1)}, u32[]{:S(2)}, u32[]{:S(2)}) collective-permute-start(f32[4,72,128]{2,1,0:T(8,128)S(1)} %pad_maximum_fusion.3), channel_id=1, source_target_pairs={{0,4},{2,6},{4,0},{6,2},{8,12},{10,14},{12,8},{14,10},{16,20},{18,... | collective-permute-start | bytes 442376 | tf_op jit(solution)/shard_map/ppermute | solution.py:302
  29.7 4.4 %collective-permute-start.7 = (f32[8,136,128]{2,1,0:T(8,128)S(1)}, f32[8,136,128]{2,1,0:T(8,128)S(1)}, u32[]{:S(2)}, u32[]{:S(2)}) collective-permute-start(f32[8,136,128]{2,1,0:T(8,128)S(1)} %pad_maximum_fusion), channel_id=1, source_target_pairs={{0,2},{2,0},{4,6},{6,4},{8,10},{10,8},{12,14},{14,12},{16,18},{18,... | collective-permute-start | bytes 1671176 | tf_op jit(solution)/shard_map/ppermute | solution.py:302
  32.5 10.2 %copy-start.2 = (f32[128,128]{1,0:T(8,128)S(1)}, f32[128,128]{1,0:T(8,128)}, u32[]{:S(2)}) copy-start(f32[128,128]{1,0:T(8,128)} %matrix.3) | copy-start | bytes 196612
  32.5 1.6 %collective-permute-start.3 = (f32[8,72,128]{2,1,0:T(8,128)S(1)}, f32[8,72,128]{2,1,0:T(8,128)S(1)}, u32[]{:S(2)}, u32[]{:S(2)}) collective-permute-start(f32[8,72,128]{2,1,0:T(8,128)S(1)} %pad_maximum_fusion.1), channel_id=1, source_target_pairs={{0,2},{2,0},{4,6},{6,4},{8,10},{10,8},{12,14},{14,12},{16,18},{18,... | collective-permute-start | bytes 884744 | tf_op jit(solution)/shard_map/ppermute | solution.py:302
  38.6 4.0 %collective-permute-start.8 = (f32[72,128]{1,0:T(8,128)S(1)}, f32[72,128]{1,0:T(8,128)S(1)}, u32[]{:S(2)}, u32[]{:S(2)}) collective-permute-start(f32[72,128]{1,0:T(8,128)S(1)} %get-tuple-element.13.refs_0_), channel_id=1, source_target_pairs={{0,1},{1,0},{2,3},{3,2},{4,5},{5,4},{6,7},{7,6},{8,9},{9,8},{10,11... | collective-permute-start | bytes 110600 | tf_op jit(solution)/shard_map/ppermute | solution.py:318
  42.7 0.7 %copy-start.4 = (f32[128]{0:T(128)S(1)}, f32[128]{0:T(128)}, u32[]{:S(2)}) copy-start(f32[128]{0:T(128)} %param.17) | copy-start | bytes 1540

commit v2 on v1

v2 whole, which is shorter than its diff:
```python
import functools

import jax
import jax.numpy as jnp
from jax import lax
from jax.experimental import pallas as pl
from jax.experimental.pallas import tpu as pltpu
from jax.sharding import PartitionSpec as P

f32 = jnp.float32
bf16 = jnp.bfloat16
FLOOR = 0.1
STEPS = 5
ROOT_STEPS = 6
COST = 3_000_000_000
KERNEL_VMEM = 24 << 20
ACCEPT = 4e-5


def mul(a, b):
    return jnp.dot(a, b, preferred_element_type=f32)


def split(a):
    high = a.astype(bf16)
    return high, (a - high.astype(f32)).astype(bf16)


def split3(a):
    high = a.astype(bf16)
    rest = a - high.astype(f32)
    mid = rest.astype(bf16)
    return high, mid, (rest - mid.astype(f32)).astype(bf16)


def beside(*parts):
    return jnp.concatenate(parts, axis=1)


def above(*parts):
    return jnp.concatenate(parts, axis=0)


def mul3(a, b):
    ah, al = split(a)
    bh, bl = split(b)
    return mul(beside(ah, ah, al), above(bh, bl, bh))


def grid_of(rows, cols):
    return (
        lax.broadcasted_iota(jnp.int32, (rows, cols), 0),
        lax.broadcasted_iota(jnp.int32, (rows, cols), 1),
    )


def identity(n):
    row, col = grid_of(n, n)
    return (row == col).astype(f32)


def pack_symmetric(full, extra):
    n = full.shape[0]
    half = n // 2
    row, col = grid_of(half, n)
    lower = full[half:]
    moved = pltpu.roll(lower, half, 1)
    top = jnp.where(col < row, moved, full[:half])
    diagonal = jnp.sum(jnp.where(col == row + half, lower, 0.0), axis=0, keepdims=True)
    row8, _ = grid_of(8, n)
    tail = jnp.where(row8 == 0, jnp.broadcast_to(extra, (8, n)), 0.0)
    tail = jnp.where(row8 == 1, jnp.broadcast_to(diagonal, (8, n)), tail)
    return top, tail


def unpack_symmetric(top, diagonal):
    half, n = top.shape
    row, col = grid_of(half, n)
    flipped = jnp.concatenate([top, jnp.zeros_like(top)], axis=0).T
    upper = jnp.where((col < half) & (col < row), flipped[:half], top)
    inner = pltpu.roll(jnp.where(col < row, top, flipped[:half]), half, 1)
    inner = jnp.where(col == row + half, jnp.broadcast_to(diagonal, (half, n)), inner)
    lower = jnp.where(col < half, flipped[half:], inner)
    return jnp.concatenate([upper, lower], axis=0)


def coarse_inverse(bound, matrices, steps):
    one = identity(matrices[0].shape[0])
    alpha = 2.0 / (bound + FLOOR)
    delta = (bound - FLOOR) / (bound + FLOOR)
    square = delta * delta
    scale = 2.0 / (2.0 - square)
    scaled = [alpha * m for m in matrices]
    errors = [(one - s).astype(bf16) for s in scaled]
    inverses = [((scale * alpha) * (2.0 * one - s)).astype(bf16) for s in scaled]
    for _ in range(steps - 1):
        errors = [(scale * (mul(e, e) - (0.5 * square) * one)).astype(bf16) for e in errors]
        delta = square / (2.0 - square)
        square = delta * delta
        scale = 2.0 / (2.0 - square)
        inverses = [
            (scale * (v.astype(f32) + mul(e, v))).astype(bf16) for e, v in zip(errors, inverses)
        ]
    return inverses


def finish(matrices, inverses, rights):
    errors = [
        identity(m.shape[0]) - mul(beside(v, v, v), above(*split3(m)))
        for m, v in zip(matrices, inverses)
    ]
    pieces = [split(e) for e in errors]
    squares = [mul(h, h).astype(bf16) for h, _ in pieces]
    first = []
    for right, (eh, el) in zip(rights, pieces):
        rh, rl = split(right)
        first.append(right + mul(beside(rh, rh, rl), above(eh, el, eh)))
    second = [mul(z.astype(bf16), s) for z, s in zip(first, squares)]
    found = [
        mul(beside(*split3(z + d)), above(v, v, v)) for z, d, v in zip(first, second, inverses)
    ]
    return found, [misfits(d, z) for z, d in zip(first, second)]


def misfits(change, values):
    got = jnp.sum(change * change, axis=1, keepdims=True)
    allowed = ACCEPT * jnp.sum(values * values, axis=1, keepdims=True)
    return jnp.where(got <= allowed, 0.0, 1.0)


def eliminate(work):
    n, width = work.shape

    def step(k, carry):
        row, col = grid_of(8, width)
        base = pl.multiple_of((k // 8) * 8, 8)
        block = work[pl.ds(base, 8), :]
        pivot_row = jnp.sum(jnp.where(row == k - base, block, 0.0), axis=0, keepdims=True)
        pivot = jnp.sum(jnp.where(col[:1] == k, pivot_row, 0.0), axis=1, keepdims=True)
        scaled = pivot_row / pivot
        full = work[...]
        row, col = grid_of(n, width)
        column = jnp.sum(jnp.where(col == k, full, 0.0), axis=1, keepdims=True)
        work[...] = jnp.where(row == k, scaled, full - column * scaled)
        return carry

    lax.fori_loop(0, n, step, 0)


def solve_again(work, matrix, right):
    n, rows = matrix.shape[0], right.shape[0]
    work[:, :n] = matrix
    padded = above(right, jnp.zeros((work.shape[1] - n - rows, n), f32))
    work[:, n:] = padded.T
    eliminate(work)
    return work[:, n:].T[:rows]


def norm_bound(*matrices):
    sums = [jnp.sum(jnp.abs(m), axis=0, keepdims=True) for m in matrices]
    most = sums[0]
    for other in sums[1:]:
        most = jnp.maximum(most, other)
    return jnp.max(most, axis=1, keepdims=True)


def stage_kernel(parent, matrix, link, rhs, owners, own, matrix_rows, link_rows, rhs_rows, sems):
    copies = [
        pltpu.make_async_copy(source, target, sems.at[i])
        for i, (source, target) in enumerate(
            ((matrix, matrix_rows), (link, link_rows), (rhs, rhs_rows))
        )
    ]
    for copy in copies:
        copy.start()
    for s in range(owners.shape[0]):
        owners[s] = jnp.full(owners.shape[1:], parent[s].astype(f32))
    groups, band, _ = matrix_rows.shape
    rows = groups * band
    own[0, 2 * rows :, :] = jnp.zeros((groups, own.shape[2]), f32)
    for copy in copies:
        copy.wait()
    for q in range(groups):
        own[0, q * band : (q + 1) * band, :] = matrix_rows[q]
        own[0, rows + q * band : rows + (q + 1) * band, :] = link_rows[q]
    own[0, 2 * rows :, :band] = rhs_rows[...]


def invert_kernel(*refs):
    count = (len(refs) - 2) // 2
    inputs, outputs, (inverse, sems) = refs[:count], refs[count:-2], refs[-2:]
    copies = [
        pltpu.make_async_copy(source, target, sems.at[i])
        for i, (source, target) in enumerate(zip(inputs, outputs))
    ]
    for copy in copies:
        copy.start()
    copies[0].wait()
    matrix = outputs[0]
    for s in range(matrix.shape[0]):
        block = matrix[s]
        inverse[s] = coarse_inverse(norm_bound(block), [block], STEPS)[0]
    for copy in copies[1:]:
        copy.wait()


def leaf_kernel(owners, matrix, coupling, residual, inverse, solved, message, work):
    n = matrix.shape[1]
    width = coupling.shape[2]
    for s in range(matrix.shape[0]):
        right = above(coupling[s].T, jnp.broadcast_to(residual[s : s + 1, :], (16, n)))
        found, bad = finish([matrix[s]], [inverse[s]], [right])
        solved[s] = found[0]

        @pl.when(jnp.sum(bad[0]) > 0.0)
        def _():
            right = above(coupling[s].T, jnp.broadcast_to(residual[s : s + 1, :], (16, n)))
            solved[s] = solve_again(work, matrix[s], right)

        product = mul3(solved[s], coupling[s])
        top, tail = pack_symmetric(product[:width], product[width : width + 1])
        row8, _ = grid_of(8, width)
        tail = jnp.where(row8 == 2, owners[s], tail)
        message[s, : width // 2, :] = top
        message[s, width // 2 :, :] = tail


def assemble_kernel(sources, groups, band, *refs):
    data = refs[:-3]
    full, links, shift = refs[-3:]
    rows = groups * band
    here = lax.axis_index("leaf") if len(sources) > 1 else 0
    at = 0
    total = None
    for piece in data:
        for j in range(piece.shape[0]):
            place = pl.multiple_of((here ^ sources[at]) * band, band) if len(sources) > 1 else 0
            at += 1
            for q in range(groups):
                full[q, pl.ds(place, band), :] = piece[j, q * band : (q + 1) * band, :]
                links[q, pl.ds(place, band), :] = piece[j, rows + q * band : rows + (q + 1) * band, :]
            last = piece[j, 2 * rows :, :]
            if len(sources) > 1:
                last = pltpu.roll(last, place, 1)
            total = last if total is None else total + last
    shift[...] = total


def node_kernel(regular, links, shift, *refs):
    messages = refs[:-5]
    answers, message, full, rights, work = refs[-5:]
    groups, n, width = links.shape
    half = n // 2
    tops = [jnp.zeros((half, n), f32)] * groups
    tails = [jnp.zeros((8, n), f32)] * groups
    for piece in messages:
        for j in range(piece.shape[0]):
            owner = piece[j, half + 2 : half + 3, :]
            for q in range(groups):
                hit = owner == q
                tops[q] = tops[q] + jnp.where(hit, piece[j, :half, :], 0.0)
                tails[q] = tails[q] + jnp.where(hit, piece[j, half:, :], 0.0)
    for q in range(groups):
        full[q] = regular[q] + unpack_symmetric(tops[q], tails[q][1:2])
        rights[q, :width] = links[q].T
        rights[q, width:] = jnp.broadcast_to(tails[q][:1] - shift[q : q + 1], (16, n))
    blocks = [full[q] for q in range(groups)]
    inverses = coarse_inverse(norm_bound(*blocks), blocks, STEPS)
    found, bad = finish(blocks, inverses, [rights[q] for q in range(groups)])
    for q in range(groups):
        answers[q] = found[q]

    @pl.when(jnp.sum(sum(bad)) > 0.0)
    def _():
        for q in range(groups):
            answers[q] = solve_again(work, full[q], rights[q])

    total = None
    for q in range(groups):
        part = mul3(answers[q], links[q])
        total = part if q == 0 else total + part
    top, tail = pack_symmetric(total[:width], total[width : width + 1])
    message[: width // 2, :] = top
    message[width // 2 :, :] = tail


def prepare_kernel(
    owners, part, matrix, rhs, answers, solved, base, base_row, moves, fixed, leaf_moves, leaf_fixed
):
    size = matrix.shape[0]
    half = size // 2
    groups, _, n = answers.shape
    base[...] = matrix[...] + unpack_symmetric(part[:half, :], part[half + 1 : half + 2, :])
    base_row[...] = jnp.broadcast_to(rhs[...] - part[half : half + 1, :], base_row.shape)
    for q in range(groups):
        fixed[q : q + 1, :] = answers[q, size : size + 1, :]
        moves[q] = answers[q, :size, :]
    for s in range(solved.shape[0]):
        owner = owners[s, :1, :1]
        own = jnp.zeros_like(answers[0])
        for q in range(groups):
            own = jnp.where(owner == q, answers[q], own)
        product = mul3(own, solved[s, :n, :])
        live = owner >= 0.0
        leaf_moves[s] = jnp.where(live, -product[:size], 0.0)
        last = solved[s, n : n + 8, :] - product[size : size + 8]
        leaf_fixed[s] = jnp.where(live, last, 0.0)


def root_kernel(
    band, base, base_row, moves, fixed, leaf_moves, leaf_fixed, *refs
):
    others = refs[:-6]
    leaf_dir, node_dir, root_dir, full, found_root, work = refs[-6:]
    size = base.shape[0]
    half = size // 2
    groups, _, n = moves.shape
    system = base[...]
    right = base_row[...]
    for other in others:
        system = system + unpack_symmetric(other[:half, :], other[half + 1 : half + 2, :])
        right = right - other[half : half + 1, :]
    full[...] = system
    inverses = coarse_inverse(norm_bound(system), [system], ROOT_STEPS)
    found, bad = finish([system], inverses, [right])
    found_root[...] = found[0]

    @pl.when(jnp.sum(bad[0]) > 0.0)
    def _():
        found_root[...] = solve_again(work, full[...], right)

    answer = found_root[:1, :]
    root_dir[...] = answer
    column = jnp.broadcast_to(answer, (size, size)).T
    each = [jnp.sum(column * moves[q], axis=0, keepdims=True) for q in range(groups)]
    every = above(*each) + fixed[...]
    if band == n:
        node_dir[...] = every
    else:
        me = lax.axis_index("leaf")
        node_dir[...] = pltpu.roll(every, lax.rem(n - me * band, n), 1)[:, :band]
    wide = leaf_moves.shape[2] // size
    for s in range(leaf_moves.shape[0]):
        terms = beside(*[column] * wide) * leaf_moves[s]
        leaf_dir[s : s + 1, :] = jnp.sum(terms, axis=0, keepdims=True) + leaf_fixed[s, :1, :]


def gather_steps(extent):
    steps = []
    while extent > 1:
        extent //= 2
        steps.append(extent)
    return steps


def moved(values, axis, extent, distance):
    return lax.ppermute(values, axis, [(i, i ^ distance) for i in range(extent)])


def exchange(pieces, axis, extent, distance):
    sent = pieces[0] if len(pieces) == 1 else jnp.concatenate(pieces, axis=0)
    pieces.append(moved(sent, axis, extent, distance))


def doubled(values, axis, extent):
    pieces = [values]
    for distance in gather_steps(extent):
        exchange(pieces, axis, extent, distance)
    return pieces


def after(value, pieces):
    value, pieces[-1] = lax.optimization_barrier((value, pieces[-1]))
    return value


def source_offsets(steps):
    offsets = [0]
    for distance in steps:
        offsets = offsets + [o ^ distance for o in offsets]
    return tuple(offsets)


def other_parts(values, axis, extent):
    if extent == 1:
        return []
    if extent & (extent - 1):
        return [lax.psum(values, axis) - values]
    steps = gather_steps(extent)
    pieces = []
    for distance in reversed(steps):
        pieces.append(moved(values, axis, extent, distance))
        values = values + pieces[-1]
    return pieces


def remote(*values):
    return [pltpu.with_memory_space_constraint(v, pltpu.HBM) for v in values]


def local(*values):
    return [pltpu.with_memory_space_constraint(v, pltpu.VMEM) for v in values]


def body(
    leaves,
    sets,
    slot_parent,
    leaf_matrix,
    coupling,
    leaf_residual_rows,
    node_matrix,
    node_link,
    node_rhs,
    root_matrix,
    root_rhs,
):
    slots, n = leaf_residual_rows.shape
    groups, band, width = node_matrix.shape
    size = node_link.shape[2]
    doubling = leaves & (leaves - 1) == 0
    vmem = pl.BlockSpec(memory_space=pltpu.VMEM)
    smem = pl.BlockSpec(memory_space=pltpu.SMEM)
    params = pltpu.CompilerParams(vmem_limit_bytes=KERNEL_VMEM)

    paced = doubling and band % 8 == 0
    hbm = pl.BlockSpec(memory_space=pltpu.HBM)
    nodes = [node_matrix, node_link, node_rhs]
    owners, own = pl.pallas_call(
        stage_kernel,
        out_shape=(
            pltpu.VMEM((slots, 8, width), f32),
            pltpu.VMEM((1, 2 * groups * band + groups, width), f32),
        ),
        in_specs=[smem, hbm, hbm, hbm],
        out_specs=(vmem, vmem),
        scratch_shapes=[pltpu.VMEM(a.shape, f32) for a in nodes] + [pltpu.SemaphoreType.DMA((3,))],
        compiler_params=params,
        name="stage",
    )(slot_parent, *remote(*nodes))
    if paced:
        data = [own]
        order = [4, 8, 2, 1]
        held = band
        sources = source_offsets(order)
    else:
        rank = lax.axis_index("leaf")
        placed = lax.dynamic_update_slice(
            jnp.zeros((groups, width), f32), node_rhs, (jnp.zeros((), jnp.int32), rank * band)
        )
        every = lax.all_gather(
            jnp.concatenate([node_matrix, node_link], axis=0), "leaf", axis=1, tiled=True
        )
        data = [
            jnp.concatenate([every.reshape(-1, width), lax.psum(placed, "leaf")], axis=0)[None]
        ]
        held = width
        sources = (0,)

    if paced:
        exchange(data, "leaf", leaves, 4)
    staged = [leaf_matrix, coupling, leaf_residual_rows, root_matrix, root_rhs[None, :]]
    leaf_matrix, coupling, leaf_residual_rows, root_matrix, root_row, inverse = pl.pallas_call(
        invert_kernel,
        out_shape=[pltpu.VMEM(a.shape, f32) for a in staged] + [pltpu.VMEM((slots, n, n), bf16)],
        in_specs=[hbm] * len(staged),
        out_specs=[vmem] * (len(staged) + 1),
        scratch_shapes=[pltpu.SemaphoreType.DMA((len(staged),))],
        compiler_params=params,
        cost_estimate=pl.CostEstimate(flops=COST, bytes_accessed=0, transcendentals=0),
        name="leaf_invert",
    )(*remote(*staged))
    if paced:
        inverse = after(inverse, data)
        exchange(data, "leaf", leaves, 8)
    solved, message = pl.pallas_call(
        leaf_kernel,
        out_shape=(
            pltpu.VMEM((slots, width + 16, n), f32),
            pltpu.VMEM((slots, width // 2 + 8, width), f32),
        ),
        in_specs=[vmem] * 5,
        out_specs=(vmem, vmem),
        scratch_shapes=[
            pltpu.VMEM((n, n + 2 * width), f32),
        ],
        compiler_params=params,
        cost_estimate=pl.CostEstimate(flops=COST, bytes_accessed=0, transcendentals=0),
        name="leaf_solve",
    )(*local(owners, leaf_matrix, coupling, leaf_residual_rows, inverse))
    if paced:
        messages = [message]
        exchange(messages, "leaf", leaves, 2)
        messages[-1] = after(messages[-1], data)
        exchange(data, "leaf", leaves, 2)
        exchange(messages, "leaf", leaves, 8)
        exchange(messages, "leaf", leaves, 4)
        messages[-1] = after(messages[-1], data)
        exchange(messages, "leaf", leaves, 1)
        exchange(data, "leaf", leaves, 1)
    elif doubling:
        messages = doubled(message, "leaf", leaves)
    else:
        messages = [lax.all_gather(message, "leaf", axis=0, tiled=True)]

    node_blocks = pl.pallas_call(
        functools.partial(assemble_kernel, sources, groups, held),
        out_shape=(
            pltpu.VMEM((groups, width, width), f32),
            pltpu.VMEM((groups, width, size), f32),
            pltpu.VMEM((groups, width), f32),
        ),
        in_specs=[vmem] * len(data),
        out_specs=(vmem, vmem, vmem),
        compiler_params=params,
        name="node_assemble",
    )(*local(*data))

    answers, part = pl.pallas_call(
        node_kernel,
        out_shape=(
            pltpu.VMEM((groups, size + 16, width), f32),
            pltpu.VMEM((size // 2 + 8, size), f32),
        ),
        in_specs=[vmem] * (3 + len(messages)),
        out_specs=(vmem, vmem),
        scratch_shapes=[
            pltpu.VMEM((groups, width, width), f32),
            pltpu.VMEM((groups, size + 16, width), f32),
            pltpu.VMEM((width, width + 2 * size), f32),
        ],
        compiler_params=params,
        name="node_solve",
    )(*local(*node_blocks, *messages))

    others = other_parts(part, "grp", sets)
    prepared = pl.pallas_call(
        prepare_kernel,
        out_shape=(
            pltpu.VMEM((size, size), f32),
            pltpu.VMEM((16, size), f32),
            pltpu.VMEM((groups, size, width), f32),
            pltpu.VMEM((groups, width), f32),
            pltpu.VMEM((slots, size, n), f32),
            pltpu.VMEM((slots, 8, n), f32),
        ),
        in_specs=[vmem] * 6,
        out_specs=[vmem] * 6,
        compiler_params=params,
        cost_estimate=pl.CostEstimate(flops=COST // 2, bytes_accessed=0, transcendentals=0),
        name="root_prepare",
    )(*local(owners, part, root_matrix, root_row, answers, solved))

    leaf_dir, node_dir, root_dir = pl.pallas_call(
        functools.partial(root_kernel, band),
        out_shape=(
            jax.ShapeDtypeStruct((slots, n), f32),
            jax.ShapeDtypeStruct((groups, band), f32),
            jax.ShapeDtypeStruct((1, size), f32),
        ),
        in_specs=[vmem] * (6 + len(others)),
        out_specs=(vmem, vmem, vmem),
        scratch_shapes=[
            pltpu.VMEM((size, size), f32),
            pltpu.VMEM((16, size), f32),
            pltpu.VMEM((size, 2 * size), f32),
        ],
        compiler_params=params,
        name="root_solve",
    )(*local(*prepared, *others))
    return leaf_dir, node_dir, root_dir[0]


def solution(mesh):
    return jax.shard_map(
        functools.partial(body, mesh.shape["leaf"], mesh.shape["grp"]),
        mesh=mesh,
        in_specs=(
            P(("leaf", "grp")),
            P(("leaf", "grp"), None, None),
            P(("leaf", "grp"), None, None),
            P(("leaf", "grp"), None),
            P("grp", "leaf", None),
            P("grp", "leaf", None),
            P("grp", "leaf"),
            P(),
            P(),
        ),
        out_specs=(P(("leaf", "grp"), None), P("grp", "leaf"), P()),
        check_vma=False,
    )
```

time: 47.2 us -> 41.4 us (0.88)
  local copies, waits for them, and re-layouts: 2.54 us -> 0 us
  starting transfers between devices: 14 us -> 11.5 us
  other arithmetic: 0.92 us -> 0.13 us
  waiting for transfers between devices: 15.1 us -> 15.7 us
    pallas_call x1, Pallas kernels: 4.82 us -> 1.97 us  [body(): pl.pallas_call(leaf_kernel, out_shape=(pltpu.VMEM((slots, width + 16, n),...]
    ppermute x9, starting transfers between devices: 14 us -> 11.5 us  [moved(): lax.ppermute(values, axis, [(i, i ^ distance) for i in range(extent)])]
    pallas_call x2 -> x6, Pallas kernels: 8.08 us -> 10.5 us  [the longest x1 3.59 us: body(): pl.pallas_call(node_kernel, out_shape=(pltpu.VMEM((groups, size + 16, wid...]
    unnamed x12 -> x0, local copies, waits for them, and re-layouts: 1.73 us -> none
    dynamic_update_slice x1 -> x0, local copies, waits for them, and re-layouts: 0.81 us -> none  [body(): lax.dynamic_update_slice(jnp.zeros((groups, width), f32), node_rhs, (jnp....]
    broadcast_in_dim x1 -> x0, other arithmetic: 0.81 us -> none  [body(): data = doubled(own[None], 'leaf', leaves)]
    ppermute x9, waiting for transfers between devices: 15.1 us -> 15.7 us  [moved(): lax.ppermute(values, axis, [(i, i ^ distance) for i in range(extent)])]
  transfers between devices with their start and end apart: 9 -> 9, of which waited for: 7 -> 7; matrix products, arithmetic and copies ran while one was open for 0% -> 0% of each run, Pallas kernels for 10% -> 14%
where the time goes in v2:
time: 41.4 us; the launch traced here: 41.2 us
  waiting for transfers between devices  15.7 us (38%)
  Pallas kernels  12.5 us (30%)
  starting transfers between devices  11.5 us (28%)
  between operations  1.35 us (3%)
    ppermute x9, waiting for transfers between devices, moved(): lax.ppermute(values, axis, [(i, i ^ distance) for i in range(extent)])  15.7 us
    ppermute x9, starting transfers between devices, moved(): lax.ppermute(values, axis, [(i, i ^ distance) for i in range(extent)])  11.5 us
    pallas_call x1, Pallas kernels, body(): pl.pallas_call(node_kernel, out_shape=(pltpu.VMEM((groups, size + 16, wid...  3.59 us
    pallas_call x1, Pallas kernels, body(): pl.pallas_call(invert_kernel, out_shape=[pltpu.VMEM(a.shape, f32) for a i...  3.21 us
    pallas_call x1, Pallas kernels, body(): pl.pallas_call(functools.partial(root_kernel, band), out_shape=(jax.Shape...  2.46 us
    pallas_call x1, Pallas kernels, body(): pl.pallas_call(leaf_kernel, out_shape=(pltpu.VMEM((slots, width + 16, n),...  1.97 us
  transfers between devices with their start and end apart: 9, of which 7 were waited for; matrix products, arithmetic and copies ran while one was open for 0% of the time, Pallas kernels for 14%

profile of v2, /device:TPU:0, one launch (start us, length us, event | category | flops | bytes accessed | tf_op | source)
XLA Modules:
  0.0 41.2 jit_solution(9893029307285457628)
XLA Ops:
  1.3 0.8 %stage.1 = (f32[1,8,128]{2,1,0:T(8,128)S(1)}, f32[1,136,128]{2,1,0:T(8,128)S(1)}) custom-call(s32[1]{0:T(128)S(6)} %copy.12.parent, f32[8,8,128]{2,1,0:T(8,128)} %matrix.1, f32[8,8,128]{2,1,0:T(8,128)} %link.1, f32[8,8]{1,0:T(8,128)} %rhs.1), custom_call_target="tpu_custom_call" | custom-call | tf_op jit(solution)/shard_map/stage/pallas_call | solution.py:429
  2.1 3.1 %collective-permute-start = (f32[1,136,128]{2,1,0:T(8,128)S(1)}, f32[1,136,128]{2,1,0:T(8,128)S(1)}, u32[]{:S(2)}, u32[]{:S(2)}) collective-permute-start(f32[1,136,128]{2,1,0:T(8,128)S(1)} %get-tuple-element.34.refs_0_), channel_id=1, source_target_pairs={{0,8},{2,10},{4,12},{6,14},{8,0},{10,2},{12,4},{14,6},{16,24},{18,... | collective-permute-start | bytes 208904 | tf_op jit(solution)/shard_map/ppermute | solution.py:357
  5.2 3.2 %leaf_invert.1 = (f32[1,384,384]{2,1,0:T(8,128)S(1)}, f32[1,384,128]{2,1,0:T(8,128)S(1)}, f32[1,384]{1,0:T(1,128)S(1)}, f32[128,128]{1,0:T(8,128)S(1)}, f32[1,12...) custom-call(f32[1,384,384]{2,1,0:T(8,128)} %refs_0_.1, f32[1,384,128]{2,1,0:T(8,128)} %refs_1_.1, f32[1,384]{1,0:T(1,128)} %refs_2_.1, ...), custom_call_target="tpu_custom_call" | custom-call | flops 3000000000 | tf_op jit(solution)/shard_map/leaf_invert/pallas_call | solution.py:463
  8.4 0.0 collective-permute-done.refs_1_
  8.4 2.7 %collective-permute-start.2 = (f32[2,136,128]{2,1,0:T(8,128)S(1)}, f32[2,136,128]{2,1,0:T(8,128)S(1)}, u32[]{:S(2)}, u32[]{:S(2)}) collective-permute-start(f32[2,136,128]{2,1,0:T(8,128)S(1)} %pad_maximum_fusion.4), channel_id=1, source_target_pairs={{0,16},{2,18},{4,20},{6,22},{8,24},{10,26},{12,28},{14,30},{16,0},... | collective-permute-start | bytes 417800 | tf_op jit(solution)/shard_map/ppermute | solution.py:357
  11.1 2.0 %leaf_solve.1 = (f32[1,144,384]{2,1,0:T(8,128)S(1)}, f32[1,72,128]{2,1,0:T(8,128)S(1)}) custom-call(f32[1,8,128]{2,1,0:T(8,128)S(1)} %get-tuple-element.33.owners, f32[1,384,384]{2,1,0:T(8,128)S(1)} %get-tuple-element.37.matrix, f32[1,384,128]{2,1,0:T(8,128)S(1)} %get-tuple-element.38.coupling, f32[1,384]{1,0:T(1,128)S(1)} %get-tuple-element.39.residual, ...), custom_call_target="tpu_custom_call" | custom-call | flops 3000000000 | tf_op jit(solution)/shard_map/leaf_solve/pallas_call | solution.py:476
  13.1 1.6 %collective-permute-start.1 = (f32[1,72,128]{2,1,0:T(8,128)S(1)}, f32[1,72,128]{2,1,0:T(8,128)S(1)}, u32[]{:S(2)}, u32[]{:S(2)}) collective-permute-start(f32[1,72,128]{2,1,0:T(8,128)S(1)} %get-tuple-element.41.refs_0_), channel_id=1, source_target_pairs={{0,4},{2,6},{4,0},{6,2},{8,12},{10,14},{12,8},{14,10},{16,20},{18,... | collective-permute-start | bytes 110600 | tf_op jit(solution)/shard_map/ppermute | solution.py:357
  14.7 2.4 %collective-permute-done.1.refs_1_ = f32[1,72,128]{2,1,0:T(8,128)S(1)} collective-permute-done((f32[1,72,128]{2,1,0:T(8,128)S(1)}, f32[1,72,128]{2,1,0:T(8,128)S(1)}, u32[]{:S(2)}, u32[]{:S(2)}) %collective-permute-start.1) | collective-permute-done | bytes 36896 | tf_op jit(solution)/shard_map/ppermute | solution.py:357
  17.1 0.3 collective-permute-done.2.refs_2_
  17.4 0.1 collective-permute-start.3
  17.5 1.6 %collective-permute-start.5 = (f32[4,136,128]{2,1,0:T(8,128)S(1)}, f32[4,136,128]{2,1,0:T(8,128)S(1)}, u32[]{:S(2)}, u32[]{:S(2)}) collective-permute-start(f32[4,136,128]{2,1,0:T(8,128)S(1)} %pad_maximum_fusion.2), channel_id=1, source_target_pairs={{0,4},{2,6},{4,0},{6,2},{8,12},{10,14},{12,8},{14,10},{16,20},{18,... | collective-permute-start | bytes 835592 | tf_op jit(solution)/shard_map/ppermute | solution.py:357
  19.1 4.3 %collective-permute-done.3.refs_2_ = f32[2,72,128]{2,1,0:T(8,128)S(1)} collective-permute-done((f32[2,72,128]{2,1,0:T(8,128)S(1)}, f32[2,72,128]{2,1,0:T(8,128)S(1)}, u32[]{:S(2)}, u32[]{:S(2)}) %collective-permute-start.3) | collective-permute-done | bytes 73760 | tf_op jit(solution)/shard_map/ppermute | solution.py:357
  23.4 0.2 collective-permute-start.4
  23.7 5.0 %collective-permute-done.4.refs_3_ = f32[4,72,128]{2,1,0:T(8,128)S(1)} collective-permute-done((f32[4,72,128]{2,1,0:T(8,128)S(1)}, f32[4,72,128]{2,1,0:T(8,128)S(1)}, u32[]{:S(2)}, u32[]{:S(2)}) %collective-permute-start.4) | collective-permute-done | bytes 147488 | tf_op jit(solution)/shard_map/ppermute | solution.py:357
  28.6 0.0 collective-permute-done.5.refs_3_
  28.7 0.1 collective-permute-start.6
  28.8 0.6 %collective-permute-start.7 = (f32[8,72,128]{2,1,0:T(8,128)S(1)}, f32[8,72,128]{2,1,0:T(8,128)S(1)}, u32[]{:S(2)}, u32[]{:S(2)}) collective-permute-start(f32[8,72,128]{2,1,0:T(8,128)S(1)} %pad_maximum_fusion.1), channel_id=1, source_target_pairs={{0,2},{2,0},{4,6},{6,4},{8,10},{10,8},{12,14},{14,12},{16,18},{18,... | collective-permute-start | bytes 884744 | tf_op jit(solution)/shard_map/ppermute | solution.py:357
  29.3 1.4 %collective-permute-done.6.refs_4_ = f32[8,136,128]{2,1,0:T(8,128)S(1)} collective-permute-done((f32[8,136,128]{2,1,0:T(8,128)S(1)}, f32[8,136,128]{2,1,0:T(8,128)S(1)}, u32[]{:S(2)}, u32[]{:S(2)}) %collective-permute-start.6) | collective-permute-done | bytes 557088 | tf_op jit(solution)/shard_map/ppermute | solution.py:357
  30.7 0.1 node_assemble.1
  30.9 0.3 collective-permute-done.7.refs_4_
  31.1 3.6 %node_solve.1 = (f32[8,144,128]{2,1,0:T(8,128)S(1)}, f32[72,128]{1,0:T(8,128)S(1)}) custom-call(f32[8,128,128]{2,1,0:T(8,128)S(1)} %get-tuple-element.45.regular, f32[8,128,128]{2,1,0:T(8,128)S(1)} %get-tuple-element.46.links, f32[8,128]{1,0:T(8,128)S(1)} %get-tuple-element.47.shift, f32[1,72,128]{2,1,0:T(8,128)S(1)} %get-tuple-element.41.refs_0_, ...), custom_call_target="tpu_custom_call" | custom-call | tf_op jit(solution)/shard_map/node_solve/pallas_call | solution.py:519
  34.7 1.6 %collective-permute-start.8 = (f32[72,128]{1,0:T(8,128)S(1)}, f32[72,128]{1,0:T(8,128)S(1)}, u32[]{:S(2)}, u32[]{:S(2)}) collective-permute-start(f32[72,128]{1,0:T(8,128)S(1)} %get-tuple-element.49.part), channel_id=1, source_target_pairs={{0,1},{1,0},{2,3},{3,2},{4,5},{5,4},{6,7},{7,6},{8,9},{9,8},{10,11... | collective-permute-start | bytes 110600 | tf_op jit(solution)/shard_map/ppermute | solution.py:357
  36.3 0.3 root_prepare.1
  36.6 2.1 %collective-permute-done.8.refs_0_ = f32[72,128]{1,0:T(8,128)S(1)} collective-permute-done((f32[72,128]{1,0:T(8,128)S(1)}, f32[72,128]{1,0:T(8,128)S(1)}, u32[]{:S(2)}, u32[]{:S(2)}) %collective-permute-start.8) | collective-permute-done | bytes 36896 | tf_op jit(solution)/shard_map/ppermute | solution.py:357
  38.7 2.5 %root_solve.1 = (f32[1,384]{1,0:T(1,128)}, f32[8,8]{1,0:T(8,128)}, f32[1,128]{1,0:T(1,128)}) custom-call(f32[128,128]{1,0:T(8,128)S(1)} %get-tuple-element.54.base, f32[16,128]{1,0:T(8,128)S(1)} %get-tuple-element.55.base_row, f32[8,128,128]{2,1,0:T(8,128)S(1)} %get-tuple-element.56.moves, f32[8,128]{1,0:T(8,128)S(1)} %get-tuple-element.57.fixed, ...), custom_call_target="tpu_custom_call" | custom-call | tf_op jit(solution)/shard_map/root_solve/pallas_call | solution.py:554
  (6 shorter events, 0.1 us)
Async XLA Ops:
  2.1 6.3 %collective-permute-start = (f32[1,136,128]{2,1,0:T(8,128)S(1)}, f32[1,136,128]{2,1,0:T(8,128)S(1)}, u32[]{:S(2)}, u32[]{:S(2)}) collective-permute-start(f32[1,136,128]{2,1,0:T(8,128)S(1)} %get-tuple-element.34.refs_0_), channel_id=1, source_target_pairs={{0,8},{2,10},{4,12},{6,14},{8,0},{10,2},{12,4},{14,6},{16,24},{18,... | collective-permute-start | bytes 208904 | tf_op jit(solution)/shard_map/ppermute | solution.py:357
  8.4 8.9 %collective-permute-start.2 = (f32[2,136,128]{2,1,0:T(8,128)S(1)}, f32[2,136,128]{2,1,0:T(8,128)S(1)}, u32[]{:S(2)}, u32[]{:S(2)}) collective-permute-start(f32[2,136,128]{2,1,0:T(8,128)S(1)} %pad_maximum_fusion.4), channel_id=1, source_target_pairs={{0,16},{2,18},{4,20},{6,22},{8,24},{10,26},{12,28},{14,30},{16,0},... | collective-permute-start | bytes 417800 | tf_op jit(solution)/shard_map/ppermute | solution.py:357
  13.1 4.0 %collective-permute-start.1 = (f32[1,72,128]{2,1,0:T(8,128)S(1)}, f32[1,72,128]{2,1,0:T(8,128)S(1)}, u32[]{:S(2)}, u32[]{:S(2)}) collective-permute-start(f32[1,72,128]{2,1,0:T(8,128)S(1)} %get-tuple-element.41.refs_0_), channel_id=1, source_target_pairs={{0,4},{2,6},{4,0},{6,2},{8,12},{10,14},{12,8},{14,10},{16,20},{18,... | collective-permute-start | bytes 110600 | tf_op jit(solution)/shard_map/ppermute | solution.py:357
  17.4 6.0 %collective-permute-start.3 = (f32[2,72,128]{2,1,0:T(8,128)S(1)}, f32[2,72,128]{2,1,0:T(8,128)S(1)}, u32[]{:S(2)}, u32[]{:S(2)}) collective-permute-start(f32[2,72,128]{2,1,0:T(8,128)S(1)} %pad_maximum_fusion.5), channel_id=1, source_target_pairs={{0,16},{2,18},{4,20},{6,22},{8,24},{10,26},{12,28},{14,30},{16,0},... | collective-permute-start | bytes 221192 | tf_op jit(solution)/shard_map/ppermute | solution.py:357
  17.5 11.1 %collective-permute-start.5 = (f32[4,136,128]{2,1,0:T(8,128)S(1)}, f32[4,136,128]{2,1,0:T(8,128)S(1)}, u32[]{:S(2)}, u32[]{:S(2)}) collective-permute-start(f32[4,136,128]{2,1,0:T(8,128)S(1)} %pad_maximum_fusion.2), channel_id=1, source_target_pairs={{0,4},{2,6},{4,0},{6,2},{8,12},{10,14},{12,8},{14,10},{16,20},{18,... | collective-permute-start | bytes 835592 | tf_op jit(solution)/shard_map/ppermute | solution.py:357
  23.4 5.2 %collective-permute-start.4 = (f32[4,72,128]{2,1,0:T(8,128)S(1)}, f32[4,72,128]{2,1,0:T(8,128)S(1)}, u32[]{:S(2)}, u32[]{:S(2)}) collective-permute-start(f32[4,72,128]{2,1,0:T(8,128)S(1)} %pad_maximum_fusion.3), channel_id=1, source_target_pairs={{0,8},{2,10},{4,12},{6,14},{8,0},{10,2},{12,4},{14,6},{16,24},{18,... | collective-permute-start | bytes 442376 | tf_op jit(solution)/shard_map/ppermute | solution.py:357
  28.7 2.0 %collective-permute-start.6 = (f32[8,136,128]{2,1,0:T(8,128)S(1)}, f32[8,136,128]{2,1,0:T(8,128)S(1)}, u32[]{:S(2)}, u32[]{:S(2)}) collective-permute-start(f32[8,136,128]{2,1,0:T(8,128)S(1)} %pad_maximum_fusion), channel_id=1, source_target_pairs={{0,2},{2,0},{4,6},{6,4},{8,10},{10,8},{12,14},{14,12},{16,18},{18,... | collective-permute-start | bytes 1671176 | tf_op jit(solution)/shard_map/ppermute | solution.py:357
  28.8 2.3 %collective-permute-start.7 = (f32[8,72,128]{2,1,0:T(8,128)S(1)}, f32[8,72,128]{2,1,0:T(8,128)S(1)}, u32[]{:S(2)}, u32[]{:S(2)}) collective-permute-start(f32[8,72,128]{2,1,0:T(8,128)S(1)} %pad_maximum_fusion.1), channel_id=1, source_target_pairs={{0,2},{2,0},{4,6},{6,4},{8,10},{10,8},{12,14},{14,12},{16,18},{18,... | collective-permute-start | bytes 884744 | tf_op jit(solution)/shard_map/ppermute | solution.py:357
  34.7 4.0 %collective-permute-start.8 = (f32[72,128]{1,0:T(8,128)S(1)}, f32[72,128]{1,0:T(8,128)S(1)}, u32[]{:S(2)}, u32[]{:S(2)}) collective-permute-start(f32[72,128]{1,0:T(8,128)S(1)} %get-tuple-element.49.part), channel_id=1, source_target_pairs={{0,1},{1,0},{2,3},{3,2},{4,5},{5,4},{6,7},{7,6},{8,9},{9,8},{10,11... | collective-permute-start | bytes 110600 | tf_op jit(solution)/shard_map/ppermute | solution.py:357

commit v3 on v2

--- a/solution.py
+++ b/solution.py
@@ -12,6 +12,7 @@
 FLOOR = 0.1
 STEPS = 5
 ROOT_STEPS = 6
+WARM_STEPS = 3
 COST = 3_000_000_000
 KERNEL_VMEM = 24 << 20
 ACCEPT = 4e-5
@@ -104,6 +105,26 @@
     return inverses
 
 
+def warm_inverse(matrix, near, low, steps):
+    one = identity(matrix.shape[0])
+    product = mul(near, matrix.astype(bf16))
+    bound = jnp.maximum(norm_bound(product), 2.0 * low)
+    alpha = 2.0 / (bound + low)
+    delta = (bound - low) / (bound + low)
+    square = delta * delta
+    scale = 2.0 / (2.0 - square)
+    error = (one - alpha * product).astype(bf16)
+    inverse = (alpha * near.astype(f32)).astype(bf16)
+    for step in range(steps):
+        inverse = (scale * (inverse.astype(f32) + mul(error, inverse))).astype(bf16)
+        if step + 1 < steps:
+            error = (scale * (mul(error, error) - (0.5 * square) * one)).astype(bf16)
+            delta = square / (2.0 - square)
+            square = delta * delta
+            scale = 2.0 / (2.0 - square)
+    return inverse
+
+
 def finish(matrices, inverses, rights):
     errors = [
         identity(m.shape[0]) - mul(beside(v, v, v), above(*split3(m)))
@@ -164,12 +185,14 @@
     return jnp.max(most, axis=1, keepdims=True)
 
 
-def stage_kernel(parent, matrix, link, rhs, owners, own, matrix_rows, link_rows, rhs_rows, sems):
+def stage_kernel(parent, matrix, link, rhs, *refs):
+    matrix_rows, link_rows, rhs_rows, sems = refs[-4:]
+    count = (len(refs) - 6) // 2
+    rest, owners, own, targets = refs[:count], refs[count], refs[count + 1], refs[count + 2 : -4]
+    pairs = ((matrix, matrix_rows), (link, link_rows), (rhs, rhs_rows), *zip(rest, targets))
     copies = [
         pltpu.make_async_copy(source, target, sems.at[i])
-        for i, (source, target) in enumerate(
-            ((matrix, matrix_rows), (link, link_rows), (rhs, rhs_rows))
-        )
+        for i, (source, target) in enumerate(pairs)
     ]
     for copy in copies:
         copy.start()
@@ -178,30 +201,20 @@
     groups, band, _ = matrix_rows.shape
     rows = groups * band
     own[0, 2 * rows :, :] = jnp.zeros((groups, own.shape[2]), f32)
-    for copy in copies:
+    for copy in copies[:3]:
         copy.wait()
     for q in range(groups):
         own[0, q * band : (q + 1) * band, :] = matrix_rows[q]
         own[0, rows + q * band : rows + (q + 1) * band, :] = link_rows[q]
     own[0, 2 * rows :, :band] = rhs_rows[...]
-
-
-def invert_kernel(*refs):
-    count = (len(refs) - 2) // 2
-    inputs, outputs, (inverse, sems) = refs[:count], refs[count:-2], refs[-2:]
-    copies = [
-        pltpu.make_async_copy(source, target, sems.at[i])
-        for i, (source, target) in enumerate(zip(inputs, outputs))
-    ]
-    for copy in copies:
-        copy.start()
-    copies[0].wait()
-    matrix = outputs[0]
+    for copy in copies[3:]:
+        copy.wait()
+
+
+def invert_kernel(matrix, inverse):
     for s in range(matrix.shape[0]):
         block = matrix[s]
         inverse[s] = coarse_inverse(norm_bound(block), [block], STEPS)[0]
-    for copy in copies[1:]:
-        copy.wait()
 
 
 def leaf_kernel(owners, matrix, coupling, residual, inverse, solved, message, work):
@@ -246,20 +259,34 @@
     shift[...] = total
 
 
-def node_kernel(regular, links, shift, *refs):
+def add_messages(sums, messages):
+    if not messages:
+        return sums
+    row = messages[0].shape[1] - 6
+    for piece in messages:
+        for j in range(piece.shape[0]):
+            message = piece[j]
+            owner = message[row : row + 1, :]
+            sums = [x + jnp.where(owner == q, message, 0.0) for q, x in enumerate(sums)]
+    return sums
+
+
+def sum_kernel(*refs):
+    sums = refs[-1]
+    groups = sums.shape[0]
+    zero = jnp.zeros(sums.shape[1:], f32)
+    for q, total in enumerate(add_messages([zero] * groups, refs[:-1])):
+        sums[q] = total
+
+
+def node_kernel(regular, links, shift, partial, *refs):
     messages = refs[:-5]
     answers, message, full, rights, work = refs[-5:]
     groups, n, width = links.shape
     half = n // 2
-    tops = [jnp.zeros((half, n), f32)] * groups
-    tails = [jnp.zeros((8, n), f32)] * groups
-    for piece in messages:
-        for j in range(piece.shape[0]):
-            owner = piece[j, half + 2 : half + 3, :]
-            for q in range(groups):
-                hit = owner == q
-                tops[q] = tops[q] + jnp.where(hit, piece[j, :half, :], 0.0)
-                tails[q] = tails[q] + jnp.where(hit, piece[j, half:, :], 0.0)
+    sums = add_messages([partial[q] for q in range(groups)], messages)
+    tops = [x[:half] for x in sums]
+    tails = [x[half:] for x in sums]
     for q in range(groups):
         full[q] = regular[q] + unpack_symmetric(tops[q], tails[q][1:2])
         rights[q, :width] = links[q].T
@@ -285,12 +312,15 @@
 
 
 def prepare_kernel(
-    owners, part, matrix, rhs, answers, solved, base, base_row, moves, fixed, leaf_moves, leaf_fixed
+    sets, owners, part, matrix, rhs, answers, solved, base, base_row, near, moves, fixed, leaf_moves, leaf_fixed
 ):
     size = matrix.shape[0]
     half = size // 2
     groups, _, n = answers.shape
-    base[...] = matrix[...] + unpack_symmetric(part[:half, :], part[half + 1 : half + 2, :])
+    mine = unpack_symmetric(part[:half, :], part[half + 1 : half + 2, :])
+    base[...] = matrix[...] + mine
+    guess = matrix[...] + sets * mine
+    near[...] = coarse_inverse(norm_bound(guess), [guess], ROOT_STEPS)[0]
     base_row[...] = jnp.broadcast_to(rhs[...] - part[half : half + 1, :], base_row.shape)
     for q in range(groups):
         fixed[q : q + 1, :] = answers[q, size : size + 1, :]
@@ -308,7 +338,7 @@
 
 
 def root_kernel(
-    band, base, base_row, moves, fixed, leaf_moves, leaf_fixed, *refs
+    sets, band, base, base_row, near, moves, fixed, leaf_moves, leaf_fixed, *refs
 ):
     others = refs[:-6]
     leaf_dir, node_dir, root_dir, full, found_root, work = refs[-6:]
@@ -321,8 +351,8 @@
         system = system + unpack_symmetric(other[:half, :], other[half + 1 : half + 2, :])
         right = right - other[half : half + 1, :]
     full[...] = system
-    inverses = coarse_inverse(norm_bound(system), [system], ROOT_STEPS)
-    found, bad = finish([system], inverses, [right])
+    inverse = warm_inverse(system, near[...], 1.0 / sets, WARM_STEPS)
+    found, bad = finish([system], [inverse], [right])
     found_root[...] = found[0]
 
     @pl.when(jnp.sum(bad[0]) > 0.0)
@@ -369,9 +399,8 @@
     return pieces
 
 
-def after(value, pieces):
-    value, pieces[-1] = lax.optimization_barrier((value, pieces[-1]))
-    return value
+def hold(pieces, value):
+    pieces[-1] = lax.optimization_barrier((value, pieces[-1]))[1]
 
 
 def source_offsets(steps):
@@ -426,23 +455,68 @@
     paced = doubling and band % 8 == 0
     hbm = pl.BlockSpec(memory_space=pltpu.HBM)
     nodes = [node_matrix, node_link, node_rhs]
-    owners, own = pl.pallas_call(
+    staged = [leaf_matrix, coupling, leaf_residual_rows, root_matrix, root_rhs[None, :]]
+    owners, own, *near, root_matrix, root_row = pl.pallas_call(
         stage_kernel,
         out_shape=(
             pltpu.VMEM((slots, 8, width), f32),
             pltpu.VMEM((1, 2 * groups * band + groups, width), f32),
+            *[pltpu.VMEM(a.shape, f32) for a in staged],
         ),
-        in_specs=[smem, hbm, hbm, hbm],
-        out_specs=(vmem, vmem),
-        scratch_shapes=[pltpu.VMEM(a.shape, f32) for a in nodes] + [pltpu.SemaphoreType.DMA((3,))],
+        in_specs=[smem] + [hbm] * (3 + len(staged)),
+        out_specs=[vmem] * (2 + len(staged)),
+        scratch_shapes=[pltpu.VMEM(a.shape, f32) for a in nodes]
+        + [pltpu.SemaphoreType.DMA((3 + len(staged),))],
         compiler_params=params,
         name="stage",
-    )(slot_parent, *remote(*nodes))
+    )(slot_parent, *remote(*nodes, *staged))
+    def invert():
+        return pl.pallas_call(
+            invert_kernel,
+            out_shape=pltpu.VMEM((slots, n, n), bf16),
+            in_specs=[vmem],
+            out_specs=vmem,
+            compiler_params=params,
+            cost_estimate=pl.CostEstimate(flops=COST, bytes_accessed=0, transcendentals=0),
+            name="leaf_invert",
+        )(*local(near[0]))
+
+    def solve(matrix, coupling, residual, inverse):
+        return pl.pallas_call(
+            leaf_kernel,
+            out_shape=(
+                pltpu.VMEM((slots, width + 16, n), f32),
+                pltpu.VMEM((slots, width // 2 + 8, width), f32),
+            ),
+            in_specs=[vmem] * 5,
+            out_specs=(vmem, vmem),
+            scratch_shapes=[
+                pltpu.VMEM((n, n + 2 * width), f32),
+            ],
+            compiler_params=params,
+            cost_estimate=pl.CostEstimate(flops=COST, bytes_accessed=0, transcendentals=0),
+            name="leaf_solve",
+        )(*local(owners, matrix, coupling, residual, inverse))
+
     if paced:
         data = [own]
-        order = [4, 8, 2, 1]
         held = band
+        order = [8, 4, 2, 1]
         sources = source_offsets(order)
+        exchange(data, "leaf", leaves, 8)
+        inverse = invert()
+        hold(data, inverse)
+        exchange(data, "leaf", leaves, 4)
+        solved, message = solve(*near, inverse)
+        messages = [message]
+        exchange(messages, "leaf", leaves, 2)
+        hold(data, messages[-1])
+        exchange(data, "leaf", leaves, 2)
+        exchange(messages, "leaf", leaves, 8)
+        exchange(messages, "leaf", leaves, 4)
+        hold(data, messages[-1])
+        exchange(messages, "leaf", leaves, 1)
+        exchange(data, "leaf", leaves, 1)
     else:
         rank = lax.axis_index("leaf")
         placed = lax.dynamic_update_slice(
@@ -457,51 +531,12 @@
         held = width
         sources = (0,)
 
-    if paced:
-        exchange(data, "leaf", leaves, 4)
-    staged = [leaf_matrix, coupling, leaf_residual_rows, root_matrix, root_rhs[None, :]]
-    leaf_matrix, coupling, leaf_residual_rows, root_matrix, root_row, inverse = pl.pallas_call(
-        invert_kernel,
-        out_shape=[pltpu.VMEM(a.shape, f32) for a in staged] + [pltpu.VMEM((slots, n, n), bf16)],
-        in_specs=[hbm] * len(staged),
-        out_specs=[vmem] * (len(staged) + 1),
-        scratch_shapes=[pltpu.SemaphoreType.DMA((len(staged),))],
-        compiler_params=params,
-        cost_estimate=pl.CostEstimate(flops=COST, bytes_accessed=0, transcendentals=0),
-        name="leaf_invert",
-    )(*remote(*staged))
-    if paced:
-        inverse = after(inverse, data)
-        exchange(data, "leaf", leaves, 8)
-    solved, message = pl.pallas_call(
-        leaf_kernel,
-        out_shape=(
-            pltpu.VMEM((slots, width + 16, n), f32),
-            pltpu.VMEM((slots, width // 2 + 8, width), f32),
-        ),
-        in_specs=[vmem] * 5,
-        out_specs=(vmem, vmem),
-        scratch_shapes=[
-            pltpu.VMEM((n, n + 2 * width), f32),
-        ],
-        compiler_params=params,
-        cost_estimate=pl.CostEstimate(flops=COST, bytes_accessed=0, transcendentals=0),
-        name="leaf_solve",
-    )(*local(owners, leaf_matrix, coupling, leaf_residual_rows, inverse))
-    if paced:
-        messages = [message]
-        exchange(messages, "leaf", leaves, 2)
-        messages[-1] = after(messages[-1], data)
-        exchange(data, "leaf", leaves, 2)
-        exchange(messages, "leaf", leaves, 8)
-        exchange(messages, "leaf", leaves, 4)
-        messages[-1] = after(messages[-1], data)
-        exchange(messages, "leaf", leaves, 1)
-        exchange(data, "leaf", leaves, 1)
-    elif doubling:
-        messages = doubled(message, "leaf", leaves)
-    else:
-        messages = [lax.all_gather(message, "leaf", axis=0, tiled=True)]
+        inverse = invert()
+        solved, message = solve(*near, inverse)
+        if doubling:
+            messages = doubled(message, "leaf", leaves)
+        else:
+            messages = [lax.all_gather(message, "leaf", axis=0, tiled=True)]
 
     node_blocks = pl.pallas_call(
         functools.partial(assemble_kernel, sources, groups, held),
@@ -516,13 +551,25 @@
         name="node_assemble",
     )(*local(*data))
 
+    early = messages[:-1] or messages
+    partial = pl.pallas_call(
+        sum_kernel,
+        out_shape=pltpu.VMEM((groups, width // 2 + 8, width), f32),
+        in_specs=[vmem] * len(early),
+        out_specs=vmem,
+        compiler_params=params,
+        cost_estimate=pl.CostEstimate(flops=COST // 4, bytes_accessed=0, transcendentals=0),
+        name="node_sum",
+    )(*local(*early))
+    late = messages[len(early) :]
+
     answers, part = pl.pallas_call(
         node_kernel,
         out_shape=(
             pltpu.VMEM((groups, size + 16, width), f32),
             pltpu.VMEM((size // 2 + 8, size), f32),
         ),
-        in_specs=[vmem] * (3 + len(messages)),
+        in_specs=[vmem] * (4 + len(late)),
         out_specs=(vmem, vmem),
         scratch_shapes=[
             pltpu.VMEM((groups, width, width), f32),
@@ -531,34 +578,35 @@
         ],
         compiler_params=params,
         name="node_solve",
-    )(*local(*node_blocks, *messages))
+    )(*local(*node_blocks, partial, *late))
 
     others = other_parts(part, "grp", sets)
     prepared = pl.pallas_call(
-        prepare_kernel,
+        functools.partial(prepare_kernel, sets),
         out_shape=(
             pltpu.VMEM((size, size), f32),
             pltpu.VMEM((16, size), f32),
+            pltpu.VMEM((size, size), bf16),
             pltpu.VMEM((groups, size, width), f32),
             pltpu.VMEM((groups, width), f32),
             pltpu.VMEM((slots, size, n), f32),
             pltpu.VMEM((slots, 8, n), f32),
         ),
         in_specs=[vmem] * 6,
-        out_specs=[vmem] * 6,
+        out_specs=[vmem] * 7,
         compiler_params=params,
         cost_estimate=pl.CostEstimate(flops=COST // 2, bytes_accessed=0, transcendentals=0),
         name="root_prepare",
     )(*local(owners, part, root_matrix, root_row, answers, solved))
 
     leaf_dir, node_dir, root_dir = pl.pallas_call(
-        functools.partial(root_kernel, band),
+        functools.partial(root_kernel, sets, band),
         out_shape=(
             jax.ShapeDtypeStruct((slots, n), f32),
             jax.ShapeDtypeStruct((groups, band), f32),
             jax.ShapeDtypeStruct((1, size), f32),
         ),
-        in_specs=[vmem] * (6 + len(others)),
+        in_specs=[vmem] * (7 + len(others)),
         out_specs=(vmem, vmem, vmem),
         scratch_shapes=[
             pltpu.VMEM((size, size), f32),

time: 41.4 us -> 37.4 us (0.903)
  waiting for transfers between devices: 15.7 us -> 12.2 us
    ppermute x9, waiting for transfers between devices: 15.7 us -> 12.2 us  [moved(): lax.ppermute(values, axis, [(i, i ^ distance) for i in range(extent)])]
    pallas_call x1, Pallas kernels: 0.81 us -> 1.24 us  [body(): pl.pallas_call(stage_kernel, out_shape=(pltpu.VMEM((slots, 8, width), f32...]
    pallas_call x4 -> x5, Pallas kernels: 7.94 us -> 7.66 us  [the longest x1 2.23 us: body(): pl.pallas_call(functools.partial(root_kernel, sets, band), out_shape=(jax...]
  transfers between devices with their start and end apart: 9 -> 9, of which waited for: 7 -> 7; matrix products, arithmetic and copies ran while one was open for 0% -> 0% of each run, Pallas kernels for 14% -> 15%
where the time goes in v3:
time: 37.4 us; the launch traced here: 37.3 us
  Pallas kernels  12.4 us (33%)
  waiting for transfers between devices  12.2 us (33%)
  starting transfers between devices  11.2 us (30%)
  between operations  1.35 us (4%)
    ppermute x9, waiting for transfers between devices, moved(): lax.ppermute(values, axis, [(i, i ^ distance) for i in range(extent)])  12.2 us
    ppermute x9, starting transfers between devices, moved(): lax.ppermute(values, axis, [(i, i ^ distance) for i in range(extent)])  11.2 us
    pallas_call x1, Pallas kernels, body(): pl.pallas_call(node_kernel, out_shape=(pltpu.VMEM((groups, size + 16, wid...  3.29 us
    pallas_call x1, Pallas kernels, body(): pl.pallas_call(functools.partial(root_kernel, sets, band), out_shape=(jax...  2.23 us
    pallas_call x1, Pallas kernels, invert(): pl.pallas_call(invert_kernel, out_shape=pltpu.VMEM((slots, n, n), bf16),...  2.1 us
    pallas_call x1, Pallas kernels, solve(): pl.pallas_call(leaf_kernel, out_shape=(pltpu.VMEM((slots, width + 16, n),...  1.97 us
    pallas_call x1, Pallas kernels, body(): pl.pallas_call(stage_kernel, out_shape=(pltpu.VMEM((slots, 8, width), f32...  1.24 us
    pallas_call x1, Pallas kernels, body(): pl.pallas_call(functools.partial(prepare_kernel, sets), out_shape=(pltpu....  1.16 us
  transfers between devices with their start and end apart: 9, of which 7 were waited for; matrix products, arithmetic and copies ran while one was open for 0% of the time, Pallas kernels for 15%

profile of v3, /device:TPU:0, one launch (start us, length us, event | category | flops | bytes accessed | tf_op | source)
XLA Modules:
  0.0 37.3 jit_solution(239543524674042056)
XLA Ops:
  1.3 1.2 %stage.1 = (f32[1,8,128]{2,1,0:T(8,128)S(1)}, f32[1,136,128]{2,1,0:T(8,128)S(1)}, f32[1,384,384]{2,1,0:T(8,128)S(1)}, f32[1,384,128]{2,1,0:T(8,128)S(1)}, f32[1,...) custom-call(s32[1]{0:T(128)S(6)} %copy.12.parent, f32[8,8,128]{2,1,0:T(8,128)} %matrix.1, ...), custom_call_target="tpu_custom_call" | custom-call | tf_op jit(solution)/shard_map/stage/pallas_call | solution.py:459
  2.5 4.1 %collective-permute-start = (f32[1,136,128]{2,1,0:T(8,128)S(1)}, f32[1,136,128]{2,1,0:T(8,128)S(1)}, u32[]{:S(2)}, u32[]{:S(2)}) collective-permute-start(f32[1,136,128]{2,1,0:T(8,128)S(1)} %get-tuple-element.31.refs_0_), channel_id=1, source_target_pairs={{0,16},{2,18},{4,20},{6,22},{8,24},{10,26},{12,28},{14,30},{16,0},... | collective-permute-start | bytes 208904 | tf_op jit(solution)/shard_map/ppermute | solution.py:387
  6.6 2.1 %leaf_invert.1.inverse = bf16[1,384,384]{2,1,0:T(8,128)(2,1)S(1)} custom-call(f32[1,384,384]{2,1,0:T(8,128)S(1)} %get-tuple-element.32.matrix), custom_call_target="tpu_custom_call" | custom-call | flops 3000000000 | tf_op jit(solution)/shard_map/leaf_invert/pallas_call | solution.py:474
  8.7 2.0 %leaf_solve.1 = (f32[1,144,384]{2,1,0:T(8,128)S(1)}, f32[1,72,128]{2,1,0:T(8,128)S(1)}) custom-call(f32[1,8,128]{2,1,0:T(8,128)S(1)} %get-tuple-element.30.owners, f32[1,384,384]{2,1,0:T(8,128)S(1)} %get-tuple-element.32.matrix, f32[1,384,128]{2,1,0:T(8,128)S(1)} %get-tuple-element.34.coupling, f32[1,384]{1,0:T(1,128)S(1)} %get-tuple-element.35.residual, ...), custom_call_target="tpu_custom_call" | custom-call | flops 3000000000 | tf_op jit(solution)/shard_map/leaf_solve/pallas_call | solution.py:485
  10.7 1.6 %collective-permute-start.1 = (f32[1,72,128]{2,1,0:T(8,128)S(1)}, f32[1,72,128]{2,1,0:T(8,128)S(1)}, u32[]{:S(2)}, u32[]{:S(2)}) collective-permute-start(f32[1,72,128]{2,1,0:T(8,128)S(1)} %get-tuple-element.36.refs_0_), channel_id=1, source_target_pairs={{0,4},{2,6},{4,0},{6,2},{8,12},{10,14},{12,8},{14,10},{16,20},{18,... | collective-permute-start | bytes 110600 | tf_op jit(solution)/shard_map/ppermute | solution.py:387
  12.3 0.0 collective-permute-done.refs_1_
  12.3 1.6 %collective-permute-start.2 = (f32[2,136,128]{2,1,0:T(8,128)S(1)}, f32[2,136,128]{2,1,0:T(8,128)S(1)}, u32[]{:S(2)}, u32[]{:S(2)}) collective-permute-start(f32[2,136,128]{2,1,0:T(8,128)S(1)} %pad_maximum_fusion.4), channel_id=1, source_target_pairs={{0,8},{2,10},{4,12},{6,14},{8,0},{10,2},{12,4},{14,6},{16,24},{18,... | collective-permute-start | bytes 417800 | tf_op jit(solution)/shard_map/ppermute | solution.py:387
  14.0 0.8 %collective-permute-done.1.refs_1_ = f32[1,72,128]{2,1,0:T(8,128)S(1)} collective-permute-done((f32[1,72,128]{2,1,0:T(8,128)S(1)}, f32[1,72,128]{2,1,0:T(8,128)S(1)}, u32[]{:S(2)}, u32[]{:S(2)}) %collective-permute-start.1) | collective-permute-done | bytes 36896 | tf_op jit(solution)/shard_map/ppermute | solution.py:387
  14.7 0.0 collective-permute-start.3
  14.8 3.5 %collective-permute-done.2.refs_2_ = f32[2,136,128]{2,1,0:T(8,128)S(1)} collective-permute-done((f32[2,136,128]{2,1,0:T(8,128)S(1)}, f32[2,136,128]{2,1,0:T(8,128)S(1)}, u32[]{:S(2)}, u32[]{:S(2)}) %collective-permute-start.2) | collective-permute-done | bytes 139296 | tf_op jit(solution)/shard_map/ppermute | solution.py:387
  18.2 0.1 collective-permute-start.5
  18.3 1.7 %collective-permute-done.3.refs_2_ = f32[2,72,128]{2,1,0:T(8,128)S(1)} collective-permute-done((f32[2,72,128]{2,1,0:T(8,128)S(1)}, f32[2,72,128]{2,1,0:T(8,128)S(1)}, u32[]{:S(2)}, u32[]{:S(2)}) %collective-permute-start.3) | collective-permute-done | bytes 73760 | tf_op jit(solution)/shard_map/ppermute | solution.py:387
  20.0 1.6 %collective-permute-start.4 = (f32[4,72,128]{2,1,0:T(8,128)S(1)}, f32[4,72,128]{2,1,0:T(8,128)S(1)}, u32[]{:S(2)}, u32[]{:S(2)}) collective-permute-start(f32[4,72,128]{2,1,0:T(8,128)S(1)} %pad_maximum_fusion.3), channel_id=1, source_target_pairs={{0,8},{2,10},{4,12},{6,14},{8,0},{10,2},{12,4},{14,6},{16,24},{18,... | collective-permute-start | bytes 442376 | tf_op jit(solution)/shard_map/ppermute | solution.py:387
  21.7 3.6 %collective-permute-done.4.refs_3_ = f32[4,72,128]{2,1,0:T(8,128)S(1)} collective-permute-done((f32[4,72,128]{2,1,0:T(8,128)S(1)}, f32[4,72,128]{2,1,0:T(8,128)S(1)}, u32[]{:S(2)}, u32[]{:S(2)}) %collective-permute-start.4) | collective-permute-done | bytes 147488 | tf_op jit(solution)/shard_map/ppermute | solution.py:387
  25.2 0.0 collective-permute-done.5.refs_3_
  25.3 0.1 collective-permute-start.6
  25.4 0.6 %collective-permute-start.7 = (f32[8,72,128]{2,1,0:T(8,128)S(1)}, f32[8,72,128]{2,1,0:T(8,128)S(1)}, u32[]{:S(2)}, u32[]{:S(2)}) collective-permute-start(f32[8,72,128]{2,1,0:T(8,128)S(1)} %pad_maximum_fusion.1), channel_id=1, source_target_pairs={{0,2},{2,0},{4,6},{6,4},{8,10},{10,8},{12,14},{14,12},{16,18},{18,... | collective-permute-start | bytes 884744 | tf_op jit(solution)/shard_map/ppermute | solution.py:387
  25.9 0.2 node_sum.1.partial
  26.1 1.2 %collective-permute-done.6.refs_4_ = f32[8,136,128]{2,1,0:T(8,128)S(1)} collective-permute-done((f32[8,136,128]{2,1,0:T(8,128)S(1)}, f32[8,136,128]{2,1,0:T(8,128)S(1)}, u32[]{:S(2)}, u32[]{:S(2)}) %collective-permute-start.6) | collective-permute-done | bytes 557088 | tf_op jit(solution)/shard_map/ppermute | solution.py:387
  27.3 0.2 node_assemble.1
  27.5 0.2 collective-permute-done.7.refs_0_
  27.7 3.3 %node_solve.1 = (f32[8,144,128]{2,1,0:T(8,128)S(1)}, f32[72,128]{1,0:T(8,128)S(1)}) custom-call(f32[8,128,128]{2,1,0:T(8,128)S(1)} %get-tuple-element.39.regular, f32[8,128,128]{2,1,0:T(8,128)S(1)} %get-tuple-element.40.links, f32[8,128]{1,0:T(8,128)S(1)} %get-tuple-element.41.shift, f32[8,72,128]{2,1,0:T(8,128)S(1)} %node_sum.1.partial, ...), custom_call_target="tpu_custom_call" | custom-call | tf_op jit(solution)/shard_map/node_solve/pallas_call | solution.py:566
  31.0 1.6 %collective-permute-start.8 = (f32[72,128]{1,0:T(8,128)S(1)}, f32[72,128]{1,0:T(8,128)S(1)}, u32[]{:S(2)}, u32[]{:S(2)}) collective-permute-start(f32[72,128]{1,0:T(8,128)S(1)} %get-tuple-element.42.part), channel_id=1, source_target_pairs={{0,1},{1,0},{2,3},{3,2},{4,5},{5,4},{6,7},{7,6},{8,9},{9,8},{10,11... | collective-permute-start | bytes 110600 | tf_op jit(solution)/shard_map/ppermute | solution.py:387
  32.6 1.2 %root_prepare.1 = (f32[128,128]{1,0:T(8,128)S(1)}, f32[16,128]{1,0:T(8,128)S(1)}, bf16[128,128]{1,0:T(8,128)(2,1)S(1)}, f32[8,128,128]{2,1,0:T(8,128)S(1)}, f32[...) custom-call(f32[1,8,128]{2,1,0:T(8,128)S(1)} %get-tuple-element.30.owners, ...), custom_call_target="tpu_custom_call" | custom-call | flops 1500000000 | tf_op jit(solution)/shard_map/root_prepare/pallas_call | solution.py:584
  33.7 1.3 %collective-permute-done.8.refs_0_ = f32[72,128]{1,0:T(8,128)S(1)} collective-permute-done((f32[72,128]{1,0:T(8,128)S(1)}, f32[72,128]{1,0:T(8,128)S(1)}, u32[]{:S(2)}, u32[]{:S(2)}) %collective-permute-start.8) | collective-permute-done | bytes 36896 | tf_op jit(solution)/shard_map/ppermute | solution.py:387
  35.0 2.2 %root_solve.1 = (f32[1,384]{1,0:T(1,128)}, f32[8,8]{1,0:T(8,128)}, f32[1,128]{1,0:T(1,128)}) custom-call(f32[128,128]{1,0:T(8,128)S(1)} %get-tuple-element.47.base, f32[16,128]{1,0:T(8,128)S(1)} %get-tuple-element.48.base_row, bf16[128,128]{1,0:T(8,128)(2,1)S(1)} %get-tuple-element.49.near, f32[8,128,128]{2,1,0:T(8,128)S(1)} %get-tuple-element.50.moves, ...), custom_call_target="tpu_custom_call" | custom-call | tf_op jit(solution)/shard_map/root_solve/pallas_call | solution.py:602
  (6 shorter events, 0.1 us)
Async XLA Ops:
  2.5 9.8 %collective-permute-start = (f32[1,136,128]{2,1,0:T(8,128)S(1)}, f32[1,136,128]{2,1,0:T(8,128)S(1)}, u32[]{:S(2)}, u32[]{:S(2)}) collective-permute-start(f32[1,136,128]{2,1,0:T(8,128)S(1)} %get-tuple-element.31.refs_0_), channel_id=1, source_target_pairs={{0,16},{2,18},{4,20},{6,22},{8,24},{10,26},{12,28},{14,30},{16,0},... | collective-permute-start | bytes 208904 | tf_op jit(solution)/shard_map/ppermute | solution.py:387
  10.7 4.0 %collective-permute-start.1 = (f32[1,72,128]{2,1,0:T(8,128)S(1)}, f32[1,72,128]{2,1,0:T(8,128)S(1)}, u32[]{:S(2)}, u32[]{:S(2)}) collective-permute-start(f32[1,72,128]{2,1,0:T(8,128)S(1)} %get-tuple-element.36.refs_0_), channel_id=1, source_target_pairs={{0,4},{2,6},{4,0},{6,2},{8,12},{10,14},{12,8},{14,10},{16,20},{18,... | collective-permute-start | bytes 110600 | tf_op jit(solution)/shard_map/ppermute | solution.py:387
  12.3 5.9 %collective-permute-start.2 = (f32[2,136,128]{2,1,0:T(8,128)S(1)}, f32[2,136,128]{2,1,0:T(8,128)S(1)}, u32[]{:S(2)}, u32[]{:S(2)}) collective-permute-start(f32[2,136,128]{2,1,0:T(8,128)S(1)} %pad_maximum_fusion.4), channel_id=1, source_target_pairs={{0,8},{2,10},{4,12},{6,14},{8,0},{10,2},{12,4},{14,6},{16,24},{18,... | collective-permute-start | bytes 417800 | tf_op jit(solution)/shard_map/ppermute | solution.py:387
  14.7 5.3 %collective-permute-start.3 = (f32[2,72,128]{2,1,0:T(8,128)S(1)}, f32[2,72,128]{2,1,0:T(8,128)S(1)}, u32[]{:S(2)}, u32[]{:S(2)}) collective-permute-start(f32[2,72,128]{2,1,0:T(8,128)S(1)} %pad_maximum_fusion.5), channel_id=1, source_target_pairs={{0,16},{2,18},{4,20},{6,22},{8,24},{10,26},{12,28},{14,30},{16,0},... | collective-permute-start | bytes 221192 | tf_op jit(solution)/shard_map/ppermute | solution.py:387
  18.2 7.0 %collective-permute-start.5 = (f32[4,136,128]{2,1,0:T(8,128)S(1)}, f32[4,136,128]{2,1,0:T(8,128)S(1)}, u32[]{:S(2)}, u32[]{:S(2)}) collective-permute-start(f32[4,136,128]{2,1,0:T(8,128)S(1)} %pad_maximum_fusion.2), channel_id=1, source_target_pairs={{0,4},{2,6},{4,0},{6,2},{8,12},{10,14},{12,8},{14,10},{16,20},{18,... | collective-permute-start | bytes 835592 | tf_op jit(solution)/shard_map/ppermute | solution.py:387
  20.0 5.2 %collective-permute-start.4 = (f32[4,72,128]{2,1,0:T(8,128)S(1)}, f32[4,72,128]{2,1,0:T(8,128)S(1)}, u32[]{:S(2)}, u32[]{:S(2)}) collective-permute-start(f32[4,72,128]{2,1,0:T(8,128)S(1)} %pad_maximum_fusion.3), channel_id=1, source_target_pairs={{0,8},{2,10},{4,12},{6,14},{8,0},{10,2},{12,4},{14,6},{16,24},{18,... | collective-permute-start | bytes 442376 | tf_op jit(solution)/shard_map/ppermute | solution.py:387
  25.3 2.0 %collective-permute-start.6 = (f32[8,136,128]{2,1,0:T(8,128)S(1)}, f32[8,136,128]{2,1,0:T(8,128)S(1)}, u32[]{:S(2)}, u32[]{:S(2)}) collective-permute-start(f32[8,136,128]{2,1,0:T(8,128)S(1)} %pad_maximum_fusion), channel_id=1, source_target_pairs={{0,2},{2,0},{4,6},{6,4},{8,10},{10,8},{12,14},{14,12},{16,18},{18,... | collective-permute-start | bytes 1671176 | tf_op jit(solution)/shard_map/ppermute | solution.py:387
  25.4 2.3 %collective-permute-start.7 = (f32[8,72,128]{2,1,0:T(8,128)S(1)}, f32[8,72,128]{2,1,0:T(8,128)S(1)}, u32[]{:S(2)}, u32[]{:S(2)}) collective-permute-start(f32[8,72,128]{2,1,0:T(8,128)S(1)} %pad_maximum_fusion.1), channel_id=1, source_target_pairs={{0,2},{2,0},{4,6},{6,4},{8,10},{10,8},{12,14},{14,12},{16,18},{18,... | collective-permute-start | bytes 884744 | tf_op jit(solution)/shard_map/ppermute | solution.py:387
  31.0 4.0 %collective-permute-start.8 = (f32[72,128]{1,0:T(8,128)S(1)}, f32[72,128]{1,0:T(8,128)S(1)}, u32[]{:S(2)}, u32[]{:S(2)}) collective-permute-start(f32[72,128]{1,0:T(8,128)S(1)} %get-tuple-element.42.part), channel_id=1, source_target_pairs={{0,1},{1,0},{2,3},{3,2},{4,5},{5,4},{6,7},{7,6},{8,9},{9,8},{10,11... | collective-permute-start | bytes 110600 | tf_op jit(solution)/shard_map/ppermute | solution.py:387

commit v4 on v3

--- a/solution.py
+++ b/solution.py
@@ -127,7 +127,7 @@
 
 def finish(matrices, inverses, rights):
     errors = [
-        identity(m.shape[0]) - mul(beside(v, v, v), above(*split3(m)))
+        identity(m.shape[0]) - mul(beside(v, v), above(*split(m)))
         for m, v in zip(matrices, inverses)
     ]
     pieces = [split(e) for e in errors]
@@ -138,7 +138,7 @@
         first.append(right + mul(beside(rh, rh, rl), above(eh, el, eh)))
     second = [mul(z.astype(bf16), s) for z, s in zip(first, squares)]
     found = [
-        mul(beside(*split3(z + d)), above(v, v, v)) for z, d, v in zip(first, second, inverses)
+        mul(beside(*split(z + d)), above(v, v)) for z, d, v in zip(first, second, inverses)
     ]
     return found, [misfits(d, z) for z, d in zip(first, second)]
 
@@ -238,25 +238,68 @@
         message[s, width // 2 :, :] = tail
 
 
-def assemble_kernel(sources, groups, band, *refs):
-    data = refs[:-3]
-    full, links, shift = refs[-3:]
+def pack_kernel(leaves, own, other, packed):
+    n = own.shape[2]
+    half = n // 2
+    band = half // (leaves // 2)
+    groups = own.shape[1] // (2 * band + 1)
     rows = groups * band
-    here = lax.axis_index("leaf") if len(sources) > 1 else 0
+    here = lax.axis_index("leaf")
+    is_top = here < leaves // 2
+    place = lax.rem(here, leaves // 2) * band
+    top = jnp.where(is_top, own[0], other[0])
+    low = jnp.where(is_top, other[0], own[0])
+    row, col = grid_of(band, n)
+    row = row + place
+    diagonals = []
+    for q in range(groups):
+        at = slice(q * band, (q + 1) * band)
+        packed[0, at, :] = jnp.where(col < row, pltpu.roll(low[at], half, 1), top[at])
+        diagonals.append(
+            jnp.sum(jnp.where(col == row + half, low[at], 0.0), axis=0, keepdims=True)
+        )
+    packed[0, rows : 2 * rows, :] = top[rows : 2 * rows]
+    packed[0, 2 * rows : 3 * rows, :] = low[rows : 2 * rows]
+    _, col = grid_of(groups, n)
+    diagonal = pltpu.roll(above(*diagonals), lax.rem(half + 2 * band - place, n), 1)
+    last = jnp.where(col < 2 * band, pltpu.roll(low[2 * rows :], band, 1), diagonal)
+    last = jnp.where(col < band, top[2 * rows :], last)
+    packed[0, 3 * rows :, :] = jnp.where(col < 3 * band, last, 0.0)
+
+
+def assemble_kernel(leaves, sources, groups, band, *refs):
+    data = refs[:-2]
+    regular, links = refs[-2:]
+    n = regular.shape[2]
+    half = n // 2
+    rows = groups * band
+    here = lax.axis_index("leaf")
+    row, col = grid_of(groups, n)
     at = 0
-    total = None
+    shift = jnp.zeros((groups, n), f32)
+    diagonal = jnp.zeros((groups, n), f32)
     for piece in data:
         for j in range(piece.shape[0]):
-            place = pl.multiple_of((here ^ sources[at]) * band, band) if len(sources) > 1 else 0
+            place = lax.rem(here ^ sources[at], leaves // 2) * band
+            place = pl.multiple_of(place, band)
             at += 1
             for q in range(groups):
-                full[q, pl.ds(place, band), :] = piece[j, q * band : (q + 1) * band, :]
-                links[q, pl.ds(place, band), :] = piece[j, rows + q * band : rows + (q + 1) * band, :]
-            last = piece[j, 2 * rows :, :]
-            if len(sources) > 1:
-                last = pltpu.roll(last, place, 1)
-            total = last if total is None else total + last
-    shift[...] = total
+                regular[q, pl.ds(place, band), :] = piece[j, q * band : (q + 1) * band, :]
+                start = rows + q * band
+                links[q, pl.ds(place, band), :] = piece[j, start : start + band, :]
+                start = start + rows
+                links[q, pl.ds(half + place, band), :] = piece[j, start : start + band, :]
+            last = piece[j, 3 * rows :, :]
+            first = jnp.where(col < band, last, 0.0)
+            second = jnp.where((col >= band) & (col < 2 * band), last, 0.0)
+            third = jnp.where(col >= 2 * band, last, 0.0)
+            shift = shift + pltpu.roll(first, place, 1)
+            shift = shift + pltpu.roll(second, lax.rem(half + place - band + n, n), 1)
+            diagonal = diagonal + pltpu.roll(third, lax.rem(half + place - 2 * band + n, n), 1)
+    row8, _ = grid_of(8, n)
+    for q in range(groups):
+        tail = jnp.where(row8 == 0, -shift[q : q + 1], 0.0)
+        regular[q, half:, :] = jnp.where(row8 == 1, diagonal[q : q + 1], tail)
 
 
 def add_messages(sums, messages):
@@ -279,18 +322,18 @@
         sums[q] = total
 
 
-def node_kernel(regular, links, shift, partial, *refs):
+def node_kernel(regular, links, partial, *refs):
     messages = refs[:-5]
     answers, message, full, rights, work = refs[-5:]
     groups, n, width = links.shape
     half = n // 2
-    sums = add_messages([partial[q] for q in range(groups)], messages)
+    sums = add_messages([regular[q] + partial[q] for q in range(groups)], messages)
     tops = [x[:half] for x in sums]
     tails = [x[half:] for x in sums]
     for q in range(groups):
-        full[q] = regular[q] + unpack_symmetric(tops[q], tails[q][1:2])
+        full[q] = unpack_symmetric(tops[q], tails[q][1:2])
         rights[q, :width] = links[q].T
-        rights[q, width:] = jnp.broadcast_to(tails[q][:1] - shift[q : q + 1], (16, n))
+        rights[q, width:] = jnp.broadcast_to(tails[q][:1], (16, n))
     blocks = [full[q] for q in range(groups)]
     inverses = coarse_inverse(norm_bound(*blocks), blocks, STEPS)
     found, bad = finish(blocks, inverses, [rights[q] for q in range(groups)])
@@ -452,7 +495,7 @@
     smem = pl.BlockSpec(memory_space=pltpu.SMEM)
     params = pltpu.CompilerParams(vmem_limit_bytes=KERNEL_VMEM)
 
-    paced = doubling and band % 8 == 0
+    paced = doubling and band % 8 == 0 and 4 <= leaves and 3 * band <= width
     hbm = pl.BlockSpec(memory_space=pltpu.HBM)
     nodes = [node_matrix, node_link, node_rhs]
     staged = [leaf_matrix, coupling, leaf_residual_rows, root_matrix, root_rhs[None, :]]
@@ -499,24 +542,44 @@
         )(*local(owners, matrix, coupling, residual, inverse))
 
     if paced:
-        data = [own]
-        held = band
-        order = [8, 4, 2, 1]
-        sources = source_offsets(order)
-        exchange(data, "leaf", leaves, 8)
+        steps = gather_steps(leaves)
+        pair = [own]
+        exchange(pair, "leaf", leaves, steps[0])
         inverse = invert()
+        data = [
+            pl.pallas_call(
+                functools.partial(pack_kernel, leaves),
+                out_shape=pltpu.VMEM((1, 3 * groups * band + groups, width), f32),
+                in_specs=[vmem, vmem],
+                out_specs=vmem,
+                compiler_params=params,
+                name="node_pack",
+            )(*local(*pair))
+        ]
         hold(data, inverse)
-        exchange(data, "leaf", leaves, 4)
+        exchange(data, "leaf", leaves, steps[1])
         solved, message = solve(*near, inverse)
         messages = [message]
-        exchange(messages, "leaf", leaves, 2)
+        exchange(messages, "leaf", leaves, steps[-2])
+        for step in steps[2:-1]:
+            hold(data, messages[-1])
+            exchange(data, "leaf", leaves, step)
+        for step in steps[:-2]:
+            exchange(messages, "leaf", leaves, step)
         hold(data, messages[-1])
-        exchange(data, "leaf", leaves, 2)
-        exchange(messages, "leaf", leaves, 8)
-        exchange(messages, "leaf", leaves, 4)
-        hold(data, messages[-1])
-        exchange(messages, "leaf", leaves, 1)
-        exchange(data, "leaf", leaves, 1)
+        for pieces in (messages, data):
+            exchange(pieces, "leaf", leaves, steps[-1])
+        node_blocks = pl.pallas_call(
+            functools.partial(assemble_kernel, leaves, source_offsets(steps[1:]), groups, band),
+            out_shape=(
+                pltpu.VMEM((groups, width // 2 + 8, width), f32),
+                pltpu.VMEM((groups, width, size), f32),
+            ),
+            in_specs=[vmem] * len(data),
+            out_specs=(vmem, vmem),
+            compiler_params=params,
+            name="node_assemble",
+        )(*local(*data))
     else:
         rank = lax.axis_index("leaf")
         placed = lax.dynamic_update_slice(
@@ -525,31 +588,22 @@
         every = lax.all_gather(
             jnp.concatenate([node_matrix, node_link], axis=0), "leaf", axis=1, tiled=True
         )
-        data = [
-            jnp.concatenate([every.reshape(-1, width), lax.psum(placed, "leaf")], axis=0)[None]
-        ]
-        held = width
-        sources = (0,)
-
+        blocks = every[:groups]
+        half = width // 2
+        row, col = grid_of(half, width)
+        tops = jnp.where(col < row, jnp.roll(blocks[:, half:], half, 2), blocks[:, :half])
+        shift = lax.psum(placed, "leaf")
+        diagonal = jnp.where(
+            jnp.arange(width) < half, 0.0, jnp.diagonal(blocks, axis1=1, axis2=2)
+        )
+        tails = jnp.stack([-shift, diagonal] + [jnp.zeros_like(shift)] * 6, axis=1)
+        node_blocks = [jnp.concatenate([tops, tails], axis=1), every[groups:]]
         inverse = invert()
         solved, message = solve(*near, inverse)
         if doubling:
             messages = doubled(message, "leaf", leaves)
         else:
             messages = [lax.all_gather(message, "leaf", axis=0, tiled=True)]
-
-    node_blocks = pl.pallas_call(
-        functools.partial(assemble_kernel, sources, groups, held),
-        out_shape=(
-            pltpu.VMEM((groups, width, width), f32),
-            pltpu.VMEM((groups, width, size), f32),
-            pltpu.VMEM((groups, width), f32),
-        ),
-        in_specs=[vmem] * len(data),
-        out_specs=(vmem, vmem, vmem),
-        compiler_params=params,
-        name="node_assemble",
-    )(*local(*data))
 
     early = messages[:-1] or messages
     partial = pl.pallas_call(
@@ -569,7 +623,7 @@
             pltpu.VMEM((groups, size + 16, width), f32),
             pltpu.VMEM((size // 2 + 8, size), f32),
         ),
-        in_specs=[vmem] * (4 + len(late)),
+        in_specs=[vmem] * (3 + len(late)),
         out_specs=(vmem, vmem),
         scratch_shapes=[
             pltpu.VMEM((groups, width, width), f32),

time: 37.4 us -> 36.8 us (0.984)
  waiting for transfers between devices: 12.2 us -> 11.4 us
  starting transfers between devices: 11.2 us -> 11.8 us
  Pallas kernels: 12.4 us -> 12 us
    ppermute x9, waiting for transfers between devices: 12.2 us -> 11.4 us  [moved(): lax.ppermute(values, axis, [(i, i ^ distance) for i in range(extent)])]
    ppermute x9, starting transfers between devices: 11.2 us -> 11.8 us  [moved(): lax.ppermute(values, axis, [(i, i ^ distance) for i in range(extent)])]
where the time goes in v4:
time: 36.8 us; the launch traced here: 36.6 us
  Pallas kernels  12 us (33%)
  starting transfers between devices  11.8 us (32%)
  waiting for transfers between devices  11.4 us (31%)
  between operations  1.36 us (4%)
    ppermute x9, starting transfers between devices, moved(): lax.ppermute(values, axis, [(i, i ^ distance) for i in range(extent)])  11.8 us
    ppermute x9, waiting for transfers between devices, moved(): lax.ppermute(values, axis, [(i, i ^ distance) for i in range(extent)])  11.4 us
    pallas_call x1, Pallas kernels, body(): pl.pallas_call(node_kernel, out_shape=(pltpu.VMEM((groups, size + 16, wid...  3.18 us
    pallas_call x1, Pallas kernels, body(): pl.pallas_call(functools.partial(root_kernel, sets, band), out_shape=(jax...  2.22 us
    pallas_call x1, Pallas kernels, invert(): pl.pallas_call(invert_kernel, out_shape=pltpu.VMEM((slots, n, n), bf16),...  2.1 us
    pallas_call x1, Pallas kernels, solve(): pl.pallas_call(leaf_kernel, out_shape=(pltpu.VMEM((slots, width + 16, n),...  1.67 us
    pallas_call x1, Pallas kernels, body(): pl.pallas_call(stage_kernel, out_shape=(pltpu.VMEM((slots, 8, width), f32...  1.24 us
    pallas_call x1, Pallas kernels, body(): pl.pallas_call(functools.partial(prepare_kernel, sets), out_shape=(pltpu....  1.16 us
  transfers between devices with their start and end apart: 9, of which 7 were waited for; matrix products, arithmetic and copies ran while one was open for 0% of the time, Pallas kernels for 15%

profile of v4, /device:TPU:0, one launch (start us, length us, event | category | flops | bytes accessed | tf_op | source)
XLA Modules:
  0.0 36.6 jit_solution(12498100756408387419)
XLA Ops:
  1.3 1.2 %stage.1 = (f32[1,8,128]{2,1,0:T(8,128)S(1)}, f32[1,136,128]{2,1,0:T(8,128)S(1)}, f32[1,384,384]{2,1,0:T(8,128)S(1)}, f32[1,384,128]{2,1,0:T(8,128)S(1)}, f32[1,...) custom-call(s32[1]{0:T(128)S(6)} %copy.12.parent, f32[8,8,128]{2,1,0:T(8,128)} %matrix.1, ...), custom_call_target="tpu_custom_call" | custom-call | tf_op jit(solution)/shard_map/stage/pallas_call | solution.py:502
  2.5 4.1 %collective-permute-start = (f32[1,136,128]{2,1,0:T(8,128)S(1)}, f32[1,136,128]{2,1,0:T(8,128)S(1)}, u32[]{:S(2)}, u32[]{:S(2)}) collective-permute-start(f32[1,136,128]{2,1,0:T(8,128)S(1)} %get-tuple-element.31.own), channel_id=1, source_target_pairs={{0,16},{2,18},{4,20},{6,22},{8,24},{10,26},{12,28},{14,30},{16,0},... | collective-permute-start | bytes 208904 | tf_op jit(solution)/shard_map/ppermute | solution.py:430
  6.6 2.1 %leaf_invert.1.inverse = bf16[1,384,384]{2,1,0:T(8,128)(2,1)S(1)} custom-call(f32[1,384,384]{2,1,0:T(8,128)S(1)} %get-tuple-element.30.matrix), custom_call_target="tpu_custom_call" | custom-call | flops 3000000000 | tf_op jit(solution)/shard_map/leaf_invert/pallas_call | solution.py:517
  8.7 1.7 %leaf_solve.1 = (f32[1,144,384]{2,1,0:T(8,128)S(1)}, f32[1,72,128]{2,1,0:T(8,128)S(1)}) custom-call(f32[1,8,128]{2,1,0:T(8,128)S(1)} %get-tuple-element.29.owners, f32[1,384,384]{2,1,0:T(8,128)S(1)} %get-tuple-element.30.matrix, f32[1,384,128]{2,1,0:T(8,128)S(1)} %get-tuple-element.33.coupling, f32[1,384]{1,0:T(1,128)S(1)} %get-tuple-element.34.residual, ...), custom_call_target="tpu_custom_call" | custom-call | flops 3000000000 | tf_op jit(solution)/shard_map/leaf_solve/pallas_call | solution.py:528
  10.4 1.6 %collective-permute-start.1 = (f32[1,72,128]{2,1,0:T(8,128)S(1)}, f32[1,72,128]{2,1,0:T(8,128)S(1)}, u32[]{:S(2)}, u32[]{:S(2)}) collective-permute-start(f32[1,72,128]{2,1,0:T(8,128)S(1)} %get-tuple-element.35.refs_0_), channel_id=1, source_target_pairs={{0,4},{2,6},{4,0},{6,2},{8,12},{10,14},{12,8},{14,10},{16,20},{18,... | collective-permute-start | bytes 110600 | tf_op jit(solution)/shard_map/ppermute | solution.py:430
  12.0 0.0 collective-permute-done.other
  12.0 0.1 node_pack.1.refs_0_
  12.1 1.6 %collective-permute-start.2 = (f32[1,200,128]{2,1,0:T(8,128)S(1)}, f32[1,200,128]{2,1,0:T(8,128)S(1)}, u32[]{:S(2)}, u32[]{:S(2)}) collective-permute-start(f32[1,200,128]{2,1,0:T(8,128)S(1)} %node_pack.1.refs_0_), channel_id=1, source_target_pairs={{0,8},{2,10},{4,12},{6,14},{8,0},{10,2},{12,4},{14,6},{16,24},{18,... | collective-permute-start | bytes 307208 | tf_op jit(solution)/shard_map/ppermute | solution.py:430
  13.7 0.7 %collective-permute-done.1.refs_1_ = f32[1,72,128]{2,1,0:T(8,128)S(1)} collective-permute-done((f32[1,72,128]{2,1,0:T(8,128)S(1)}, f32[1,72,128]{2,1,0:T(8,128)S(1)}, u32[]{:S(2)}, u32[]{:S(2)}) %collective-permute-start.1) | collective-permute-done | bytes 36896 | tf_op jit(solution)/shard_map/ppermute | solution.py:430
  14.4 0.2 collective-permute-start.3
  14.6 3.0 %collective-permute-done.2.refs_1_ = f32[1,200,128]{2,1,0:T(8,128)S(1)} collective-permute-done((f32[1,200,128]{2,1,0:T(8,128)S(1)}, f32[1,200,128]{2,1,0:T(8,128)S(1)}, u32[]{:S(2)}, u32[]{:S(2)}) %collective-permute-start.2) | collective-permute-done | bytes 102432 | tf_op jit(solution)/shard_map/ppermute | solution.py:430
  17.6 0.1 collective-permute-start.5
  17.7 2.0 %collective-permute-done.3.refs_2_ = f32[2,72,128]{2,1,0:T(8,128)S(1)} collective-permute-done((f32[2,72,128]{2,1,0:T(8,128)S(1)}, f32[2,72,128]{2,1,0:T(8,128)S(1)}, u32[]{:S(2)}, u32[]{:S(2)}) %collective-permute-start.3) | collective-permute-done | bytes 73760 | tf_op jit(solution)/shard_map/ppermute | solution.py:430
  19.7 2.0 %collective-permute-start.4 = (f32[4,72,128]{2,1,0:T(8,128)S(1)}, f32[4,72,128]{2,1,0:T(8,128)S(1)}, u32[]{:S(2)}, u32[]{:S(2)}) collective-permute-start(f32[4,72,128]{2,1,0:T(8,128)S(1)} %pad_maximum_fusion.3), channel_id=1, source_target_pairs={{0,8},{2,10},{4,12},{6,14},{8,0},{10,2},{12,4},{14,6},{16,24},{18,... | collective-permute-start | bytes 442376 | tf_op jit(solution)/shard_map/ppermute | solution.py:430
  21.7 3.2 %collective-permute-done.4.refs_3_ = f32[4,72,128]{2,1,0:T(8,128)S(1)} collective-permute-done((f32[4,72,128]{2,1,0:T(8,128)S(1)}, f32[4,72,128]{2,1,0:T(8,128)S(1)}, u32[]{:S(2)}, u32[]{:S(2)}) %collective-permute-start.4) | collective-permute-done | bytes 147488 | tf_op jit(solution)/shard_map/ppermute | solution.py:430
  24.9 0.0 collective-permute-done.5.refs_2_
  25.0 0.1 collective-permute-start.6
  25.1 0.6 %collective-permute-start.7 = (f32[8,72,128]{2,1,0:T(8,128)S(1)}, f32[8,72,128]{2,1,0:T(8,128)S(1)}, u32[]{:S(2)}, u32[]{:S(2)}) collective-permute-start(f32[8,72,128]{2,1,0:T(8,128)S(1)} %pad_maximum_fusion.1), channel_id=1, source_target_pairs={{0,2},{2,0},{4,6},{6,4},{8,10},{10,8},{12,14},{14,12},{16,18},{18,... | collective-permute-start | bytes 884744 | tf_op jit(solution)/shard_map/ppermute | solution.py:430
  25.6 0.2 node_sum.1.partial
  25.8 1.0 %collective-permute-done.6.refs_3_ = f32[4,200,128]{2,1,0:T(8,128)S(1)} collective-permute-done((f32[4,200,128]{2,1,0:T(8,128)S(1)}, f32[4,200,128]{2,1,0:T(8,128)S(1)}, u32[]{:S(2)}, u32[]{:S(2)}) %collective-permute-start.6) | collective-permute-done | bytes 409632 | tf_op jit(solution)/shard_map/ppermute | solution.py:430
  26.8 0.2 node_assemble.1
  27.0 0.2 collective-permute-done.7.refs_0_
  27.2 3.2 %node_solve.1 = (f32[8,144,128]{2,1,0:T(8,128)S(1)}, f32[72,128]{1,0:T(8,128)S(1)}) custom-call(f32[8,72,128]{2,1,0:T(8,128)S(1)} %get-tuple-element.38.regular, f32[8,128,128]{2,1,0:T(8,128)S(1)} %get-tuple-element.39.links, f32[8,72,128]{2,1,0:T(8,128)S(1)} %node_sum.1.partial, f32[8,72,128]{2,1,0:T(8,128)S(1)} %collective-permute-done.7.refs_0_), custom_call_target="tpu_custom_call" | custom-call | tf_op jit(solution)/shard_map/node_solve/pallas_call | solution.py:620
  30.4 1.6 %collective-permute-start.8 = (f32[72,128]{1,0:T(8,128)S(1)}, f32[72,128]{1,0:T(8,128)S(1)}, u32[]{:S(2)}, u32[]{:S(2)}) collective-permute-start(f32[72,128]{1,0:T(8,128)S(1)} %get-tuple-element.40.part), channel_id=1, source_target_pairs={{0,1},{1,0},{2,3},{3,2},{4,5},{5,4},{6,7},{7,6},{8,9},{9,8},{10,11... | collective-permute-start | bytes 110600 | tf_op jit(solution)/shard_map/ppermute | solution.py:430
  31.9 1.2 %root_prepare.1 = (f32[128,128]{1,0:T(8,128)S(1)}, f32[16,128]{1,0:T(8,128)S(1)}, bf16[128,128]{1,0:T(8,128)(2,1)S(1)}, f32[8,128,128]{2,1,0:T(8,128)S(1)}, f32[...) custom-call(f32[1,8,128]{2,1,0:T(8,128)S(1)} %get-tuple-element.29.owners, ...), custom_call_target="tpu_custom_call" | custom-call | flops 1500000000 | tf_op jit(solution)/shard_map/root_prepare/pallas_call | solution.py:638
  33.1 1.3 %collective-permute-done.8.refs_0_ = f32[72,128]{1,0:T(8,128)S(1)} collective-permute-done((f32[72,128]{1,0:T(8,128)S(1)}, f32[72,128]{1,0:T(8,128)S(1)}, u32[]{:S(2)}, u32[]{:S(2)}) %collective-permute-start.8) | collective-permute-done | bytes 36896 | tf_op jit(solution)/shard_map/ppermute | solution.py:430
  34.4 2.2 %root_solve.1 = (f32[1,384]{1,0:T(1,128)}, f32[8,8]{1,0:T(8,128)}, f32[1,128]{1,0:T(1,128)}) custom-call(f32[128,128]{1,0:T(8,128)S(1)} %get-tuple-element.45.base, f32[16,128]{1,0:T(8,128)S(1)} %get-tuple-element.46.base_row, bf16[128,128]{1,0:T(8,128)(2,1)S(1)} %get-tuple-element.47.near, f32[8,128,128]{2,1,0:T(8,128)S(1)} %get-tuple-element.48.moves, ...), custom_call_target="tpu_custom_call" | custom-call | tf_op jit(solution)/shard_map/root_solve/pallas_call | solution.py:656
  (5 shorter events, 0.1 us)
Async XLA Ops:
  2.5 9.5 %collective-permute-start = (f32[1,136,128]{2,1,0:T(8,128)S(1)}, f32[1,136,128]{2,1,0:T(8,128)S(1)}, u32[]{:S(2)}, u32[]{:S(2)}) collective-permute-start(f32[1,136,128]{2,1,0:T(8,128)S(1)} %get-tuple-element.31.own), channel_id=1, source_target_pairs={{0,16},{2,18},{4,20},{6,22},{8,24},{10,26},{12,28},{14,30},{16,0},... | collective-permute-start | bytes 208904 | tf_op jit(solution)/shard_map/ppermute | solution.py:430
  10.4 4.0 %collective-permute-start.1 = (f32[1,72,128]{2,1,0:T(8,128)S(1)}, f32[1,72,128]{2,1,0:T(8,128)S(1)}, u32[]{:S(2)}, u32[]{:S(2)}) collective-permute-start(f32[1,72,128]{2,1,0:T(8,128)S(1)} %get-tuple-element.35.refs_0_), channel_id=1, source_target_pairs={{0,4},{2,6},{4,0},{6,2},{8,12},{10,14},{12,8},{14,10},{16,20},{18,... | collective-permute-start | bytes 110600 | tf_op jit(solution)/shard_map/ppermute | solution.py:430
  12.1 5.5 %collective-permute-start.2 = (f32[1,200,128]{2,1,0:T(8,128)S(1)}, f32[1,200,128]{2,1,0:T(8,128)S(1)}, u32[]{:S(2)}, u32[]{:S(2)}) collective-permute-start(f32[1,200,128]{2,1,0:T(8,128)S(1)} %node_pack.1.refs_0_), channel_id=1, source_target_pairs={{0,8},{2,10},{4,12},{6,14},{8,0},{10,2},{12,4},{14,6},{16,24},{18,... | collective-permute-start | bytes 307208 | tf_op jit(solution)/shard_map/ppermute | solution.py:430
  14.4 5.3 %collective-permute-start.3 = (f32[2,72,128]{2,1,0:T(8,128)S(1)}, f32[2,72,128]{2,1,0:T(8,128)S(1)}, u32[]{:S(2)}, u32[]{:S(2)}) collective-permute-start(f32[2,72,128]{2,1,0:T(8,128)S(1)} %pad_maximum_fusion.4), channel_id=1, source_target_pairs={{0,16},{2,18},{4,20},{6,22},{8,24},{10,26},{12,28},{14,30},{16,0},... | collective-permute-start | bytes 221192 | tf_op jit(solution)/shard_map/ppermute | solution.py:430
  17.6 7.3 %collective-permute-start.5 = (f32[2,200,128]{2,1,0:T(8,128)S(1)}, f32[2,200,128]{2,1,0:T(8,128)S(1)}, u32[]{:S(2)}, u32[]{:S(2)}) collective-permute-start(f32[2,200,128]{2,1,0:T(8,128)S(1)} %pad_maximum_fusion.2), channel_id=1, source_target_pairs={{0,4},{2,6},{4,0},{6,2},{8,12},{10,14},{12,8},{14,10},{16,20},{18,... | collective-permute-start | bytes 614408 | tf_op jit(solution)/shard_map/ppermute | solution.py:430
  19.7 5.2 %collective-permute-start.4 = (f32[4,72,128]{2,1,0:T(8,128)S(1)}, f32[4,72,128]{2,1,0:T(8,128)S(1)}, u32[]{:S(2)}, u32[]{:S(2)}) collective-permute-start(f32[4,72,128]{2,1,0:T(8,128)S(1)} %pad_maximum_fusion.3), channel_id=1, source_target_pairs={{0,8},{2,10},{4,12},{6,14},{8,0},{10,2},{12,4},{14,6},{16,24},{18,... | collective-permute-start | bytes 442376 | tf_op jit(solution)/shard_map/ppermute | solution.py:430
  25.0 1.8 %collective-permute-start.6 = (f32[4,200,128]{2,1,0:T(8,128)S(1)}, f32[4,200,128]{2,1,0:T(8,128)S(1)}, u32[]{:S(2)}, u32[]{:S(2)}) collective-permute-start(f32[4,200,128]{2,1,0:T(8,128)S(1)} %pad_maximum_fusion), channel_id=1, source_target_pairs={{0,2},{2,0},{4,6},{6,4},{8,10},{10,8},{12,14},{14,12},{16,18},{18,... | collective-permute-start | bytes 1228808 | tf_op jit(solution)/shard_map/ppermute | solution.py:430
  25.1 2.1 %collective-permute-start.7 = (f32[8,72,128]{2,1,0:T(8,128)S(1)}, f32[8,72,128]{2,1,0:T(8,128)S(1)}, u32[]{:S(2)}, u32[]{:S(2)}) collective-permute-start(f32[8,72,128]{2,1,0:T(8,128)S(1)} %pad_maximum_fusion.1), channel_id=1, source_target_pairs={{0,2},{2,0},{4,6},{6,4},{8,10},{10,8},{12,14},{14,12},{16,18},{18,... | collective-permute-start | bytes 884744 | tf_op jit(solution)/shard_map/ppermute | solution.py:430
  30.4 4.0 %collective-permute-start.8 = (f32[72,128]{1,0:T(8,128)S(1)}, f32[72,128]{1,0:T(8,128)S(1)}, u32[]{:S(2)}, u32[]{:S(2)}) collective-permute-start(f32[72,128]{1,0:T(8,128)S(1)} %get-tuple-element.40.part), channel_id=1, source_target_pairs={{0,1},{1,0},{2,3},{3,2},{4,5},{5,4},{6,7},{7,6},{8,9},{9,8},{10,11... | collective-permute-start | bytes 110600 | tf_op jit(solution)/shard_map/ppermute | solution.py:430

commit v5 on v4

--- a/solution.py
+++ b/solution.py
@@ -221,21 +221,24 @@
     n = matrix.shape[1]
     width = coupling.shape[2]
     for s in range(matrix.shape[0]):
-        right = above(coupling[s].T, jnp.broadcast_to(residual[s : s + 1, :], (16, n)))
-        found, bad = finish([matrix[s]], [inverse[s]], [right])
-        solved[s] = found[0]
+
+        def right_side():
+            return above(coupling[s].T, jnp.broadcast_to(residual[s : s + 1, :], (16, n)))
+
+        def give(found):
+            solved[s] = found
+            product = mul3(found, coupling[s])
+            top, tail = pack_symmetric(product[:width], product[width : width + 1])
+            row8, _ = grid_of(8, width)
+            message[s, : width // 2, :] = top
+            message[s, width // 2 :, :] = jnp.where(row8 == 2, owners[s], tail)
+
+        found, bad = finish([matrix[s]], [inverse[s]], [right_side()])
+        give(found[0])
 
         @pl.when(jnp.sum(bad[0]) > 0.0)
         def _():
-            right = above(coupling[s].T, jnp.broadcast_to(residual[s : s + 1, :], (16, n)))
-            solved[s] = solve_again(work, matrix[s], right)
-
-        product = mul3(solved[s], coupling[s])
-        top, tail = pack_symmetric(product[:width], product[width : width + 1])
-        row8, _ = grid_of(8, width)
-        tail = jnp.where(row8 == 2, owners[s], tail)
-        message[s, : width // 2, :] = top
-        message[s, width // 2 :, :] = tail
+            give(solve_again(work, matrix[s], right_side()))
 
 
 def pack_kernel(leaves, own, other, packed):
@@ -337,21 +340,24 @@
     blocks = [full[q] for q in range(groups)]
     inverses = coarse_inverse(norm_bound(*blocks), blocks, STEPS)
     found, bad = finish(blocks, inverses, [rights[q] for q in range(groups)])
-    for q in range(groups):
-        answers[q] = found[q]
+
+    def give(found):
+        total = None
+        for q in range(groups):
+            answers[q] = found(q)
+            part = mul3(found(q), links[q])
+            total = part if q == 0 else total + part
+        top, tail = pack_symmetric(total[:width], total[width : width + 1])
+        message[: width // 2, :] = top
+        message[width // 2 :, :] = tail
+
+    give(lambda q: found[q])
 
     @pl.when(jnp.sum(sum(bad)) > 0.0)
     def _():
         for q in range(groups):
             answers[q] = solve_again(work, full[q], rights[q])
-
-    total = None
-    for q in range(groups):
-        part = mul3(answers[q], links[q])
-        total = part if q == 0 else total + part
-    top, tail = pack_symmetric(total[:width], total[width : width + 1])
-    message[: width // 2, :] = top
-    message[width // 2 :, :] = tail
+        give(lambda q: answers[q])
 
 
 def prepare_kernel(
@@ -383,8 +389,8 @@
 def root_kernel(
     sets, band, base, base_row, near, moves, fixed, leaf_moves, leaf_fixed, *refs
 ):
-    others = refs[:-6]
-    leaf_dir, node_dir, root_dir, full, found_root, work = refs[-6:]
+    others = refs[:-5]
+    leaf_dir, node_dir, root_dir, full, work = refs[-5:]
     size = base.shape[0]
     half = size // 2
     groups, _, n = moves.shape
@@ -396,26 +402,27 @@
     full[...] = system
     inverse = warm_inverse(system, near[...], 1.0 / sets, WARM_STEPS)
     found, bad = finish([system], [inverse], [right])
-    found_root[...] = found[0]
+
+    def give(answer):
+        root_dir[...] = answer
+        column = jnp.broadcast_to(answer, (size, size)).T
+        each = [jnp.sum(column * moves[q], axis=0, keepdims=True) for q in range(groups)]
+        every = above(*each) + fixed[...]
+        if band == n:
+            node_dir[...] = every
+        else:
+            me = lax.axis_index("leaf")
+            node_dir[...] = pltpu.roll(every, lax.rem(n - me * band, n), 1)[:, :band]
+        wide = leaf_moves.shape[2] // size
+        for s in range(leaf_moves.shape[0]):
+            terms = beside(*[column] * wide) * leaf_moves[s]
+            leaf_dir[s : s + 1, :] = jnp.sum(terms, axis=0, keepdims=True) + leaf_fixed[s, :1, :]
+
+    give(found[0][:1])
 
     @pl.when(jnp.sum(bad[0]) > 0.0)
     def _():
-        found_root[...] = solve_again(work, full[...], right)
-
-    answer = found_root[:1, :]
-    root_dir[...] = answer
-    column = jnp.broadcast_to(answer, (size, size)).T
-    each = [jnp.sum(column * moves[q], axis=0, keepdims=True) for q in range(groups)]
-    every = above(*each) + fixed[...]
-    if band == n:
-        node_dir[...] = every
-    else:
-        me = lax.axis_index("leaf")
-        node_dir[...] = pltpu.roll(every, lax.rem(n - me * band, n), 1)[:, :band]
-    wide = leaf_moves.shape[2] // size
-    for s in range(leaf_moves.shape[0]):
-        terms = beside(*[column] * wide) * leaf_moves[s]
-        leaf_dir[s : s + 1, :] = jnp.sum(terms, axis=0, keepdims=True) + leaf_fixed[s, :1, :]
+        give(solve_again(work, full[...], right)[:1])
 
 
 def gather_steps(extent):
@@ -664,7 +671,6 @@
         out_specs=(vmem, vmem, vmem),
         scratch_shapes=[
             pltpu.VMEM((size, size), f32),
-            pltpu.VMEM((16, size), f32),
             pltpu.VMEM((size, 2 * size), f32),
         ],
         compiler_params=params,

time: 36.8 us -> 36.5 us (level)
  no operation moved by 1% of the time
where the time goes in v5:
time: 36.5 us; the launch traced here: 36.4 us
  Pallas kernels  11.8 us (32%)
  starting transfers between devices  11.6 us (32%)
  waiting for transfers between devices  11.5 us (32%)
  between operations  1.36 us (4%)
    ppermute x9, starting transfers between devices, moved(): lax.ppermute(values, axis, [(i, i ^ distance) for i in range(extent)])  11.6 us
    ppermute x9, waiting for transfers between devices, moved(): lax.ppermute(values, axis, [(i, i ^ distance) for i in range(extent)])  11.5 us
    pallas_call x1, Pallas kernels, body(): pl.pallas_call(node_kernel, out_shape=(pltpu.VMEM((groups, size + 16, wid...  3.04 us
    pallas_call x1, Pallas kernels, body(): pl.pallas_call(functools.partial(root_kernel, sets, band), out_shape=(jax...  2.15 us
    pallas_call x1, Pallas kernels, invert(): pl.pallas_call(invert_kernel, out_shape=pltpu.VMEM((slots, n, n), bf16),...  2.1 us
    pallas_call x1, Pallas kernels, solve(): pl.pallas_call(leaf_kernel, out_shape=(pltpu.VMEM((slots, width + 16, n),...  1.62 us
    pallas_call x1, Pallas kernels, body(): pl.pallas_call(stage_kernel, out_shape=(pltpu.VMEM((slots, 8, width), f32...  1.24 us
    pallas_call x1, Pallas kernels, body(): pl.pallas_call(functools.partial(prepare_kernel, sets), out_shape=(pltpu....  1.16 us
  transfers between devices with their start and end apart: 9, of which 7 were waited for; matrix products, arithmetic and copies ran while one was open for 0% of the time, Pallas kernels for 15%

profile of v5, /device:TPU:0, one launch (start us, length us, event | category | flops | bytes accessed | tf_op | source)
XLA Modules:
  0.0 36.4 jit_solution(17930258370051897215)
XLA Ops:
  1.3 1.2 %stage.1 = (f32[1,8,128]{2,1,0:T(8,128)S(1)}, f32[1,136,128]{2,1,0:T(8,128)S(1)}, f32[1,384,384]{2,1,0:T(8,128)S(1)}, f32[1,384,128]{2,1,0:T(8,128)S(1)}, f32[1,...) custom-call(s32[1]{0:T(128)S(6)} %copy.12.parent, f32[8,8,128]{2,1,0:T(8,128)} %matrix.1, ...), custom_call_target="tpu_custom_call" | custom-call | tf_op jit(solution)/shard_map/stage/pallas_call | solution.py:509
  2.5 4.1 %collective-permute-start = (f32[1,136,128]{2,1,0:T(8,128)S(1)}, f32[1,136,128]{2,1,0:T(8,128)S(1)}, u32[]{:S(2)}, u32[]{:S(2)}) collective-permute-start(f32[1,136,128]{2,1,0:T(8,128)S(1)} %get-tuple-element.31.own), channel_id=1, source_target_pairs={{0,16},{2,18},{4,20},{6,22},{8,24},{10,26},{12,28},{14,30},{16,0},... | collective-permute-start | bytes 208904 | tf_op jit(solution)/shard_map/ppermute | solution.py:437
  6.6 2.1 %leaf_invert.1.inverse = bf16[1,384,384]{2,1,0:T(8,128)(2,1)S(1)} custom-call(f32[1,384,384]{2,1,0:T(8,128)S(1)} %get-tuple-element.30.matrix), custom_call_target="tpu_custom_call" | custom-call | flops 3000000000 | tf_op jit(solution)/shard_map/leaf_invert/pallas_call | solution.py:524
  8.7 1.6 %leaf_solve.1 = (f32[1,144,384]{2,1,0:T(8,128)S(1)}, f32[1,72,128]{2,1,0:T(8,128)S(1)}) custom-call(f32[1,8,128]{2,1,0:T(8,128)S(1)} %get-tuple-element.29.owners, f32[1,384,384]{2,1,0:T(8,128)S(1)} %get-tuple-element.30.matrix, f32[1,384,128]{2,1,0:T(8,128)S(1)} %get-tuple-element.33.coupling, f32[1,384]{1,0:T(1,128)S(1)} %get-tuple-element.34.residual, ...), custom_call_target="tpu_custom_call" | custom-call | flops 3000000000 | tf_op jit(solution)/shard_map/leaf_solve/pallas_call | solution.py:535
  10.4 1.6 %collective-permute-start.1 = (f32[1,72,128]{2,1,0:T(8,128)S(1)}, f32[1,72,128]{2,1,0:T(8,128)S(1)}, u32[]{:S(2)}, u32[]{:S(2)}) collective-permute-start(f32[1,72,128]{2,1,0:T(8,128)S(1)} %get-tuple-element.35.refs_0_), channel_id=1, source_target_pairs={{0,4},{2,6},{4,0},{6,2},{8,12},{10,14},{12,8},{14,10},{16,20},{18,... | collective-permute-start | bytes 110600 | tf_op jit(solution)/shard_map/ppermute | solution.py:437
  11.9 0.0 collective-permute-done.other
  11.9 0.1 node_pack.1.refs_0_
  12.0 1.6 %collective-permute-start.2 = (f32[1,200,128]{2,1,0:T(8,128)S(1)}, f32[1,200,128]{2,1,0:T(8,128)S(1)}, u32[]{:S(2)}, u32[]{:S(2)}) collective-permute-start(f32[1,200,128]{2,1,0:T(8,128)S(1)} %node_pack.1.refs_0_), channel_id=1, source_target_pairs={{0,8},{2,10},{4,12},{6,14},{8,0},{10,2},{12,4},{14,6},{16,24},{18,... | collective-permute-start | bytes 307208 | tf_op jit(solution)/shard_map/ppermute | solution.py:437
  13.7 0.7 %collective-permute-done.1.refs_1_ = f32[1,72,128]{2,1,0:T(8,128)S(1)} collective-permute-done((f32[1,72,128]{2,1,0:T(8,128)S(1)}, f32[1,72,128]{2,1,0:T(8,128)S(1)}, u32[]{:S(2)}, u32[]{:S(2)}) %collective-permute-start.1) | collective-permute-done | bytes 36896 | tf_op jit(solution)/shard_map/ppermute | solution.py:437
  14.4 0.3 collective-permute-start.3
  14.6 2.9 %collective-permute-done.2.refs_1_ = f32[1,200,128]{2,1,0:T(8,128)S(1)} collective-permute-done((f32[1,200,128]{2,1,0:T(8,128)S(1)}, f32[1,200,128]{2,1,0:T(8,128)S(1)}, u32[]{:S(2)}, u32[]{:S(2)}) %collective-permute-start.2) | collective-permute-done | bytes 102432 | tf_op jit(solution)/shard_map/ppermute | solution.py:437
  17.6 0.1 collective-permute-start.5
  17.7 2.0 %collective-permute-done.3.refs_2_ = f32[2,72,128]{2,1,0:T(8,128)S(1)} collective-permute-done((f32[2,72,128]{2,1,0:T(8,128)S(1)}, f32[2,72,128]{2,1,0:T(8,128)S(1)}, u32[]{:S(2)}, u32[]{:S(2)}) %collective-permute-start.3) | collective-permute-done | bytes 73760 | tf_op jit(solution)/shard_map/ppermute | solution.py:437
  19.7 1.8 %collective-permute-start.4 = (f32[4,72,128]{2,1,0:T(8,128)S(1)}, f32[4,72,128]{2,1,0:T(8,128)S(1)}, u32[]{:S(2)}, u32[]{:S(2)}) collective-permute-start(f32[4,72,128]{2,1,0:T(8,128)S(1)} %pad_maximum_fusion.3), channel_id=1, source_target_pairs={{0,8},{2,10},{4,12},{6,14},{8,0},{10,2},{12,4},{14,6},{16,24},{18,... | collective-permute-start | bytes 442376 | tf_op jit(solution)/shard_map/ppermute | solution.py:437
  21.4 3.4 %collective-permute-done.4.refs_3_ = f32[4,72,128]{2,1,0:T(8,128)S(1)} collective-permute-done((f32[4,72,128]{2,1,0:T(8,128)S(1)}, f32[4,72,128]{2,1,0:T(8,128)S(1)}, u32[]{:S(2)}, u32[]{:S(2)}) %collective-permute-start.4) | collective-permute-done | bytes 147488 | tf_op jit(solution)/shard_map/ppermute | solution.py:437
  24.9 0.0 collective-permute-done.5.refs_2_
  24.9 0.1 collective-permute-start.6
  25.0 0.6 %collective-permute-start.7 = (f32[8,72,128]{2,1,0:T(8,128)S(1)}, f32[8,72,128]{2,1,0:T(8,128)S(1)}, u32[]{:S(2)}, u32[]{:S(2)}) collective-permute-start(f32[8,72,128]{2,1,0:T(8,128)S(1)} %pad_maximum_fusion.1), channel_id=1, source_target_pairs={{0,2},{2,0},{4,6},{6,4},{8,10},{10,8},{12,14},{14,12},{16,18},{18,... | collective-permute-start | bytes 884744 | tf_op jit(solution)/shard_map/ppermute | solution.py:437
  25.6 0.2 node_sum.1.partial
  25.8 1.0 %collective-permute-done.6.refs_3_ = f32[4,200,128]{2,1,0:T(8,128)S(1)} collective-permute-done((f32[4,200,128]{2,1,0:T(8,128)S(1)}, f32[4,200,128]{2,1,0:T(8,128)S(1)}, u32[]{:S(2)}, u32[]{:S(2)}) %collective-permute-start.6) | collective-permute-done | bytes 409632 | tf_op jit(solution)/shard_map/ppermute | solution.py:437
  26.7 0.2 node_assemble.1
  26.9 0.2 collective-permute-done.7.refs_0_
  27.1 3.0 %node_solve.1 = (f32[8,144,128]{2,1,0:T(8,128)S(1)}, f32[72,128]{1,0:T(8,128)S(1)}) custom-call(f32[8,72,128]{2,1,0:T(8,128)S(1)} %get-tuple-element.38.regular, f32[8,128,128]{2,1,0:T(8,128)S(1)} %get-tuple-element.39.links, f32[8,72,128]{2,1,0:T(8,128)S(1)} %node_sum.1.partial, f32[8,72,128]{2,1,0:T(8,128)S(1)} %collective-permute-done.7.refs_0_), custom_call_target="tpu_custom_call" | custom-call | tf_op jit(solution)/shard_map/node_solve/pallas_call | solution.py:627
  30.2 1.5 %collective-permute-start.8 = (f32[72,128]{1,0:T(8,128)S(1)}, f32[72,128]{1,0:T(8,128)S(1)}, u32[]{:S(2)}, u32[]{:S(2)}) collective-permute-start(f32[72,128]{1,0:T(8,128)S(1)} %get-tuple-element.40.part), channel_id=1, source_target_pairs={{0,1},{1,0},{2,3},{3,2},{4,5},{5,4},{6,7},{7,6},{8,9},{9,8},{10,11... | collective-permute-start | bytes 110600 | tf_op jit(solution)/shard_map/ppermute | solution.py:437
  31.7 1.2 %root_prepare.1 = (f32[128,128]{1,0:T(8,128)S(1)}, f32[16,128]{1,0:T(8,128)S(1)}, bf16[128,128]{1,0:T(8,128)(2,1)S(1)}, f32[8,128,128]{2,1,0:T(8,128)S(1)}, f32[...) custom-call(f32[1,8,128]{2,1,0:T(8,128)S(1)} %get-tuple-element.29.owners, ...), custom_call_target="tpu_custom_call" | custom-call | flops 1500000000 | tf_op jit(solution)/shard_map/root_prepare/pallas_call | solution.py:645
  32.9 1.3 %collective-permute-done.8.refs_0_ = f32[72,128]{1,0:T(8,128)S(1)} collective-permute-done((f32[72,128]{1,0:T(8,128)S(1)}, f32[72,128]{1,0:T(8,128)S(1)}, u32[]{:S(2)}, u32[]{:S(2)}) %collective-permute-start.8) | collective-permute-done | bytes 36896 | tf_op jit(solution)/shard_map/ppermute | solution.py:437
  34.2 2.2 %root_solve.1 = (f32[1,384]{1,0:T(1,128)}, f32[8,8]{1,0:T(8,128)}, f32[1,128]{1,0:T(1,128)}) custom-call(f32[128,128]{1,0:T(8,128)S(1)} %get-tuple-element.45.base, f32[16,128]{1,0:T(8,128)S(1)} %get-tuple-element.46.base_row, bf16[128,128]{1,0:T(8,128)(2,1)S(1)} %get-tuple-element.47.near, f32[8,128,128]{2,1,0:T(8,128)S(1)} %get-tuple-element.48.moves, ...), custom_call_target="tpu_custom_call" | custom-call | tf_op jit(solution)/shard_map/root_solve/pallas_call | solution.py:663
  (5 shorter events, 0.1 us)
Async XLA Ops:
  2.5 9.4 %collective-permute-start = (f32[1,136,128]{2,1,0:T(8,128)S(1)}, f32[1,136,128]{2,1,0:T(8,128)S(1)}, u32[]{:S(2)}, u32[]{:S(2)}) collective-permute-start(f32[1,136,128]{2,1,0:T(8,128)S(1)} %get-tuple-element.31.own), channel_id=1, source_target_pairs={{0,16},{2,18},{4,20},{6,22},{8,24},{10,26},{12,28},{14,30},{16,0},... | collective-permute-start | bytes 208904 | tf_op jit(solution)/shard_map/ppermute | solution.py:437
  10.4 4.0 %collective-permute-start.1 = (f32[1,72,128]{2,1,0:T(8,128)S(1)}, f32[1,72,128]{2,1,0:T(8,128)S(1)}, u32[]{:S(2)}, u32[]{:S(2)}) collective-permute-start(f32[1,72,128]{2,1,0:T(8,128)S(1)} %get-tuple-element.35.refs_0_), channel_id=1, source_target_pairs={{0,4},{2,6},{4,0},{6,2},{8,12},{10,14},{12,8},{14,10},{16,20},{18,... | collective-permute-start | bytes 110600 | tf_op jit(solution)/shard_map/ppermute | solution.py:437
  12.0 5.5 %collective-permute-start.2 = (f32[1,200,128]{2,1,0:T(8,128)S(1)}, f32[1,200,128]{2,1,0:T(8,128)S(1)}, u32[]{:S(2)}, u32[]{:S(2)}) collective-permute-start(f32[1,200,128]{2,1,0:T(8,128)S(1)} %node_pack.1.refs_0_), channel_id=1, source_target_pairs={{0,8},{2,10},{4,12},{6,14},{8,0},{10,2},{12,4},{14,6},{16,24},{18,... | collective-permute-start | bytes 307208 | tf_op jit(solution)/shard_map/ppermute | solution.py:437
  14.4 5.3 %collective-permute-start.3 = (f32[2,72,128]{2,1,0:T(8,128)S(1)}, f32[2,72,128]{2,1,0:T(8,128)S(1)}, u32[]{:S(2)}, u32[]{:S(2)}) collective-permute-start(f32[2,72,128]{2,1,0:T(8,128)S(1)} %pad_maximum_fusion.4), channel_id=1, source_target_pairs={{0,16},{2,18},{4,20},{6,22},{8,24},{10,26},{12,28},{14,30},{16,0},... | collective-permute-start | bytes 221192 | tf_op jit(solution)/shard_map/ppermute | solution.py:437
  17.6 7.3 %collective-permute-start.5 = (f32[2,200,128]{2,1,0:T(8,128)S(1)}, f32[2,200,128]{2,1,0:T(8,128)S(1)}, u32[]{:S(2)}, u32[]{:S(2)}) collective-permute-start(f32[2,200,128]{2,1,0:T(8,128)S(1)} %pad_maximum_fusion.2), channel_id=1, source_target_pairs={{0,4},{2,6},{4,0},{6,2},{8,12},{10,14},{12,8},{14,10},{16,20},{18,... | collective-permute-start | bytes 614408 | tf_op jit(solution)/shard_map/ppermute | solution.py:437
  19.7 5.2 %collective-permute-start.4 = (f32[4,72,128]{2,1,0:T(8,128)S(1)}, f32[4,72,128]{2,1,0:T(8,128)S(1)}, u32[]{:S(2)}, u32[]{:S(2)}) collective-permute-start(f32[4,72,128]{2,1,0:T(8,128)S(1)} %pad_maximum_fusion.3), channel_id=1, source_target_pairs={{0,8},{2,10},{4,12},{6,14},{8,0},{10,2},{12,4},{14,6},{16,24},{18,... | collective-permute-start | bytes 442376 | tf_op jit(solution)/shard_map/ppermute | solution.py:437
  24.9 1.8 %collective-permute-start.6 = (f32[4,200,128]{2,1,0:T(8,128)S(1)}, f32[4,200,128]{2,1,0:T(8,128)S(1)}, u32[]{:S(2)}, u32[]{:S(2)}) collective-permute-start(f32[4,200,128]{2,1,0:T(8,128)S(1)} %pad_maximum_fusion), channel_id=1, source_target_pairs={{0,2},{2,0},{4,6},{6,4},{8,10},{10,8},{12,14},{14,12},{16,18},{18,... | collective-permute-start | bytes 1228808 | tf_op jit(solution)/shard_map/ppermute | solution.py:437
  25.0 2.1 %collective-permute-start.7 = (f32[8,72,128]{2,1,0:T(8,128)S(1)}, f32[8,72,128]{2,1,0:T(8,128)S(1)}, u32[]{:S(2)}, u32[]{:S(2)}) collective-permute-start(f32[8,72,128]{2,1,0:T(8,128)S(1)} %pad_maximum_fusion.1), channel_id=1, source_target_pairs={{0,2},{2,0},{4,6},{6,4},{8,10},{10,8},{12,14},{14,12},{16,18},{18,... | collective-permute-start | bytes 884744 | tf_op jit(solution)/shard_map/ppermute | solution.py:437
  30.2 4.0 %collective-permute-start.8 = (f32[72,128]{1,0:T(8,128)S(1)}, f32[72,128]{1,0:T(8,128)S(1)}, u32[]{:S(2)}, u32[]{:S(2)}) collective-permute-start(f32[72,128]{1,0:T(8,128)S(1)} %get-tuple-element.40.part), channel_id=1, source_target_pairs={{0,1},{1,0},{2,3},{3,2},{4,5},{5,4},{6,7},{7,6},{8,9},{9,8},{10,11... | collective-permute-start | bytes 110600 | tf_op jit(solution)/shard_map/ppermute | solution.py:437

commit v6 on v5

--- a/solution.py
+++ b/solution.py
@@ -437,6 +437,15 @@
     return lax.ppermute(values, axis, [(i, i ^ distance) for i in range(extent)])
 
 
+def crossed(values, sets, distance):
+    leaves = lax.axis_size("leaf")
+    swap = 1 if leaves % 2 == 0 else 0
+    pairs = [
+        (i * sets + j, (i ^ swap) * sets + (j ^ distance)) for i in range(leaves) for j in range(sets)
+    ]
+    return lax.ppermute(values, ("leaf", "grp"), pairs)
+
+
 def exchange(pieces, axis, extent, distance):
     sent = pieces[0] if len(pieces) == 1 else jnp.concatenate(pieces, axis=0)
     pieces.append(moved(sent, axis, extent, distance))
@@ -468,7 +477,7 @@
     steps = gather_steps(extent)
     pieces = []
     for distance in reversed(steps):
-        pieces.append(moved(values, axis, extent, distance))
+        pieces.append(crossed(values, extent, distance))
         values = values + pieces[-1]
     return pieces
 

time: 36.5 us -> 36 us (0.986)
    ppermute x9 -> x8, starting transfers between devices: 11.6 us -> 10.1 us  [moved(): lax.ppermute(values, axis, [(i, i ^ distance) for i in range(extent)])]
    ppermute x9 -> x8, waiting for transfers between devices: 11.5 us -> 10.2 us  [moved(): lax.ppermute(values, axis, [(i, i ^ distance) for i in range(extent)])]
    ppermute x0 -> x1, starting transfers between devices: none -> 1.29 us  [crossed(): return lax.ppermute(values, ('leaf', 'grp'), pairs)]
    ppermute x0 -> x1, waiting for transfers between devices: none -> 1.08 us  [crossed(): return lax.ppermute(values, ('leaf', 'grp'), pairs)]
where the time goes in v6:
time: 36 us; the launch traced here: 35.9 us
  Pallas kernels  11.8 us (33%)
  starting transfers between devices  11.4 us (32%)
  waiting for transfers between devices  11.3 us (31%)
  between operations  1.36 us (4%)
    ppermute x8, waiting for transfers between devices, moved(): lax.ppermute(values, axis, [(i, i ^ distance) for i in range(extent)])  10.2 us
    ppermute x8, starting transfers between devices, moved(): lax.ppermute(values, axis, [(i, i ^ distance) for i in range(extent)])  10.1 us
    pallas_call x1, Pallas kernels, body(): pl.pallas_call(node_kernel, out_shape=(pltpu.VMEM((groups, size + 16, wid...  3.04 us
    pallas_call x1, Pallas kernels, body(): pl.pallas_call(functools.partial(root_kernel, sets, band), out_shape=(jax...  2.15 us
    pallas_call x1, Pallas kernels, invert(): pl.pallas_call(invert_kernel, out_shape=pltpu.VMEM((slots, n, n), bf16),...  2.1 us
    pallas_call x1, Pallas kernels, solve(): pl.pallas_call(leaf_kernel, out_shape=(pltpu.VMEM((slots, width + 16, n),...  1.62 us
    ppermute x1, starting transfers between devices, crossed(): return lax.ppermute(values, ('leaf', 'grp'), pairs)  1.29 us
    pallas_call x1, Pallas kernels, body(): pl.pallas_call(stage_kernel, out_shape=(pltpu.VMEM((slots, 8, width), f32...  1.24 us
  transfers between devices with their start and end apart: 9, of which 7 were waited for; matrix products, arithmetic and copies ran while one was open for 0% of the time, Pallas kernels for 15%

profile of v6, /device:TPU:0, one launch (start us, length us, event | category | flops | bytes accessed | tf_op | source)
XLA Modules:
  0.0 35.9 jit_solution(7420462053306992833)
XLA Ops:
  1.3 1.2 %stage.1 = (f32[1,8,128]{2,1,0:T(8,128)S(1)}, f32[1,136,128]{2,1,0:T(8,128)S(1)}, f32[1,384,384]{2,1,0:T(8,128)S(1)}, f32[1,384,128]{2,1,0:T(8,128)S(1)}, f32[1,...) custom-call(s32[1]{0:T(128)S(6)} %copy.12.parent, f32[8,8,128]{2,1,0:T(8,128)} %matrix.1, ...), custom_call_target="tpu_custom_call" | custom-call | tf_op jit(solution)/shard_map/stage/pallas_call | solution.py:518
  2.5 4.1 %collective-permute-start = (f32[1,136,128]{2,1,0:T(8,128)S(1)}, f32[1,136,128]{2,1,0:T(8,128)S(1)}, u32[]{:S(2)}, u32[]{:S(2)}) collective-permute-start(f32[1,136,128]{2,1,0:T(8,128)S(1)} %get-tuple-element.31.own), channel_id=1, source_target_pairs={{0,16},{2,18},{4,20},{6,22},{8,24},{10,26},{12,28},{14,30},{16,0},... | collective-permute-start | bytes 208904 | tf_op jit(solution)/shard_map/ppermute | solution.py:437
  6.6 2.1 %leaf_invert.1.inverse = bf16[1,384,384]{2,1,0:T(8,128)(2,1)S(1)} custom-call(f32[1,384,384]{2,1,0:T(8,128)S(1)} %get-tuple-element.30.matrix), custom_call_target="tpu_custom_call" | custom-call | flops 3000000000 | tf_op jit(solution)/shard_map/leaf_invert/pallas_call | solution.py:533
  8.7 1.6 %leaf_solve.1 = (f32[1,144,384]{2,1,0:T(8,128)S(1)}, f32[1,72,128]{2,1,0:T(8,128)S(1)}) custom-call(f32[1,8,128]{2,1,0:T(8,128)S(1)} %get-tuple-element.29.owners, f32[1,384,384]{2,1,0:T(8,128)S(1)} %get-tuple-element.30.matrix, f32[1,384,128]{2,1,0:T(8,128)S(1)} %get-tuple-element.33.coupling, f32[1,384]{1,0:T(1,128)S(1)} %get-tuple-element.34.residual, ...), custom_call_target="tpu_custom_call" | custom-call | flops 3000000000 | tf_op jit(solution)/shard_map/leaf_solve/pallas_call | solution.py:544
  10.4 1.6 %collective-permute-start.1 = (f32[1,72,128]{2,1,0:T(8,128)S(1)}, f32[1,72,128]{2,1,0:T(8,128)S(1)}, u32[]{:S(2)}, u32[]{:S(2)}) collective-permute-start(f32[1,72,128]{2,1,0:T(8,128)S(1)} %get-tuple-element.35.refs_0_), channel_id=1, source_target_pairs={{0,4},{2,6},{4,0},{6,2},{8,12},{10,14},{12,8},{14,10},{16,20},{18,... | collective-permute-start | bytes 110600 | tf_op jit(solution)/shard_map/ppermute | solution.py:437
  11.9 0.0 collective-permute-done.other
  11.9 0.1 node_pack.1.refs_0_
  12.0 1.6 %collective-permute-start.2 = (f32[1,200,128]{2,1,0:T(8,128)S(1)}, f32[1,200,128]{2,1,0:T(8,128)S(1)}, u32[]{:S(2)}, u32[]{:S(2)}) collective-permute-start(f32[1,200,128]{2,1,0:T(8,128)S(1)} %node_pack.1.refs_0_), channel_id=1, source_target_pairs={{0,8},{2,10},{4,12},{6,14},{8,0},{10,2},{12,4},{14,6},{16,24},{18,... | collective-permute-start | bytes 307208 | tf_op jit(solution)/shard_map/ppermute | solution.py:437
  13.7 0.7 %collective-permute-done.1.refs_1_ = f32[1,72,128]{2,1,0:T(8,128)S(1)} collective-permute-done((f32[1,72,128]{2,1,0:T(8,128)S(1)}, f32[1,72,128]{2,1,0:T(8,128)S(1)}, u32[]{:S(2)}, u32[]{:S(2)}) %collective-permute-start.1) | collective-permute-done | bytes 36896 | tf_op jit(solution)/shard_map/ppermute | solution.py:437
  14.4 0.3 collective-permute-start.3
  14.6 2.9 %collective-permute-done.2.refs_1_ = f32[1,200,128]{2,1,0:T(8,128)S(1)} collective-permute-done((f32[1,200,128]{2,1,0:T(8,128)S(1)}, f32[1,200,128]{2,1,0:T(8,128)S(1)}, u32[]{:S(2)}, u32[]{:S(2)}) %collective-permute-start.2) | collective-permute-done | bytes 102432 | tf_op jit(solution)/shard_map/ppermute | solution.py:437
  17.6 0.1 collective-permute-start.5
  17.7 2.0 %collective-permute-done.3.refs_2_ = f32[2,72,128]{2,1,0:T(8,128)S(1)} collective-permute-done((f32[2,72,128]{2,1,0:T(8,128)S(1)}, f32[2,72,128]{2,1,0:T(8,128)S(1)}, u32[]{:S(2)}, u32[]{:S(2)}) %collective-permute-start.3) | collective-permute-done | bytes 73760 | tf_op jit(solution)/shard_map/ppermute | solution.py:437
  19.7 1.8 %collective-permute-start.4 = (f32[4,72,128]{2,1,0:T(8,128)S(1)}, f32[4,72,128]{2,1,0:T(8,128)S(1)}, u32[]{:S(2)}, u32[]{:S(2)}) collective-permute-start(f32[4,72,128]{2,1,0:T(8,128)S(1)} %pad_maximum_fusion.3), channel_id=1, source_target_pairs={{0,8},{2,10},{4,12},{6,14},{8,0},{10,2},{12,4},{14,6},{16,24},{18,... | collective-permute-start | bytes 442376 | tf_op jit(solution)/shard_map/ppermute | solution.py:437
  21.4 3.4 %collective-permute-done.4.refs_3_ = f32[4,72,128]{2,1,0:T(8,128)S(1)} collective-permute-done((f32[4,72,128]{2,1,0:T(8,128)S(1)}, f32[4,72,128]{2,1,0:T(8,128)S(1)}, u32[]{:S(2)}, u32[]{:S(2)}) %collective-permute-start.4) | collective-permute-done | bytes 147488 | tf_op jit(solution)/shard_map/ppermute | solution.py:437
  24.9 0.0 collective-permute-done.5.refs_2_
  24.9 0.1 collective-permute-start.6
  25.0 0.6 %collective-permute-start.7 = (f32[8,72,128]{2,1,0:T(8,128)S(1)}, f32[8,72,128]{2,1,0:T(8,128)S(1)}, u32[]{:S(2)}, u32[]{:S(2)}) collective-permute-start(f32[8,72,128]{2,1,0:T(8,128)S(1)} %pad_maximum_fusion.1), channel_id=1, source_target_pairs={{0,2},{2,0},{4,6},{6,4},{8,10},{10,8},{12,14},{14,12},{16,18},{18,... | collective-permute-start | bytes 884744 | tf_op jit(solution)/shard_map/ppermute | solution.py:437
  25.6 0.2 node_sum.1.partial
  25.8 1.0 %collective-permute-done.6.refs_3_ = f32[4,200,128]{2,1,0:T(8,128)S(1)} collective-permute-done((f32[4,200,128]{2,1,0:T(8,128)S(1)}, f32[4,200,128]{2,1,0:T(8,128)S(1)}, u32[]{:S(2)}, u32[]{:S(2)}) %collective-permute-start.6) | collective-permute-done | bytes 409632 | tf_op jit(solution)/shard_map/ppermute | solution.py:437
  26.7 0.2 node_assemble.1
  26.9 0.2 collective-permute-done.7.refs_0_
  27.1 3.0 %node_solve.1 = (f32[8,144,128]{2,1,0:T(8,128)S(1)}, f32[72,128]{1,0:T(8,128)S(1)}) custom-call(f32[8,72,128]{2,1,0:T(8,128)S(1)} %get-tuple-element.38.regular, f32[8,128,128]{2,1,0:T(8,128)S(1)} %get-tuple-element.39.links, f32[8,72,128]{2,1,0:T(8,128)S(1)} %node_sum.1.partial, f32[8,72,128]{2,1,0:T(8,128)S(1)} %collective-permute-done.7.refs_0_), custom_call_target="tpu_custom_call" | custom-call | tf_op jit(solution)/shard_map/node_solve/pallas_call | solution.py:636
  30.2 1.3 %collective-permute-start.8 = (f32[72,128]{1,0:T(8,128)S(1)}, f32[72,128]{1,0:T(8,128)S(1)}, u32[]{:S(2)}, u32[]{:S(2)}) collective-permute-start(f32[72,128]{1,0:T(8,128)S(1)} %get-tuple-element.40.part), channel_id=1, source_target_pairs={{0,3},{1,2},{2,1},{3,0},{4,7},{5,6},{6,5},{7,4},{8,11},{9,10},{10,... | collective-permute-start | bytes 110600 | tf_op jit(solution)/shard_map/ppermute | solution.py:446
  31.5 1.2 %root_prepare.1 = (f32[128,128]{1,0:T(8,128)S(1)}, f32[16,128]{1,0:T(8,128)S(1)}, bf16[128,128]{1,0:T(8,128)(2,1)S(1)}, f32[8,128,128]{2,1,0:T(8,128)S(1)}, f32[...) custom-call(f32[1,8,128]{2,1,0:T(8,128)S(1)} %get-tuple-element.29.owners, ...), custom_call_target="tpu_custom_call" | custom-call | flops 1500000000 | tf_op jit(solution)/shard_map/root_prepare/pallas_call | solution.py:654
  32.6 1.1 %collective-permute-done.8.refs_0_ = f32[72,128]{1,0:T(8,128)S(1)} collective-permute-done((f32[72,128]{1,0:T(8,128)S(1)}, f32[72,128]{1,0:T(8,128)S(1)}, u32[]{:S(2)}, u32[]{:S(2)}) %collective-permute-start.8) | collective-permute-done | bytes 36896 | tf_op jit(solution)/shard_map/ppermute | solution.py:446
  33.7 2.2 %root_solve.1 = (f32[1,384]{1,0:T(1,128)}, f32[8,8]{1,0:T(8,128)}, f32[1,128]{1,0:T(1,128)}) custom-call(f32[128,128]{1,0:T(8,128)S(1)} %get-tuple-element.45.base, f32[16,128]{1,0:T(8,128)S(1)} %get-tuple-element.46.base_row, bf16[128,128]{1,0:T(8,128)(2,1)S(1)} %get-tuple-element.47.near, f32[8,128,128]{2,1,0:T(8,128)S(1)} %get-tuple-element.48.moves, ...), custom_call_target="tpu_custom_call" | custom-call | tf_op jit(solution)/shard_map/root_solve/pallas_call | solution.py:672
  (5 shorter events, 0.1 us)
Async XLA Ops:
  2.5 9.4 %collective-permute-start = (f32[1,136,128]{2,1,0:T(8,128)S(1)}, f32[1,136,128]{2,1,0:T(8,128)S(1)}, u32[]{:S(2)}, u32[]{:S(2)}) collective-permute-start(f32[1,136,128]{2,1,0:T(8,128)S(1)} %get-tuple-element.31.own), channel_id=1, source_target_pairs={{0,16},{2,18},{4,20},{6,22},{8,24},{10,26},{12,28},{14,30},{16,0},... | collective-permute-start | bytes 208904 | tf_op jit(solution)/shard_map/ppermute | solution.py:437
  10.4 4.0 %collective-permute-start.1 = (f32[1,72,128]{2,1,0:T(8,128)S(1)}, f32[1,72,128]{2,1,0:T(8,128)S(1)}, u32[]{:S(2)}, u32[]{:S(2)}) collective-permute-start(f32[1,72,128]{2,1,0:T(8,128)S(1)} %get-tuple-element.35.refs_0_), channel_id=1, source_target_pairs={{0,4},{2,6},{4,0},{6,2},{8,12},{10,14},{12,8},{14,10},{16,20},{18,... | collective-permute-start | bytes 110600 | tf_op jit(solution)/shard_map/ppermute | solution.py:437
  12.0 5.5 %collective-permute-start.2 = (f32[1,200,128]{2,1,0:T(8,128)S(1)}, f32[1,200,128]{2,1,0:T(8,128)S(1)}, u32[]{:S(2)}, u32[]{:S(2)}) collective-permute-start(f32[1,200,128]{2,1,0:T(8,128)S(1)} %node_pack.1.refs_0_), channel_id=1, source_target_pairs={{0,8},{2,10},{4,12},{6,14},{8,0},{10,2},{12,4},{14,6},{16,24},{18,... | collective-permute-start | bytes 307208 | tf_op jit(solution)/shard_map/ppermute | solution.py:437
  14.4 5.3 %collective-permute-start.3 = (f32[2,72,128]{2,1,0:T(8,128)S(1)}, f32[2,72,128]{2,1,0:T(8,128)S(1)}, u32[]{:S(2)}, u32[]{:S(2)}) collective-permute-start(f32[2,72,128]{2,1,0:T(8,128)S(1)} %pad_maximum_fusion.4), channel_id=1, source_target_pairs={{0,16},{2,18},{4,20},{6,22},{8,24},{10,26},{12,28},{14,30},{16,0},... | collective-permute-start | bytes 221192 | tf_op jit(solution)/shard_map/ppermute | solution.py:437
  17.6 7.3 %collective-permute-start.5 = (f32[2,200,128]{2,1,0:T(8,128)S(1)}, f32[2,200,128]{2,1,0:T(8,128)S(1)}, u32[]{:S(2)}, u32[]{:S(2)}) collective-permute-start(f32[2,200,128]{2,1,0:T(8,128)S(1)} %pad_maximum_fusion.2), channel_id=1, source_target_pairs={{0,4},{2,6},{4,0},{6,2},{8,12},{10,14},{12,8},{14,10},{16,20},{18,... | collective-permute-start | bytes 614408 | tf_op jit(solution)/shard_map/ppermute | solution.py:437
  19.7 5.2 %collective-permute-start.4 = (f32[4,72,128]{2,1,0:T(8,128)S(1)}, f32[4,72,128]{2,1,0:T(8,128)S(1)}, u32[]{:S(2)}, u32[]{:S(2)}) collective-permute-start(f32[4,72,128]{2,1,0:T(8,128)S(1)} %pad_maximum_fusion.3), channel_id=1, source_target_pairs={{0,8},{2,10},{4,12},{6,14},{8,0},{10,2},{12,4},{14,6},{16,24},{18,... | collective-permute-start | bytes 442376 | tf_op jit(solution)/shard_map/ppermute | solution.py:437
  24.9 1.8 %collective-permute-start.6 = (f32[4,200,128]{2,1,0:T(8,128)S(1)}, f32[4,200,128]{2,1,0:T(8,128)S(1)}, u32[]{:S(2)}, u32[]{:S(2)}) collective-permute-start(f32[4,200,128]{2,1,0:T(8,128)S(1)} %pad_maximum_fusion), channel_id=1, source_target_pairs={{0,2},{2,0},{4,6},{6,4},{8,10},{10,8},{12,14},{14,12},{16,18},{18,... | collective-permute-start | bytes 1228808 | tf_op jit(solution)/shard_map/ppermute | solution.py:437
  25.0 2.1 %collective-permute-start.7 = (f32[8,72,128]{2,1,0:T(8,128)S(1)}, f32[8,72,128]{2,1,0:T(8,128)S(1)}, u32[]{:S(2)}, u32[]{:S(2)}) collective-permute-start(f32[8,72,128]{2,1,0:T(8,128)S(1)} %pad_maximum_fusion.1), channel_id=1, source_target_pairs={{0,2},{2,0},{4,6},{6,4},{8,10},{10,8},{12,14},{14,12},{16,18},{18,... | collective-permute-start | bytes 884744 | tf_op jit(solution)/shard_map/ppermute | solution.py:437
  30.2 3.5 %collective-permute-start.8 = (f32[72,128]{1,0:T(8,128)S(1)}, f32[72,128]{1,0:T(8,128)S(1)}, u32[]{:S(2)}, u32[]{:S(2)}) collective-permute-start(f32[72,128]{1,0:T(8,128)S(1)} %get-tuple-element.40.part), channel_id=1, source_target_pairs={{0,3},{1,2},{2,1},{3,0},{4,7},{5,6},{6,5},{7,4},{8,11},{9,10},{10,... | collective-permute-start | bytes 110600 | tf_op jit(solution)/shard_map/ppermute | solution.py:446

commit v7 on v6

--- a/solution.py
+++ b/solution.py
@@ -94,14 +94,19 @@
     scaled = [alpha * m for m in matrices]
     errors = [(one - s).astype(bf16) for s in scaled]
     inverses = [((scale * alpha) * (2.0 * one - s)).astype(bf16) for s in scaled]
-    for _ in range(steps - 1):
-        errors = [(scale * (mul(e, e) - (0.5 * square) * one)).astype(bf16) for e in errors]
+    errors = [(scale * (mul(e, e) - (0.5 * square) * one)).astype(bf16) for e in errors]
+    n = one.shape[0]
+    for left in reversed(range(steps - 1)):
         delta = square / (2.0 - square)
         square = delta * delta
         scale = 2.0 / (2.0 - square)
-        inverses = [
-            (scale * (v.astype(f32) + mul(e, v))).astype(bf16) for e, v in zip(errors, inverses)
-        ]
+        if left:
+            both = [mul(e, beside(e, v)) for e, v in zip(errors, inverses)]
+            errors = [(scale * (b[:, :n] - (0.5 * square) * one)).astype(bf16) for b in both]
+            news = [b[:, n:] for b in both]
+        else:
+            news = [mul(e, v) for e, v in zip(errors, inverses)]
+        inverses = [(scale * (v.astype(f32) + b)).astype(bf16) for v, b in zip(inverses, news)]
     return inverses
 
 
@@ -342,11 +347,14 @@
     found, bad = finish(blocks, inverses, [rights[q] for q in range(groups)])
 
     def give(found):
-        total = None
+        lefts, rights_ = [], []
         for q in range(groups):
             answers[q] = found(q)
-            part = mul3(found(q), links[q])
-            total = part if q == 0 else total + part
+            ah, al = split(found(q))
+            bh, bl = split(links[q])
+            lefts += [ah, ah, al]
+            rights_ += [bh, bl, bh]
+        total = mul(beside(*lefts), above(*rights_))
         top, tail = pack_symmetric(total[:width], total[width : width + 1])
         message[: width // 2, :] = top
         message[width // 2 :, :] = tail

time: 36 us -> 35.8 us (level)
  no operation moved by 1% of the time
where the time goes in v7:
time: 35.8 us; the launch traced here: 35.7 us
  Pallas kernels  11.7 us (33%)
  starting transfers between devices  11.4 us (32%)
  waiting for transfers between devices  11.2 us (31%)
  between operations  1.37 us (4%)
    ppermute x8, waiting for transfers between devices, moved(): lax.ppermute(values, axis, [(i, i ^ distance) for i in range(extent)])  10.2 us
    ppermute x8, starting transfers between devices, moved(): lax.ppermute(values, axis, [(i, i ^ distance) for i in range(extent)])  10.1 us
    pallas_call x1, Pallas kernels, body(): pl.pallas_call(node_kernel, out_shape=(pltpu.VMEM((groups, size + 16, wid...  2.89 us
    pallas_call x1, Pallas kernels, body(): pl.pallas_call(functools.partial(root_kernel, sets, band), out_shape=(jax...  2.15 us
    pallas_call x1, Pallas kernels, invert(): pl.pallas_call(invert_kernel, out_shape=pltpu.VMEM((slots, n, n), bf16),...  2.09 us
    pallas_call x1, Pallas kernels, solve(): pl.pallas_call(leaf_kernel, out_shape=(pltpu.VMEM((slots, width + 16, n),...  1.61 us
    ppermute x1, starting transfers between devices, crossed(): return lax.ppermute(values, ('leaf', 'grp'), pairs)  1.31 us
    pallas_call x1, Pallas kernels, body(): pl.pallas_call(stage_kernel, out_shape=(pltpu.VMEM((slots, 8, width), f32...  1.24 us
  transfers between devices with their start and end apart: 9, of which 7 were waited for; matrix products, arithmetic and copies ran while one was open for 0% of the time, Pallas kernels for 15%

profile of v7, /device:TPU:0, one launch (start us, length us, event | category | flops | bytes accessed | tf_op | source)
XLA Modules:
  0.0 35.7 jit_solution(14388721200268155892)
XLA Ops:
  1.3 1.2 %stage.1 = (f32[1,8,128]{2,1,0:T(8,128)S(1)}, f32[1,136,128]{2,1,0:T(8,128)S(1)}, f32[1,384,384]{2,1,0:T(8,128)S(1)}, f32[1,384,128]{2,1,0:T(8,128)S(1)}, f32[1,...) custom-call(s32[1]{0:T(128)S(6)} %copy.12.parent, f32[8,8,128]{2,1,0:T(8,128)} %matrix.1, ...), custom_call_target="tpu_custom_call" | custom-call | tf_op jit(solution)/shard_map/stage/pallas_call | solution.py:526
  2.5 4.1 %collective-permute-start = (f32[1,136,128]{2,1,0:T(8,128)S(1)}, f32[1,136,128]{2,1,0:T(8,128)S(1)}, u32[]{:S(2)}, u32[]{:S(2)}) collective-permute-start(f32[1,136,128]{2,1,0:T(8,128)S(1)} %get-tuple-element.31.own), channel_id=1, source_target_pairs={{0,16},{2,18},{4,20},{6,22},{8,24},{10,26},{12,28},{14,30},{16,0},... | collective-permute-start | bytes 208904 | tf_op jit(solution)/shard_map/ppermute | solution.py:445
  6.6 2.1 %leaf_invert.1.inverse = bf16[1,384,384]{2,1,0:T(8,128)(2,1)S(1)} custom-call(f32[1,384,384]{2,1,0:T(8,128)S(1)} %get-tuple-element.30.matrix), custom_call_target="tpu_custom_call" | custom-call | flops 3000000000 | tf_op jit(solution)/shard_map/leaf_invert/pallas_call | solution.py:541
  8.7 1.6 %leaf_solve.1 = (f32[1,144,384]{2,1,0:T(8,128)S(1)}, f32[1,72,128]{2,1,0:T(8,128)S(1)}) custom-call(f32[1,8,128]{2,1,0:T(8,128)S(1)} %get-tuple-element.29.owners, f32[1,384,384]{2,1,0:T(8,128)S(1)} %get-tuple-element.30.matrix, f32[1,384,128]{2,1,0:T(8,128)S(1)} %get-tuple-element.33.coupling, f32[1,384]{1,0:T(1,128)S(1)} %get-tuple-element.34.residual, ...), custom_call_target="tpu_custom_call" | custom-call | flops 3000000000 | tf_op jit(solution)/shard_map/leaf_solve/pallas_call | solution.py:552
  10.3 1.6 %collective-permute-start.1 = (f32[1,72,128]{2,1,0:T(8,128)S(1)}, f32[1,72,128]{2,1,0:T(8,128)S(1)}, u32[]{:S(2)}, u32[]{:S(2)}) collective-permute-start(f32[1,72,128]{2,1,0:T(8,128)S(1)} %get-tuple-element.35.refs_0_), channel_id=1, source_target_pairs={{0,4},{2,6},{4,0},{6,2},{8,12},{10,14},{12,8},{14,10},{16,20},{18,... | collective-permute-start | bytes 110600 | tf_op jit(solution)/shard_map/ppermute | solution.py:445
  11.9 0.0 collective-permute-done.other
  11.9 0.1 node_pack.1.refs_0_
  12.0 1.6 %collective-permute-start.2 = (f32[1,200,128]{2,1,0:T(8,128)S(1)}, f32[1,200,128]{2,1,0:T(8,128)S(1)}, u32[]{:S(2)}, u32[]{:S(2)}) collective-permute-start(f32[1,200,128]{2,1,0:T(8,128)S(1)} %node_pack.1.refs_0_), channel_id=1, source_target_pairs={{0,8},{2,10},{4,12},{6,14},{8,0},{10,2},{12,4},{14,6},{16,24},{18,... | collective-permute-start | bytes 307208 | tf_op jit(solution)/shard_map/ppermute | solution.py:445
  13.7 0.7 %collective-permute-done.1.refs_1_ = f32[1,72,128]{2,1,0:T(8,128)S(1)} collective-permute-done((f32[1,72,128]{2,1,0:T(8,128)S(1)}, f32[1,72,128]{2,1,0:T(8,128)S(1)}, u32[]{:S(2)}, u32[]{:S(2)}) %collective-permute-start.1) | collective-permute-done | bytes 36896 | tf_op jit(solution)/shard_map/ppermute | solution.py:445
  14.4 0.3 collective-permute-start.3
  14.6 2.9 %collective-permute-done.2.refs_1_ = f32[1,200,128]{2,1,0:T(8,128)S(1)} collective-permute-done((f32[1,200,128]{2,1,0:T(8,128)S(1)}, f32[1,200,128]{2,1,0:T(8,128)S(1)}, u32[]{:S(2)}, u32[]{:S(2)}) %collective-permute-start.2) | collective-permute-done | bytes 102432 | tf_op jit(solution)/shard_map/ppermute | solution.py:445
  17.6 0.1 collective-permute-start.5
  17.6 2.0 %collective-permute-done.3.refs_2_ = f32[2,72,128]{2,1,0:T(8,128)S(1)} collective-permute-done((f32[2,72,128]{2,1,0:T(8,128)S(1)}, f32[2,72,128]{2,1,0:T(8,128)S(1)}, u32[]{:S(2)}, u32[]{:S(2)}) %collective-permute-start.3) | collective-permute-done | bytes 73760 | tf_op jit(solution)/shard_map/ppermute | solution.py:445
  19.6 1.8 %collective-permute-start.4 = (f32[4,72,128]{2,1,0:T(8,128)S(1)}, f32[4,72,128]{2,1,0:T(8,128)S(1)}, u32[]{:S(2)}, u32[]{:S(2)}) collective-permute-start(f32[4,72,128]{2,1,0:T(8,128)S(1)} %pad_maximum_fusion.3), channel_id=1, source_target_pairs={{0,8},{2,10},{4,12},{6,14},{8,0},{10,2},{12,4},{14,6},{16,24},{18,... | collective-permute-start | bytes 442376 | tf_op jit(solution)/shard_map/ppermute | solution.py:445
  21.4 3.4 %collective-permute-done.4.refs_3_ = f32[4,72,128]{2,1,0:T(8,128)S(1)} collective-permute-done((f32[4,72,128]{2,1,0:T(8,128)S(1)}, f32[4,72,128]{2,1,0:T(8,128)S(1)}, u32[]{:S(2)}, u32[]{:S(2)}) %collective-permute-start.4) | collective-permute-done | bytes 147488 | tf_op jit(solution)/shard_map/ppermute | solution.py:445
  24.9 0.0 collective-permute-done.5.refs_2_
  24.9 0.1 collective-permute-start.6
  25.0 0.6 %collective-permute-start.7 = (f32[8,72,128]{2,1,0:T(8,128)S(1)}, f32[8,72,128]{2,1,0:T(8,128)S(1)}, u32[]{:S(2)}, u32[]{:S(2)}) collective-permute-start(f32[8,72,128]{2,1,0:T(8,128)S(1)} %pad_maximum_fusion.1), channel_id=1, source_target_pairs={{0,2},{2,0},{4,6},{6,4},{8,10},{10,8},{12,14},{14,12},{16,18},{18,... | collective-permute-start | bytes 884744 | tf_op jit(solution)/shard_map/ppermute | solution.py:445
  25.6 0.2 node_sum.1.partial
  25.8 1.0 %collective-permute-done.6.refs_3_ = f32[4,200,128]{2,1,0:T(8,128)S(1)} collective-permute-done((f32[4,200,128]{2,1,0:T(8,128)S(1)}, f32[4,200,128]{2,1,0:T(8,128)S(1)}, u32[]{:S(2)}, u32[]{:S(2)}) %collective-permute-start.6) | collective-permute-done | bytes 409632 | tf_op jit(solution)/shard_map/ppermute | solution.py:445
  26.7 0.2 node_assemble.1
  26.9 0.2 collective-permute-done.7.refs_0_
  27.1 2.9 %node_solve.1 = (f32[8,144,128]{2,1,0:T(8,128)S(1)}, f32[72,128]{1,0:T(8,128)S(1)}) custom-call(f32[8,72,128]{2,1,0:T(8,128)S(1)} %get-tuple-element.38.regular, f32[8,128,128]{2,1,0:T(8,128)S(1)} %get-tuple-element.39.links, f32[8,72,128]{2,1,0:T(8,128)S(1)} %node_sum.1.partial, f32[8,72,128]{2,1,0:T(8,128)S(1)} %collective-permute-done.7.refs_0_), custom_call_target="tpu_custom_call" | custom-call | tf_op jit(solution)/shard_map/node_solve/pallas_call | solution.py:644
  30.0 1.3 %collective-permute-start.8 = (f32[72,128]{1,0:T(8,128)S(1)}, f32[72,128]{1,0:T(8,128)S(1)}, u32[]{:S(2)}, u32[]{:S(2)}) collective-permute-start(f32[72,128]{1,0:T(8,128)S(1)} %get-tuple-element.40.part), channel_id=1, source_target_pairs={{0,3},{1,2},{2,1},{3,0},{4,7},{5,6},{6,5},{7,4},{8,11},{9,10},{10,... | collective-permute-start | bytes 110600 | tf_op jit(solution)/shard_map/ppermute | solution.py:454
  31.3 1.2 %root_prepare.1 = (f32[128,128]{1,0:T(8,128)S(1)}, f32[16,128]{1,0:T(8,128)S(1)}, bf16[128,128]{1,0:T(8,128)(2,1)S(1)}, f32[8,128,128]{2,1,0:T(8,128)S(1)}, f32[...) custom-call(f32[1,8,128]{2,1,0:T(8,128)S(1)} %get-tuple-element.29.owners, ...), custom_call_target="tpu_custom_call" | custom-call | flops 1500000000 | tf_op jit(solution)/shard_map/root_prepare/pallas_call | solution.py:662
  32.6 1.0 %collective-permute-done.8.refs_0_ = f32[72,128]{1,0:T(8,128)S(1)} collective-permute-done((f32[72,128]{1,0:T(8,128)S(1)}, f32[72,128]{1,0:T(8,128)S(1)}, u32[]{:S(2)}, u32[]{:S(2)}) %collective-permute-start.8) | collective-permute-done | bytes 36896 | tf_op jit(solution)/shard_map/ppermute | solution.py:454
  33.5 2.2 %root_solve.1 = (f32[1,384]{1,0:T(1,128)}, f32[8,8]{1,0:T(8,128)}, f32[1,128]{1,0:T(1,128)}) custom-call(f32[128,128]{1,0:T(8,128)S(1)} %get-tuple-element.45.base, f32[16,128]{1,0:T(8,128)S(1)} %get-tuple-element.46.base_row, bf16[128,128]{1,0:T(8,128)(2,1)S(1)} %get-tuple-element.47.near, f32[8,128,128]{2,1,0:T(8,128)S(1)} %get-tuple-element.48.moves, ...), custom_call_target="tpu_custom_call" | custom-call | tf_op jit(solution)/shard_map/root_solve/pallas_call | solution.py:680
  (5 shorter events, 0.1 us)
Async XLA Ops:
  2.5 9.4 %collective-permute-start = (f32[1,136,128]{2,1,0:T(8,128)S(1)}, f32[1,136,128]{2,1,0:T(8,128)S(1)}, u32[]{:S(2)}, u32[]{:S(2)}) collective-permute-start(f32[1,136,128]{2,1,0:T(8,128)S(1)} %get-tuple-element.31.own), channel_id=1, source_target_pairs={{0,16},{2,18},{4,20},{6,22},{8,24},{10,26},{12,28},{14,30},{16,0},... | collective-permute-start | bytes 208904 | tf_op jit(solution)/shard_map/ppermute | solution.py:445
  10.3 4.0 %collective-permute-start.1 = (f32[1,72,128]{2,1,0:T(8,128)S(1)}, f32[1,72,128]{2,1,0:T(8,128)S(1)}, u32[]{:S(2)}, u32[]{:S(2)}) collective-permute-start(f32[1,72,128]{2,1,0:T(8,128)S(1)} %get-tuple-element.35.refs_0_), channel_id=1, source_target_pairs={{0,4},{2,6},{4,0},{6,2},{8,12},{10,14},{12,8},{14,10},{16,20},{18,... | collective-permute-start | bytes 110600 | tf_op jit(solution)/shard_map/ppermute | solution.py:445
  12.0 5.5 %collective-permute-start.2 = (f32[1,200,128]{2,1,0:T(8,128)S(1)}, f32[1,200,128]{2,1,0:T(8,128)S(1)}, u32[]{:S(2)}, u32[]{:S(2)}) collective-permute-start(f32[1,200,128]{2,1,0:T(8,128)S(1)} %node_pack.1.refs_0_), channel_id=1, source_target_pairs={{0,8},{2,10},{4,12},{6,14},{8,0},{10,2},{12,4},{14,6},{16,24},{18,... | collective-permute-start | bytes 307208 | tf_op jit(solution)/shard_map/ppermute | solution.py:445
  14.4 5.3 %collective-permute-start.3 = (f32[2,72,128]{2,1,0:T(8,128)S(1)}, f32[2,72,128]{2,1,0:T(8,128)S(1)}, u32[]{:S(2)}, u32[]{:S(2)}) collective-permute-start(f32[2,72,128]{2,1,0:T(8,128)S(1)} %pad_maximum_fusion.4), channel_id=1, source_target_pairs={{0,16},{2,18},{4,20},{6,22},{8,24},{10,26},{12,28},{14,30},{16,0},... | collective-permute-start | bytes 221192 | tf_op jit(solution)/shard_map/ppermute | solution.py:445
  17.6 7.3 %collective-permute-start.5 = (f32[2,200,128]{2,1,0:T(8,128)S(1)}, f32[2,200,128]{2,1,0:T(8,128)S(1)}, u32[]{:S(2)}, u32[]{:S(2)}) collective-permute-start(f32[2,200,128]{2,1,0:T(8,128)S(1)} %pad_maximum_fusion.2), channel_id=1, source_target_pairs={{0,4},{2,6},{4,0},{6,2},{8,12},{10,14},{12,8},{14,10},{16,20},{18,... | collective-permute-start | bytes 614408 | tf_op jit(solution)/shard_map/ppermute | solution.py:445
  19.6 5.2 %collective-permute-start.4 = (f32[4,72,128]{2,1,0:T(8,128)S(1)}, f32[4,72,128]{2,1,0:T(8,128)S(1)}, u32[]{:S(2)}, u32[]{:S(2)}) collective-permute-start(f32[4,72,128]{2,1,0:T(8,128)S(1)} %pad_maximum_fusion.3), channel_id=1, source_target_pairs={{0,8},{2,10},{4,12},{6,14},{8,0},{10,2},{12,4},{14,6},{16,24},{18,... | collective-permute-start | bytes 442376 | tf_op jit(solution)/shard_map/ppermute | solution.py:445
  24.9 1.8 %collective-permute-start.6 = (f32[4,200,128]{2,1,0:T(8,128)S(1)}, f32[4,200,128]{2,1,0:T(8,128)S(1)}, u32[]{:S(2)}, u32[]{:S(2)}) collective-permute-start(f32[4,200,128]{2,1,0:T(8,128)S(1)} %pad_maximum_fusion), channel_id=1, source_target_pairs={{0,2},{2,0},{4,6},{6,4},{8,10},{10,8},{12,14},{14,12},{16,18},{18,... | collective-permute-start | bytes 1228808 | tf_op jit(solution)/shard_map/ppermute | solution.py:445
  25.0 2.1 %collective-permute-start.7 = (f32[8,72,128]{2,1,0:T(8,128)S(1)}, f32[8,72,128]{2,1,0:T(8,128)S(1)}, u32[]{:S(2)}, u32[]{:S(2)}) collective-permute-start(f32[8,72,128]{2,1,0:T(8,128)S(1)} %pad_maximum_fusion.1), channel_id=1, source_target_pairs={{0,2},{2,0},{4,6},{6,4},{8,10},{10,8},{12,14},{14,12},{16,18},{18,... | collective-permute-start | bytes 884744 | tf_op jit(solution)/shard_map/ppermute | solution.py:445
  30.0 3.5 %collective-permute-start.8 = (f32[72,128]{1,0:T(8,128)S(1)}, f32[72,128]{1,0:T(8,128)S(1)}, u32[]{:S(2)}, u32[]{:S(2)}) collective-permute-start(f32[72,128]{1,0:T(8,128)S(1)} %get-tuple-element.40.part), channel_id=1, source_target_pairs={{0,3},{1,2},{2,1},{3,0},{4,7},{5,6},{6,5},{7,4},{8,11},{9,10},{10,... | collective-permute-start | bytes 110600 | tf_op jit(solution)/shard_map/ppermute | solution.py:454
